TPU v7x, 256 devices: a whole 4x4x8 slice. The times are simulated.
256 devices in a mesh: ctx: 32 (over x, z), head: 8 (over y, core).
Axes of the slice: x: 4, y: 4, z: 8, core: 2. Of those that a mesh axis runs over, the one named last changes fastest.
Arguments:
- queries: bfloat16 [24576, 5120], P('ctx', 'head'), may hold values from -9 to 9
- keys: bfloat16 [24576, 5120], P('ctx', 'head'), may hold values from -6 to 6
- values: bfloat16 [24576, 5120], P('ctx', 'head'), may hold values from -24 to 24
- query_label: int32 [24576, 1], P('ctx'), may hold values from 0 to 31; in each aligned block of 768 rows (0 to 767, 768 to 1535, ...) at most 48 rows name the same one
- key_label: int32 [24576, 1], P('ctx'), may hold values from 0 to 383; in each aligned block of 768 rows (0 to 767, 768 to 1535, ...) at most 4 rows name the same one
- pattern: int32 [32, 16], replicated, may hold values from 0 to 383, as said below
- out_weight: bfloat16 [5120, 5120], P('head'), may hold values from -0.125 to 0.125
Outputs:
- mixed: bfloat16 [24576, 5120], P('ctx', 'head')
Inputs may be any that keep to these rules, and one draw needn't show every extreme that they name: `query_label`: among the rows of one device, at most 48 name one query cluster. `key_label`: among the rows of one device, at most 4 name one key cluster; every key cluster holds some token. `pattern`: each row names 16 different key clusters.
All inputs are finite; a program needn't handle non-finite values.
Results may differ from a plain program's by a relative error of at most 0.017.
Values may be sent and summed in bfloat16 or wider, within the bound.
No kernel may reach another device: no remote copies, remote signals or barrier semaphores. Data moves between devices by JAX's collectives and lax.ppermute only.
A program may use at most 128 MiB of HBM per device.

v0:
```python
import math

import jax
import jax.numpy as jnp
from jax import lax
from jax.sharding import PartitionSpec as P

HDIM = 128


def rank_within(labels, count):
    onehot = (labels[:, None] == jnp.arange(count, dtype=jnp.int32)[None, :]).astype(jnp.int32)
    before = jnp.cumsum(onehot, axis=0) - onehot
    return jnp.sum(before * onehot, axis=1)


def attend(query_part, key_part, value_part, flag_part):
    query_rows = query_part.reshape(-1, query_part.shape[2], query_part.shape[3])
    key_rows = key_part.reshape(-1, key_part.shape[2], key_part.shape[3])
    value_rows = value_part.reshape(-1, value_part.shape[2], value_part.shape[3])
    live_keys = flag_part.reshape(-1, flag_part.shape[2]).T > 0
    total_rows = query_rows.shape[0]
    stride = math.gcd(total_rows, 512)
    factor = 1.0 / math.sqrt(query_part.shape[3])

    def one_block(query_block):
        scores = (
            jnp.einsum("qhd,khd->hqk", query_block, key_rows, preferred_element_type=jnp.float32)
            * factor
        )
        scores = jnp.where(live_keys[:, None, :], scores, -1e30)
        peak = jnp.max(scores, axis=2, keepdims=True)
        expon = jnp.exp(scores - peak)
        weights = (expon / jnp.sum(expon, axis=2, keepdims=True)).astype(jnp.bfloat16)
        return jnp.einsum(
            "hqk,khd->qhd", weights, value_rows, preferred_element_type=jnp.float32
        ).astype(jnp.bfloat16)

    blocks = query_rows.reshape(
        total_rows // stride, stride, query_rows.shape[1], query_rows.shape[2]
    )
    result = lax.map(one_block, blocks)
    return result.reshape(query_part.shape)


def per_device(queries, keys, values, query_label, key_label, pattern, out_weight):
    members = lax.axis_size("ctx")
    rows_here = queries.shape[0]
    heads_here = queries.shape[1] // HDIM
    query_slots = 2 * rows_here // members
    key_slots = 128 // members
    key_groups = rows_here * members // 64
    chosen = pattern.shape[1]
    query_ids = query_label[:, 0]
    key_ids = key_label[:, 0]
    query_rank = rank_within(query_ids, members)
    key_rank = rank_within(key_ids, key_groups)
    spare = jnp.arange(rows_here, dtype=jnp.int32)
    query_table = (
        jnp.full((members * query_slots,), rows_here, jnp.int32)
        .at[query_ids * query_slots + query_rank]
        .set(spare)
    )
    key_table = (
        jnp.full((key_groups * key_slots,), rows_here, jnp.int32)
        .at[key_ids * key_slots + key_rank]
        .set(spare)
    )
    key_index = key_table.reshape(key_groups, key_slots)[pattern].reshape(
        members, chosen * key_slots
    )
    blank = jnp.zeros((1, queries.shape[1]), jnp.bfloat16)
    query_send = jnp.concatenate([queries, blank])[query_table].reshape(
        members, query_slots, heads_here, HDIM
    )
    key_send = jnp.concatenate([keys, blank])[key_index].reshape(
        members, chosen * key_slots, heads_here, HDIM
    )
    value_send = jnp.concatenate([values, blank])[key_index].reshape(
        members, chosen * key_slots, heads_here, HDIM
    )
    flag_send = jnp.broadcast_to(
        (key_index < rows_here).astype(jnp.int32)[:, :, None],
        (members, chosen * key_slots, heads_here),
    )
    query_got = lax.all_to_all(query_send, "ctx", split_axis=0, concat_axis=0, tiled=True)
    key_got, value_got, flag_got = (
        lax.all_to_all(key_send, "ctx", split_axis=0, concat_axis=0, tiled=True),
        lax.all_to_all(value_send, "ctx", split_axis=0, concat_axis=0, tiled=True),
        lax.all_to_all(flag_send, "ctx", split_axis=0, concat_axis=0, tiled=True),
    )
    answer = attend(query_got, key_got, value_got, flag_got)
    returned = lax.all_to_all(answer, "ctx", split_axis=0, concat_axis=0, tiled=True)
    attended = returned.reshape(members * query_slots, queries.shape[1])[
        query_ids * query_slots + query_rank
    ]
    partial_value = jnp.dot(attended, out_weight, preferred_element_type=jnp.float32)
    return lax.psum_scatter(
        partial_value.astype(jnp.bfloat16), "head", scatter_dimension=1, tiled=True
    )


def solution(mesh):
    placed = (
        P("ctx", "head"),
        P("ctx", "head"),
        P("ctx", "head"),
        P("ctx", None),
        P("ctx", None),
        P(),
        P("head", None),
    )
    return jax.shard_map(
        per_device, mesh=mesh, in_specs=placed, out_specs=P("ctx", "head"), check_vma=False
    )
```

profile of v0, /device:TPU:1, one launch (start us, length us, event | category | flops | bytes accessed | tf_op | source)
XLA Modules:
  0.0 457.2 jit_solution(17766949749912632274)
XLA Ops:
  6.5 0.7 reduce.4
  7.2 0.1 copy.48
  7.3 0.2 fusion.28
  7.6 0.1 broadcast_add_fusion
  7.7 0.2 copy.49
  8.0 0.4 fusion.31
  8.4 3.4 scatter_custom_fusion
  11.8 0.2 reshape.106
  12.1 0.1 copy.50
  12.1 0.1 reshape.119
  12.2 1.0 gather_fusion
  13.3 0.1 reshape.116
  13.5 0.7 reshape.198
  14.2 11.9 %all-to-all-start = ((s32[32,1,320]{2,1,0:T(1,128)}), s32[32,1,320]{2,1,0:T(1,128)S(1)}, u32[]{:S(2)}, u32[]{:S(2)}) async-start(s32[32,1,320]{2,1,0:T(1,128)} %reshape.198), calls=%async_computation | async-start | bytes 98304 | tf_op jit(solution)/shard_map/all_to_all | solution.py:90
  26.1 1.7 reduce-window.16
  27.9 0.3 slice_reduce_fusion
  28.1 0.1 fusion.35
  28.3 3.4 scatter_custom_fusion.1
  31.7 0.1 concatenate.9
  31.8 5.6 %gather_fusion.1 = bf16[1536,640]{1,0:T(8,128)(2,1)} fusion(bf16[769,640]{1,0:T(8,128)(2,1)S(1)} %concatenate.9, s32[2048]{0:T(1024)S(1)} %pad_clamp_fusion), kind=kCustom, calls=%fused_computation.1 | custom fusion | bytes 3938304 | tf_op jit(solution)/shard_map/gather | solution.py:73
  37.4 4.3 reshape.108
  41.7 1.6 copy.53
  43.3 9.2 %all-to-all-start.1 = ((bf16[32,48,5,128]{3,1,2,0:T(8,128)(2,1)}), bf16[32,48,5,128]{3,1,2,0:T(8,128)(2,1)S(1)}, u32[]{:S(2)}, u32[]{:S(2)}) async-start(bf16[32,48,5,128]{3,1,2,0:T(8,128)(2,1)} %copy.53), calls=%async_computation.1 | async-start | bytes 3932160 | tf_op jit(solution)/shard_map/all_to_all | solution.py:86
  52.5 0.1 reshape.109
  52.7 0.1 reshape.135
  52.8 1.3 concatenate.11
  54.1 9.3 %gather_fusion.3 = bf16[2048,640]{1,0:T(8,128)(2,1)} fusion(bf16[769,640]{1,0:T(8,128)(2,1)S(1)} %concatenate.11, s32[2048]{0:T(1024)S(1)} %broadcast_clamp_fusion), kind=kCustom, calls=%fused_computation.3 | custom fusion | bytes 5251072 | tf_op jit(solution)/shard_map/gather | solution.py:79
  63.4 7.0 %reshape.112 = bf16[32,64,5,128]{3,2,1,0:T(8,128)(2,1)} reshape(bf16[2048,640]{1,0:T(8,128)(2,1)} %gather_fusion.3) | data formatting | bytes 5242880 | tf_op jit(solution)/shard_map/reshape | solution.py:79
  70.4 4.5 copy.57
  74.9 23.6 %all-to-all-done.1 = bf16[32,48,5,128]{3,1,2,0:T(8,128)(2,1)S(1)} async-done(((bf16[32,48,5,128]{3,1,2,0:T(8,128)(2,1)}), bf16[32,48,5,128]{3,1,2,0:T(8,128)(2,1)S(1)}, u32[]{:S(2)}, u32[]{:S(2)}) %all-to-all-start.1) | async-done | bytes 1966112 | tf_op jit(solution)/shard_map/all_to_all | solution.py:86
  98.5 1.4 copy-done
  99.9 7.0 %all-to-all-start.3 = ((bf16[32,64,5,128]{3,1,2,0:T(8,128)(2,1)}), bf16[32,64,5,128]{3,1,2,0:T(8,128)(2,1)}, u32[]{:S(2)}, u32[]{:S(2)}) async-start(bf16[32,64,5,128]{3,1,2,0:T(8,128)(2,1)} %copy.57), calls=%async_computation.3 | async-start | bytes 5242880 | tf_op jit(solution)/shard_map/all_to_all | solution.py:89
  106.9 1.3 concatenate.10
  108.2 9.3 %gather_fusion.2 = bf16[2048,640]{1,0:T(8,128)(2,1)} fusion(bf16[769,640]{1,0:T(8,128)(2,1)S(1)} %concatenate.10, s32[2048]{0:T(1024)S(1)} %broadcast_clamp_fusion), kind=kCustom, calls=%fused_computation.2 | custom fusion | bytes 5251072 | tf_op jit(solution)/shard_map/gather | solution.py:76
  117.5 7.0 %reshape.110 = bf16[32,64,5,128]{3,2,1,0:T(8,128)(2,1)} reshape(bf16[2048,640]{1,0:T(8,128)(2,1)} %gather_fusion.2) | data formatting | bytes 5242880 | tf_op jit(solution)/shard_map/reshape | solution.py:76
  124.5 4.4 copy.55
  128.9 37.9 %all-to-all-done.3 = bf16[32,64,5,128]{3,1,2,0:T(8,128)(2,1)} async-done(((bf16[32,64,5,128]{3,1,2,0:T(8,128)(2,1)}), bf16[32,64,5,128]{3,1,2,0:T(8,128)(2,1)}, u32[]{:S(2)}, u32[]{:S(2)}) %all-to-all-start.3) | async-done | bytes 2621472 | tf_op jit(solution)/shard_map/all_to_all | solution.py:89
  166.8 7.4 %all-to-all-start.2 = ((bf16[32,64,5,128]{3,1,2,0:T(8,128)(2,1)}), bf16[32,64,5,128]{3,1,2,0:T(8,128)(2,1)S(1)}, u32[]{:S(2)}, u32[]{:S(2)}) async-start(bf16[32,64,5,128]{3,1,2,0:T(8,128)(2,1)} %copy.55), calls=%async_computation.2 | async-start | bytes 5242880 | tf_op jit(solution)/shard_map/all_to_all | solution.py:88
  174.2 0.5 broadcast.149
  174.7 0.8 reduce.10
  175.5 0.1 reshape.199
  175.6 0.1 gt.14
  175.7 3.1 copy.54
  178.8 4.0 copy.58
  182.8 51.1 %all-to-all-done.2 = bf16[32,64,5,128]{3,1,2,0:T(8,128)(2,1)S(1)} async-done(((bf16[32,64,5,128]{3,1,2,0:T(8,128)(2,1)}), bf16[32,64,5,128]{3,1,2,0:T(8,128)(2,1)S(1)}, u32[]{:S(2)}, u32[]{:S(2)}) %all-to-all-start.2) | async-done | bytes 2621472 | tf_op jit(solution)/shard_map/all_to_all | solution.py:88
  233.9 2.3 copy.56
  236.2 78.1 %while.10 = (s32[]{:T(128)}, bf16[3,512,5,128]{3,1,0,2:T(8,128)(2,1)}, pred[5,2048]{1,0:T(8,128)(4,1)S(1)}, bf16[3,512,5,128]{3,1,0,2:T(8,128)(2,1)}, bf16[2048,...) while((s32[]{:T(128)}, bf16[3,512,5,128]{3,1,0,2:T(8,128)(2,1)}, ...), condition=%wide.region_11.12_spmd, body=%wide.region_8.11_spmd.sunk | while | flops 2716141568 | bytes 59014248 | solution.py:42
  236.2 15.3 %fusion.61 = (f32[5,512]{1,0:T(8,128)S(1)}, f32[5,512,2048]{2,1,0:T(8,128)}) fusion(pred[5,2048]{1,0:T(8,128)(4,1)S(1)} %get-tuple-element.133, bf16[2048,5,128]{2,0,1:T(8,128)(2,1)} %get-tuple-element.135, bf16[3,512,5,128]{3,1,0,2:T(8,128)(2,1)} %get-tuple-element.134, s32[]{:T(128)} %get-tuple-element.124), kind=kOutput, calls=%fused_computation.67.clone.1 | convolution fusion | flops 1363150848 | bytes 24269312 | tf_op jit(solution)/shard_map/while/body/eval_jaxpr/sub | solution.py:33
  251.5 10.7 %fusion.62 = bf16[3,512,5,128]{3,1,0,2:T(8,128)(2,1)} fusion(bf16[3,512,5,128]{3,1,0,2:T(8,128)(2,1)} %get-tuple-element.125, s32[]{:T(128)} %get-tuple-element.124, bf16[2048,5,128]{2,0,1:T(8,128)(2,1)S(1)} %copy-done.1, f32[5,512,2048]{2,1,0:T(8,128)} %get-tuple-element.115, f32[5,512]{1,0:T(8,128)S(1)} %get-tuple-element.116), kind=kOutput, calls=%fused_computation.19.clone.1 | convolution fusion | flops 1352990720 | bytes 24259072 | tf_op jit(solution)/shard_map/while/body/eval_jaxpr/hqk,khd->qhd/dot_general | solution.py:35
  262.2 15.3 %fusion.61 = (f32[5,512]{1,0:T(8,128)S(1)}, f32[5,512,2048]{2,1,0:T(8,128)}) fusion(pred[5,2048]{1,0:T(8,128)(4,1)S(1)} %get-tuple-element.133, bf16[2048,5,128]{2,0,1:T(8,128)(2,1)} %get-tuple-element.135, bf16[3,512,5,128]{3,1,0,2:T(8,128)(2,1)} %get-tuple-element.134, s32[]{:T(128)} %get-tuple-element.124), kind=kOutput, calls=%fused_computation.67.clone.1 | convolution fusion | flops 1363150848 | bytes 24269312 | tf_op jit(solution)/shard_map/while/body/eval_jaxpr/sub | solution.py:33
  277.5 10.7 %fusion.62 = bf16[3,512,5,128]{3,1,0,2:T(8,128)(2,1)} fusion(bf16[3,512,5,128]{3,1,0,2:T(8,128)(2,1)} %get-tuple-element.125, s32[]{:T(128)} %get-tuple-element.124, bf16[2048,5,128]{2,0,1:T(8,128)(2,1)S(1)} %copy-done.1, f32[5,512,2048]{2,1,0:T(8,128)} %get-tuple-element.115, f32[5,512]{1,0:T(8,128)S(1)} %get-tuple-element.116), kind=kOutput, calls=%fused_computation.19.clone.1 | convolution fusion | flops 1352990720 | bytes 24259072 | tf_op jit(solution)/shard_map/while/body/eval_jaxpr/hqk,khd->qhd/dot_general | solution.py:35
  288.3 15.3 %fusion.61 = (f32[5,512]{1,0:T(8,128)S(1)}, f32[5,512,2048]{2,1,0:T(8,128)}) fusion(pred[5,2048]{1,0:T(8,128)(4,1)S(1)} %get-tuple-element.133, bf16[2048,5,128]{2,0,1:T(8,128)(2,1)} %get-tuple-element.135, bf16[3,512,5,128]{3,1,0,2:T(8,128)(2,1)} %get-tuple-element.134, s32[]{:T(128)} %get-tuple-element.124), kind=kOutput, calls=%fused_computation.67.clone.1 | convolution fusion | flops 1363150848 | bytes 24269312 | tf_op jit(solution)/shard_map/while/body/eval_jaxpr/sub | solution.py:33
  303.5 10.7 %fusion.62 = bf16[3,512,5,128]{3,1,0,2:T(8,128)(2,1)} fusion(bf16[3,512,5,128]{3,1,0,2:T(8,128)(2,1)} %get-tuple-element.125, s32[]{:T(128)} %get-tuple-element.124, bf16[2048,5,128]{2,0,1:T(8,128)(2,1)S(1)} %copy-done.1, f32[5,512,2048]{2,1,0:T(8,128)} %get-tuple-element.115, f32[5,512]{1,0:T(8,128)S(1)} %get-tuple-element.116), kind=kOutput, calls=%fused_computation.19.clone.1 | convolution fusion | flops 1352990720 | bytes 24259072 | tf_op jit(solution)/shard_map/while/body/eval_jaxpr/hqk,khd->qhd/dot_general | solution.py:35
  314.3 3.2 copy.61
  317.4 7.3 %all-to-all-start.4 = ((bf16[32,48,5,128]{3,1,2,0:T(8,128)(2,1)}), bf16[32,48,5,128]{3,1,2,0:T(8,128)(2,1)S(1)}, u32[]{:S(2)}, u32[]{:S(2)}) async-start(bf16[32,48,5,128]{3,1,2,0:T(8,128)(2,1)} %copy.61), calls=%async_computation.4 | async-start | bytes 3932160 | tf_op jit(solution)/shard_map/all_to_all | solution.py:93
  324.7 0.3 reduce-scatter.4.cloned.1.call-start
  325.0 45.6 %all-to-all-done.4 = bf16[32,48,5,128]{3,1,2,0:T(8,128)(2,1)S(1)} async-done(((bf16[32,48,5,128]{3,1,2,0:T(8,128)(2,1)}), bf16[32,48,5,128]{3,1,2,0:T(8,128)(2,1)S(1)}, u32[]{:S(2)}, u32[]{:S(2)}) %all-to-all-start.4) | async-done | bytes 1966112 | tf_op jit(solution)/shard_map/all_to_all | solution.py:93
  370.6 0.8 copy.62
  371.4 0.5 copy.76
  371.9 2.8 gather_fusion.4
  374.7 11.3 %convolution_convert_fusion = bf16[768,5120]{1,0:T(8,128)(2,1)} fusion(bf16[768,640]{1,0:T(8,128)(2,1)S(1)} %gather_fusion.4, bf16[640,5120]{1,0:T(8,128)(2,1)} %param.15), kind=kOutput, calls=%fused_computation.29 | convolution fusion | flops 5037096960 | bytes 15400960 | tf_op jit(solution)/shard_map/dot_general | solution.py:97
  386.0 10.6 %copy.63 = bf16[768,5120]{0,1:T(8,128)(2,1)} copy(bf16[768,5120]{1,0:T(8,128)(2,1)} %convolution_convert_fusion) | data formatting | bytes 15728640
  396.6 51.5 %reduce-scatter.4.cloned.1.call-done = bf16[640,768]{1,0:T(8,128)(2,1)} async-done(((bf16[5120,768]{1,0:T(8,128)(2,1)}), bf16[640,768]{1,0:T(8,128)(2,1)}) %reduce-scatter.4.cloned.1.call-update) | async-done | bytes 983056
  448.1 2.2 copy.64
  (41 shorter events, 0.3 us)
Async XLA Ops:
  7.7 0.7 copy-start.5
  7.7 4.3 copy-start.7
  8.0 18.1 %copy-start.6 = (s32[768,1]{0,1:T(1,128)S(1)}, s32[768,1]{0,1:T(1,128)}, u32[]{:S(2)}) copy-start(s32[768,1]{0,1:T(1,128)} %param.12) | copy-start | bytes 9220
  8.0 23.7 %copy-start.2 = (bf16[768,640]{1,0:T(8,128)(2,1)S(1)}, bf16[768,640]{1,0:T(8,128)(2,1)}, u32[]{:S(2)}) copy-start(bf16[768,640]{1,0:T(8,128)(2,1)} %param.9) | copy-start | bytes 2949124
  14.2 29.1 %all-to-all-start = ((s32[32,1,320]{2,1,0:T(1,128)}), s32[32,1,320]{2,1,0:T(1,128)S(1)}, u32[]{:S(2)}, u32[]{:S(2)}) async-start(s32[32,1,320]{2,1,0:T(1,128)} %reshape.198), calls=%async_computation | async-start | bytes 98304 | tf_op jit(solution)/shard_map/all_to_all | solution.py:90
  28.3 3.4 copy-start.3
  43.3 55.2 %all-to-all-start.1 = ((bf16[32,48,5,128]{3,1,2,0:T(8,128)(2,1)}), bf16[32,48,5,128]{3,1,2,0:T(8,128)(2,1)S(1)}, u32[]{:S(2)}, u32[]{:S(2)}) async-start(bf16[32,48,5,128]{3,1,2,0:T(8,128)(2,1)} %copy.53), calls=%async_computation.1 | async-start | bytes 3932160 | tf_op jit(solution)/shard_map/all_to_all | solution.py:86
  98.5 1.4 copy-start
  99.9 66.9 %all-to-all-start.3 = ((bf16[32,64,5,128]{3,1,2,0:T(8,128)(2,1)}), bf16[32,64,5,128]{3,1,2,0:T(8,128)(2,1)}, u32[]{:S(2)}, u32[]{:S(2)}) async-start(bf16[32,64,5,128]{3,1,2,0:T(8,128)(2,1)} %copy.57), calls=%async_computation.3 | async-start | bytes 5242880 | tf_op jit(solution)/shard_map/all_to_all | solution.py:89
  166.8 67.1 %all-to-all-start.2 = ((bf16[32,64,5,128]{3,1,2,0:T(8,128)(2,1)}), bf16[32,64,5,128]{3,1,2,0:T(8,128)(2,1)S(1)}, u32[]{:S(2)}, u32[]{:S(2)}) async-start(bf16[32,64,5,128]{3,1,2,0:T(8,128)(2,1)} %copy.55), calls=%async_computation.2 | async-start | bytes 5242880 | tf_op jit(solution)/shard_map/all_to_all | solution.py:88
  236.2 15.3 %copy-start.1 = (bf16[2048,5,128]{2,0,1:T(8,128)(2,1)S(1)}, bf16[2048,5,128]{2,0,1:T(8,128)(2,1)}, u32[]{:S(2)}) copy-start(bf16[2048,5,128]{2,0,1:T(8,128)(2,1)} %get-tuple-element.136) | copy-start | bytes 7864324 | tf_op jit(solution)/shard_map/while
  262.2 15.3 %copy-start.1 = (bf16[2048,5,128]{2,0,1:T(8,128)(2,1)S(1)}, bf16[2048,5,128]{2,0,1:T(8,128)(2,1)}, u32[]{:S(2)}) copy-start(bf16[2048,5,128]{2,0,1:T(8,128)(2,1)} %get-tuple-element.136) | copy-start | bytes 7864324 | tf_op jit(solution)/shard_map/while
  288.3 15.3 %copy-start.1 = (bf16[2048,5,128]{2,0,1:T(8,128)(2,1)S(1)}, bf16[2048,5,128]{2,0,1:T(8,128)(2,1)}, u32[]{:S(2)}) copy-start(bf16[2048,5,128]{2,0,1:T(8,128)(2,1)} %get-tuple-element.136) | copy-start | bytes 7864324 | tf_op jit(solution)/shard_map/while
  317.4 7.6 %copy-start.4 = (s32[768]{0:T(1024)S(1)}, s32[768]{0:T(1024)}, u32[]{:S(2)}) copy-start(s32[768]{0:T(1024)} %copy-done.3) | copy-start | bytes 9220
  317.4 53.2 %all-to-all-start.4 = ((bf16[32,48,5,128]{3,1,2,0:T(8,128)(2,1)}), bf16[32,48,5,128]{3,1,2,0:T(8,128)(2,1)S(1)}, u32[]{:S(2)}, u32[]{:S(2)}) async-start(bf16[32,48,5,128]{3,1,2,0:T(8,128)(2,1)} %copy.61), calls=%async_computation.4 | async-start | bytes 3932160 | tf_op jit(solution)/shard_map/all_to_all | solution.py:93
  324.7 123.4 %reduce-scatter.4.cloned.1.call-start = ((), (), s32[]{:S(2)}) async-start(), calls=%async_computation.6 | async-start | bytes 8847360
Sparse Core Ops, SparseCore 0:
  396.7 51.3 reduce-scatter.3
where the time goes:
time: 459 us; the launch traced here: 457 us
  waiting for transfers between devices  210 us (46%)
  local copies, waits for them, and re-layouts  97.1 us (21%)
  matrix products  89.3 us (19%)
  starting transfers between devices  43 us (9%)
  between operations  13.8 us (3%)
    unnamed x2, waiting for transfers between devices  51.5 us
    all_to_all x1, waiting for transfers between devices, per_device(): lax.all_to_all(key_send, 'ctx', split_axis=0, concat_axis=0, tiled=True)  51.1 us
    sub x3, matrix products, one_block(): expon = jnp.exp(scores - peak)  45.8 us
    all_to_all x1, waiting for transfers between devices, per_device(): lax.all_to_all(answer, 'ctx', split_axis=0, concat_axis=0, tiled=True)  45.6 us
    all_to_all x1, waiting for transfers between devices, per_device(): lax.all_to_all(value_send, 'ctx', split_axis=0, concat_axis=0, tiled=True)  37.9 us
    dot_general x3, matrix products, one_block(): jnp.einsum('hqk,khd->qhd', weights, value_rows, preferred_element_type=jn...  32.2 us
    all_to_all x1, waiting for transfers between devices, per_device(): lax.all_to_all(query_send, 'ctx', split_axis=0, concat_axis=0, tiled=True)  23.6 us
    unnamed x20, local copies, waits for them, and re-layouts  15.6 us
  transfers between devices with their start and end apart: 6, of which 5 were waited for; matrix products, arithmetic and copies ran while one was open for 15% of the time, Pallas kernels for 0%

commit v1 on v0

v1 whole, which is shorter than its diff:
```python
import functools
import math

import jax
import jax.numpy as jnp
from jax import lax
from jax.experimental import pallas as pl
from jax.experimental.pallas import tpu as pltpu
from jax.sharding import PartitionSpec as P

HDIM = 128
PICKS_HERE = 4
KEEP = 40
STEP = 8
DEAD = 64.0
ALARM = 256.0
CHUNKS = ((0, 3), (3, 5))
F32, BF16 = jnp.float32, jnp.bfloat16


def params(*kinds):
    return pltpu.CompilerParams(
        dimension_semantics=kinds or None, vmem_limit_bytes=56 * 1024 * 1024
    )


def cost(flops, moved, exps=0):
    return pl.CostEstimate(flops=int(flops), bytes_accessed=int(moved), transcendentals=int(exps))


def plan_kernel(slots, qlab_ref, klab_ref, pattern_ref, qpos_ref, kpos_ref, kcount_ref, most_ref, code_ref):
    owners, rows = qpos_ref.shape
    owner = lax.broadcasted_iota(jnp.int32, (owners, rows), 0)
    q_in = qlab_ref[...] == owner
    klab = jnp.broadcast_to(klab_ref[...], (owners, rows))
    pattern = pattern_ref[...]
    k_in = klab == pattern[:, 0:1]
    for j in range(1, pattern.shape[1]):
        k_in = jnp.logical_or(k_in, klab == pattern[:, j : j + 1])
    earlier = (
        lax.broadcasted_iota(jnp.int32, (rows, rows), 0) < lax.broadcasted_iota(jnp.int32, (rows, rows), 1)
    ).astype(F32).astype(BF16)
    q_one = q_in.astype(F32)
    k_one = k_in.astype(F32)
    both = jnp.concatenate([q_one, k_one], axis=0).astype(BF16)
    before = jnp.dot(both, earlier, preferred_element_type=F32)
    q_before, k_before = before[:owners], before[owners:]
    qpos_ref[...] = jnp.where(q_in, q_before, -1.0).astype(jnp.int32)
    kpos_ref[...] = jnp.where(k_in, k_before, -1.0).astype(jnp.int32)
    counts = jnp.sum(k_one, axis=1, keepdims=True)
    kcount_ref[...] = jnp.broadcast_to(counts, kcount_ref.shape).astype(jnp.int32)
    most_ref[...] = jnp.broadcast_to(
        jnp.max(counts, axis=0, keepdims=True), most_ref.shape
    ).astype(jnp.int32)
    named = lax.broadcasted_iota(jnp.int32, (owners, 128), 0).astype(F32).astype(BF16)
    over_owner = (((0,), (0,)), ((), ()))
    label_col = lax.dot_general(q_one.astype(BF16), named, over_owner, preferred_element_type=F32)
    place_col = lax.dot_general(
        (q_one * q_before).astype(BF16),
        jnp.ones((owners, 128), BF16),
        over_owner,
        preferred_element_type=F32,
    )
    code_ref[...] = (label_col * slots + place_col).astype(jnp.int32)


def plan(qlab, klab, pattern, slots):
    owners, rows = pattern.shape[0], qlab.shape[1]
    return pl.pallas_call(
        functools.partial(plan_kernel, slots),
        out_shape=(
            jax.ShapeDtypeStruct((owners, rows), jnp.int32),
            jax.ShapeDtypeStruct((owners, rows), jnp.int32),
            jax.ShapeDtypeStruct((owners, 128), jnp.int32),
            jax.ShapeDtypeStruct((8, 128), jnp.int32),
            jax.ShapeDtypeStruct((rows, 128), jnp.int32),
        ),
        compiler_params=params(),
        cost_estimate=cost(4 * owners * rows * rows, 1 << 20),
        name="plan",
    )(qlab, klab, pattern)


def picked(pos_ref, slots):
    slot = lax.broadcasted_iota(jnp.int32, (slots, pos_ref.shape[1]), 0)
    parts = [jnp.where(pos_ref[i : i + 1, :] == slot, 1.0, 0.0) for i in range(STEP)]
    return jnp.concatenate(parts, axis=0).astype(BF16)


def pack_kernel(columns, qslots, kslots, *refs):
    qpos_ref, kpos_ref, kcount_ref, most_ref, q_ref, k_ref, v_ref, out_ref = refs
    width = out_ref.shape[2]
    if qslots:
        q_rows = jnp.dot(picked(qpos_ref, qslots), q_ref[:, columns], preferred_element_type=F32)
    pick = picked(kpos_ref, kslots)
    k_rows = jnp.dot(pick, k_ref[:, columns], preferred_element_type=F32)
    v_rows = jnp.dot(pick, v_ref[:, columns], preferred_element_type=F32)
    slot = lax.broadcasted_iota(jnp.int32, (kslots, width), 0)
    fits = most_ref[0:1, 0:1] <= kslots
    for i in range(STEP):
        live = slot < kcount_ref[i : i + 1, 0:1]
        mine = [
            jnp.where(fits, jnp.where(live, k_rows[i * kslots : (i + 1) * kslots], DEAD), ALARM),
            v_rows[i * kslots : (i + 1) * kslots],
        ]
        if qslots:
            mine.insert(0, q_rows[i * qslots : (i + 1) * qslots])
        out_ref[i] = jnp.concatenate(mine, axis=0).astype(BF16)


def pack(qpos, kpos, kcount, most, queries, keys, values, chunk, qslots, kslots):
    owners, rows = qpos.shape
    width = (chunk[1] - chunk[0]) * HDIM
    data = pl.BlockSpec((rows, queries.shape[1]), lambda i: (0, 0))
    total = qslots + 2 * kslots
    columns = slice(chunk[0] * HDIM, chunk[1] * HDIM)
    return pl.pallas_call(
        functools.partial(pack_kernel, columns, qslots, kslots),
        grid=(owners // STEP,),
        in_specs=[
            pl.BlockSpec((STEP, rows), lambda i: (i, 0)),
            pl.BlockSpec((STEP, rows), lambda i: (i, 0)),
            pl.BlockSpec((STEP, 128), lambda i: (i, 0)),
            pl.BlockSpec((8, 128), lambda i: (0, 0)),
            data,
            data,
            data,
        ],
        out_specs=pl.BlockSpec((STEP, total, width), lambda i: (i, 0, 0)),
        out_shape=jax.ShapeDtypeStruct((owners, total, width), BF16),
        compiler_params=params("arbitrary"),
        cost_estimate=cost(2 * owners * total * rows * width, 2 * owners * total * width),
        name="pack",
    )(qpos, kpos, kcount, most, queries, keys, values)


def attend_kernel(qslots, kslots, sources, over_ref, got_ref, extra_ref, out_ref, key_ref, value_ref):
    block = pl.program_id(1)
    over = over_ref[0]
    members = got_ref.shape[0]
    base = members * kslots

    def lay(rows, slots):
        rows = rows.astype(F32)
        keys = rows[:, :slots, :].reshape(-1, HDIM)
        dead = keys > DEAD / 2
        span = slice(0, members * slots)
        key_ref[span, :HDIM] = keys.astype(BF16)
        key_ref[span, HDIM:] = jnp.where(dead, -1e30, 0.0).astype(BF16)
        value_ref[span, :HDIM] = rows[:, slots:, :].reshape(-1, HDIM).astype(BF16)
        value_ref[span, HDIM:] = jnp.where(dead, 0.0, 1.0).astype(BF16)

    @pl.when(jnp.logical_and(block == 0, over == 0))
    def _():
        lay(got_ref[:, qslots:, :], kslots)

    @pl.when(jnp.logical_and(block == 0, over > 0))
    def _():
        lay(extra_ref[...], extra_ref.shape[1] // 2)

    def result(rows):
        query = got_ref[pl.ds(block * sources, sources), :qslots, :].reshape(-1, HDIM)
        query = jnp.concatenate([query, jnp.ones_like(query)], axis=1)
        scores = lax.dot_general(
            query, key_ref[:rows, :], (((1,), (1,)), ((), ())), preferred_element_type=F32
        )
        peak = jnp.max(scores, axis=1, keepdims=True)
        expon = jnp.exp2((scores - peak) * (math.log2(math.e) / math.sqrt(HDIM))).astype(BF16)
        both = jnp.dot(expon, value_ref[:rows, :], preferred_element_type=F32)
        answer = both[:, :HDIM] / both[:, HDIM:]
        out_ref[...] = answer.astype(BF16).reshape(sources, qslots, HDIM)

    @pl.when(over == 0)
    def _():
        result(base)

    @pl.when(over > 0)
    def _():
        result(key_ref.shape[0])


def attend(over, got, extra, chunk, qslots, kslots):
    members, total, width = got.shape
    heads = width // HDIM
    sources = 8
    more = extra.shape[1]
    keys = members * more // 2
    return pl.pallas_call(
        functools.partial(attend_kernel, qslots, kslots, sources),
        grid_spec=pltpu.PrefetchScalarGridSpec(
            num_scalar_prefetch=1,
            grid=(heads, members // sources),
            in_specs=[
                pl.BlockSpec((members, total, HDIM), lambda h, i, over_ref: (0, 0, h)),
                pl.BlockSpec((members, more, HDIM), lambda h, i, over_ref: (0, 0, h + chunk[0])),
            ],
            out_specs=pl.BlockSpec((sources, qslots, HDIM), lambda h, i, over_ref: (i, 0, h)),
            scratch_shapes=[
                pltpu.VMEM((keys, 2 * HDIM), BF16),
                pltpu.VMEM((keys, 2 * HDIM), BF16),
            ],
        ),
        out_shape=jax.ShapeDtypeStruct((members, qslots, width), BF16),
        compiler_params=params("arbitrary", "arbitrary"),
        cost_estimate=cost(
            8 * members * qslots * keys * width, 2 * members * total * width, members * qslots * keys * heads
        ),
        name="attend",
    )(over, got, extra)


def unpack_kernel(code_ref, got_ref, out_ref):
    rows = code_ref.shape[0]
    slots = got_ref.shape[0] * got_ref.shape[1]
    slot = lax.broadcasted_iota(jnp.int32, (rows, slots), 1)
    pick = jnp.where(code_ref[:, 0:1] == slot, 1.0, 0.0).astype(BF16)
    got = got_ref[...].reshape(slots, got_ref.shape[2])
    out_ref[...] = jnp.dot(pick, got, preferred_element_type=F32).astype(BF16)


def unpack(code, got):
    rows, width = code.shape[0], got.shape[2]
    return pl.pallas_call(
        unpack_kernel,
        out_shape=jax.ShapeDtypeStruct((rows, width), BF16),
        compiler_params=params(),
        cost_estimate=cost(2 * rows * got.shape[0] * got.shape[1] * width, 2 * got.size),
        name="unpack",
    )(code, got)


def project_kernel(rows_used, counts, *refs):
    groups, pieces = counts
    part_refs, weight_refs = refs[:pieces], refs[pieces : pieces + groups]
    out_ref, lined_ref, arrived = refs[-3:]
    first, end = rows_used
    depth = end - first

    @pl.when(pl.program_id(0) == 0)
    def _():
        copies = [
            pltpu.make_async_copy(
                weight_refs[k].at[first:end, :],
                lined_ref.at[k * depth : (k + 1) * depth, :],
                arrived.at[k],
            )
            for k in range(groups)
        ]
        for copy in copies:
            copy.start()
        for copy in copies:
            copy.wait()

    lined = jnp.concatenate([part_ref[...] for part_ref in part_refs], axis=1)
    product = jnp.dot(lined, lined_ref[...], preferred_element_type=F32)
    if len(refs) == pieces + groups + 4:
        product += refs[pieces + groups][...]
    out_ref[...] = product.astype(out_ref.dtype)


def project(parts, weights, chunk, before, kind):
    rows = parts[0].shape[0]
    groups, columns = len(weights), weights[0].shape[1]
    rows_used = (chunk[0] * HDIM, chunk[1] * HDIM)
    depth = groups * (rows_used[1] - rows_used[0])
    step = rows // 3
    block = pl.BlockSpec((step, columns), lambda i: (i, 0))
    in_specs = [pl.BlockSpec((step, part.shape[1]), lambda i: (i, 0)) for part in parts]
    in_specs += [pl.BlockSpec(memory_space=pl.ANY)] * groups
    operands = [*parts, *weights]
    if before is not None:
        in_specs.append(block)
        operands.append(before)
    return pl.pallas_call(
        functools.partial(project_kernel, rows_used, (groups, len(parts))),
        grid=(rows // step,),
        in_specs=in_specs,
        out_specs=block,
        out_shape=jax.ShapeDtypeStruct((rows, columns), kind),
        scratch_shapes=[pltpu.VMEM((depth, columns), BF16), pltpu.SemaphoreType.DMA((groups,))],
        compiler_params=params("arbitrary"),
        cost_estimate=cost(2 * rows * depth * columns, 2 * depth * (rows + columns)),
        name="project",
    )(*operands)


def shifts(groups):
    return [(along, core) for core in (0, 1) for along in range(0, groups, 2)]


def own_columns(out_weight, me, groups, which):
    columns = out_weight.shape[1] // groups
    parts = []
    for along, core in shifts(groups)[which]:
        to = lax.rem(jnp.bitwise_xor(me, core) + along, groups)
        block = lax.dynamic_slice_in_dim(out_weight, to * columns, columns, axis=1)
        if along or core:
            block = lax.ppermute(
                block, "head", [(g, ((g ^ core) + along) % groups) for g in range(groups)]
            )
        parts.append(block)
    return parts


def head_gather(rows, groups, meanwhile=None):
    def moved(part, along):
        return lax.ppermute(part, "head", [(g, (g + along) % groups) for g in range(groups)])

    cut = (rows.shape[1] // HDIM + 1) // 2 * HDIM
    after_me, before_me = moved(rows, 2), moved(rows, groups - 2)
    far = [moved(after_me[:, :cut], 2), moved(before_me[:, cut:], groups - 2)]
    if meanwhile is not None:
        after_me, before_me, meanwhile = lax.optimization_barrier((after_me, before_me, meanwhile))
    along_y = [rows, after_me, *far, before_me]
    swapped = [lax.ppermute(part, "head", [(g, g ^ 1) for g in range(groups)]) for part in along_y]
    return along_y + swapped, meanwhile


def per_device(queries, keys, values, query_label, key_label, pattern, out_weight):
    members = lax.axis_size("ctx")
    groups = lax.axis_size("head")
    me = lax.axis_index("head")
    rows = queries.shape[0]
    qslots = 2 * rows // members
    kmost = pattern.shape[1] * PICKS_HERE
    heads = queries.shape[1] // HDIM
    half = slice(0, groups // 2), slice(groups // 2, groups)
    qpos, kpos, kcount, most, code = plan(
        query_label.reshape(1, rows), key_label.reshape(1, rows), pattern, qslots
    )
    after = lax.optimization_barrier
    packed = functools.partial(pack, qpos, kpos, kcount, most, queries, keys, values)

    def exchange(block):
        return lax.all_to_all(block, "ctx", split_axis=0, concat_axis=0, tiled=True)

    def whole(over):
        return exchange(packed((0, heads), 0, kmost))

    def none(over):
        return jnp.zeros((members, 2 * kmost, heads * HDIM), BF16)

    sent0 = packed(CHUNKS[0], qslots, KEEP)
    got0 = exchange(sent0)
    sent1, late_weight = after((packed(CHUNKS[1], qslots, KEEP), out_weight))
    weights = own_columns(late_weight, me, groups, half[0])
    got0, *weights = after((got0, *weights))
    over = jnp.max((got0[:, qslots, 0:1] > (DEAD + ALARM) / 2).astype(jnp.int32), axis=0)
    extra = lax.cond(over[0] > 0, whole, none, over)
    sent1, got0, extra, late_weight = after((sent1, got0, extra, late_weight))
    got1 = exchange(sent1)
    weights += own_columns(late_weight, me, groups, half[1])
    answer0 = attend(over, got0, extra, CHUNKS[0], qslots, KEEP)
    answer0, got1, *weights = after((answer0, got1, *weights))
    back0 = exchange(answer0)
    answer1 = attend(over, got1, extra, CHUNKS[1], qslots, KEEP)
    answer1, back0 = after((answer1, back0))
    back1 = exchange(answer1)
    parts0, _ = head_gather(unpack(code, back0), groups)
    total = project(parts0, weights, CHUNKS[0], None, F32)
    parts1, total = head_gather(unpack(code, back1), groups, total)
    return project(parts1, weights, CHUNKS[1], total, BF16)


def solution(mesh):
    placed = (
        P("ctx", "head"),
        P("ctx", "head"),
        P("ctx", "head"),
        P("ctx", None),
        P("ctx", None),
        P(),
        P("head", None),
    )
    return jax.shard_map(
        per_device, mesh=mesh, in_specs=placed, out_specs=P("ctx", "head"), check_vma=False
    )
```

time: 459 us -> 270 us (0.59)
  waiting for transfers between devices: 210 us -> 113 us
  matrix products: 89.3 us -> 0 us
  local copies, waits for them, and re-layouts: 97.1 us -> 14.7 us
  Pallas kernels: 0 us -> 70.3 us
  starting transfers between devices: 43 us -> 68.2 us
  between operations: 13.8 us -> 1.15 us
    all_to_all x5 -> x4, waiting for transfers between devices: 158 us -> 42.5 us  [exchange(): return lax.all_to_all(block, 'ctx', split_axis=0, concat_axis=0, tiled=True)]
    ppermute x0 -> x25, waiting for transfers between devices: none -> 70.4 us  [the longest x7 49.1 us: own_columns(): lax.ppermute(block, 'head', [(g, ((g ^ core) + along) % groups) for g in...]
    pallas_call x0 -> x9, Pallas kernels: none -> 70.3 us  [the longest x2 34.6 us: attend(): pl.pallas_call(functools.partial(attend_kernel, qslots, kslots, sources),...]
    unnamed x2 -> x0, waiting for transfers between devices: 51.5 us -> none
    sub x3 -> x0, matrix products: 45.8 us -> none  [one_block(): expon = jnp.exp(scores - peak)]
    dot_general x4 -> x0, matrix products: 43.5 us -> none  [the longest x3 32.2 us: one_block(): jnp.einsum('hqk,khd->qhd', weights, value_rows, preferred_element_type=jn...]
    reshape x9 -> x0, local copies, waits for them, and re-layouts: 32.3 us -> none  [the longest x2 11.5 us: per_device(): jnp.concatenate([values, blank])[key_index]]
    ppermute x0 -> x25, starting transfers between devices: none -> 31.3 us  [the longest x7 11.1 us: own_columns(): lax.ppermute(block, 'head', [(g, ((g ^ core) + along) % groups) for g in...]
  transfers between devices with their start and end apart: 6 -> 29, of which waited for: 5 -> 11; matrix products, arithmetic and copies ran while one was open for 15% -> 3% of each run, Pallas kernels for 0% -> 20%
where the time goes in v1:
time: 270 us; the launch traced here: 269 us
  waiting for transfers between devices  113 us (42%)
  Pallas kernels  70.3 us (26%)
  starting transfers between devices  68.2 us (25%)
  local copies, waits for them, and re-layouts  14.7 us (5%)
    ppermute x7, waiting for transfers between devices, own_columns(): lax.ppermute(block, 'head', [(g, ((g ^ core) + along) % groups) for g in...  49.1 us
    all_to_all x4, waiting for transfers between devices, exchange(): return lax.all_to_all(block, 'ctx', split_axis=0, concat_axis=0, tiled=True)  42.5 us
    all_to_all x4, starting transfers between devices, exchange(): return lax.all_to_all(block, 'ctx', split_axis=0, concat_axis=0, tiled=True)  36.9 us
    pallas_call x2, Pallas kernels, attend(): pl.pallas_call(functools.partial(attend_kernel, qslots, kslots, sources),...  34.6 us
    ppermute x8, waiting for transfers between devices, moved(): lax.ppermute(part, 'head', [(g, (g + along) % groups) for g in range(grou...  19.9 us
    pallas_call x2, Pallas kernels, project(): pl.pallas_call(functools.partial(project_kernel, rows_used, (groups, len(...  16.7 us
    ppermute x7, starting transfers between devices, own_columns(): lax.ppermute(block, 'head', [(g, ((g ^ core) + along) % groups) for g in...  11.1 us
    ppermute x8, starting transfers between devices, moved(): lax.ppermute(part, 'head', [(g, (g + along) % groups) for g in range(grou...  11 us
  transfers between devices with their start and end apart: 29, of which 11 were waited for; matrix products, arithmetic and copies ran while one was open for 3% of the time, Pallas kernels for 20%

profile of v1, /device:TPU:1, one launch (start us, length us, event | category | flops | bytes accessed | tf_op | source)
XLA Modules:
  0.0 268.8 jit_solution(14451301100400128727)
XLA Ops:
  0.0 1.4 copy.8.pattern_ref
  1.4 2.3 plan.1
  3.6 6.8 %pack.4 = bf16[32,128,384]{2,1,0:T(8,128)(2,1)} custom-call(s32[32,768]{1,0:T(8,128)S(1)} %get-tuple-element.61.refs_0_, s32[32,768]{1,0:T(8,128)S(1)} %get-tuple-element.62.refs_1_, s32[32,128]{1,0:T(8,128)S(1)} %get-tuple-element.63.refs_2_, s32[8,128]{1,0:T(8,128)S(1)} %get-tuple-element.64.refs_3_, bf16[768,640]{1,0:T(8,128)(2,1)} %refs_4_.3, ...), custom_call_target="tpu_custom_call" | custom-call | flops 2415919104 | bytes 3145728 | tf_op jit(solution)/shard_map/pack/pallas_call | solution.py:117
  10.4 12.3 %all-to-all-start.1 = ((bf16[32,128,384]{2,1,0:T(8,128)(2,1)}), bf16[32,128,384]{2,1,0:T(8,128)(2,1)}, u32[]{:S(2)}, u32[]{:S(2)}) async-start(bf16[32,128,384]{2,1,0:T(8,128)(2,1)} %pack.4), calls=%async_computation.1 | async-start | bytes 6291456 | tf_op jit(solution)/shard_map/all_to_all | solution.py:335
  22.7 3.5 %pack.5 = bf16[32,128,256]{2,1,0:T(8,128)(2,1)} custom-call(s32[32,768]{1,0:T(8,128)S(1)} %get-tuple-element.61.refs_0_, s32[32,768]{1,0:T(8,128)S(1)} %get-tuple-element.62.refs_1_, s32[32,128]{1,0:T(8,128)S(1)} %get-tuple-element.63.refs_2_, s32[8,128]{1,0:T(8,128)S(1)} %get-tuple-element.64.refs_3_, bf16[768,640]{1,0:T(8,128)(2,1)S(1)} %copy-done.23, ...), custom_call_target="tpu_custom_call" | custom-call | flops 1610612736 | bytes 2097152 | tf_op jit(solution)/shard_map/pack/pallas_call | solution.py:117
  26.2 3.1 %constant_dynamic-slice_fusion.4 = (bf16[640,640]{1,0:T(8,128)(2,1)S(1)}, bf16[640,640]{1,0:T(8,128)(2,1)S(1)}, bf16[640,640]{1,0:T(8,128)(2,1)S(1)}, bf16[640,640]{1,0:T(8,128)(2,1)}) fusion(bf16[640,5120]{1,0:T(8,128)(2,1)} %param.15, s32[]{:T(128)S(6)} %select_n.27, s32[]{:T(128)S(6)} %select_n.26, s32[]{:T(128)S(6)} %select_n.25, s32[]{:T(128)S(6)} %select_n.24), kind=kLoop, calls=%fused_computation.6 | loop fusion | bytes 6553616 | tf_op jit(solution)/shard_map/dynamic_slice | solution.py:296
  29.2 1.3 collective-permute-start
  30.5 2.6 collective-permute-start.1
  33.2 1.1 collective-permute-start.2
  34.2 15.3 %collective-permute-done.refs_11_ = bf16[640,640]{1,0:T(8,128)(2,1)S(1)} collective-permute-done((bf16[640,640]{1,0:T(8,128)(2,1)S(1)}, bf16[640,640]{1,0:T(8,128)(2,1)S(1)}, u32[]{:S(2)}, u32[]{:S(2)}) %collective-permute-start) | collective-permute-done | bytes 819232 | tf_op jit(solution)/shard_map/ppermute | solution.py:298
  49.5 18.7 %collective-permute-done.1.refs_12_ = bf16[640,640]{1,0:T(8,128)(2,1)S(1)} collective-permute-done((bf16[640,640]{1,0:T(8,128)(2,1)S(1)}, bf16[640,640]{1,0:T(8,128)(2,1)S(1)}, u32[]{:S(2)}, u32[]{:S(2)}) %collective-permute-start.1) | collective-permute-done | bytes 819232 | tf_op jit(solution)/shard_map/ppermute | solution.py:298
  68.2 0.0 collective-permute-done.2.refs_13_
  68.2 26.0 %all-to-all-done.1.got_ref = bf16[32,128,384]{2,1,0:T(8,128)(2,1)} async-done(((bf16[32,128,384]{2,1,0:T(8,128)(2,1)}), bf16[32,128,384]{2,1,0:T(8,128)(2,1)}, u32[]{:S(2)}, u32[]{:S(2)}) %all-to-all-start.1) | async-done | bytes 3145760 | tf_op jit(solution)/shard_map/all_to_all | solution.py:335
  94.2 1.5 fusion
  96.3 3.1 %conditional.1 = (bf16[32,128,640]{2,1,0:T(8,128)(2,1)}) conditional(s32[]{:T(128)} %convert_element_type.16, () %tuple.19, (s32[32,768]{1,0:T(8,128)S(1)}, s32[32,768]{1,0:T(8,128)S(1)}, s32[32,128]{1,0:T(8,128)S(1)}, s32[8,128]{1,0:T(8,128)S(1)}, bf16[768,640]{1,0:T(8,128)(2,1)}, /*index=5*/bf16[768,640]{1,0:T(8,128)(2,1)}, ...), branch_computations={%region_1.0_spmd, %region_2.0_spmd} | conditional | flops 4026531840 | bytes 15728648 | solution.py:349
  96.3 3.1 %broadcast.20 = bf16[32,128,640]{2,1,0:T(8,128)(2,1)} broadcast(bf16[]{:T(256)} %constant.30.clone), dimensions={} | broadcast | bytes 5242882 | tf_op jit(solution)/shard_map/broadcast.1
  99.4 9.1 %all-to-all-start.2 = ((bf16[32,128,256]{2,1,0:T(8,128)(2,1)}), bf16[32,128,256]{2,1,0:T(8,128)(2,1)}, u32[]{:S(2)}, u32[]{:S(2)}) async-start(bf16[32,128,256]{2,1,0:T(8,128)(2,1)} %pack.5), calls=%async_computation.2 | async-start | bytes 4194304 | tf_op jit(solution)/shard_map/all_to_all | solution.py:335
  108.5 3.9 %constant_dynamic-slice_fusion = (bf16[640,640]{1,0:T(8,128)(2,1)}, bf16[640,640]{1,0:T(8,128)(2,1)}, bf16[640,640]{1,0:T(8,128)(2,1)}, bf16[640,640]{1,0:T(8,128)(2,1)}) fusion(bf16[640,5120]{1,0:T(8,128)(2,1)} %param.15, s32[]{:T(128)S(6)} %select_n.31, s32[]{:T(128)S(6)} %select_n.30, s32[]{:T(128)S(6)} %select_n.29, s32[]{:T(128)S(6)} %select_n.28), kind=kLoop, calls=%fused_computation.2 | loop fusion | bytes 6553616 | tf_op jit(solution)/shard_map/dynamic_slice | solution.py:296
  112.4 1.0 collective-permute-start.3
  113.4 1.1 collective-permute-start.4
  114.5 3.0 %collective-permute-start.5 = (bf16[640,640]{1,0:T(8,128)(2,1)}, bf16[640,640]{1,0:T(8,128)(2,1)S(1)}, u32[]{:S(2)}, u32[]{:S(2)}) collective-permute-start(bf16[640,640]{1,0:T(8,128)(2,1)} %get-tuple-element.92), channel_id=1, source_target_pairs={{0,5},{1,4},{2,7},{3,6},{4,1},{5,0},{6,3},{7,2},{8,13},{9,12},{10,... | collective-permute-start | bytes 2457608 | tf_op jit(solution)/shard_map/ppermute | solution.py:298
  117.5 1.0 collective-permute-start.6
  118.5 20.1 %attend.2 = bf16[32,48,384]{2,1,0:T(8,128)(2,1)} custom-call(s32[1]{0:T(128)} %bitcast.2.over_ref, bf16[32,128,384]{2,1,0:T(8,128)(2,1)} %all-to-all-done.1.got_ref, bf16[32,128,640]{2,1,0:T(8,128)(2,1)S(1)} %copy-done), custom_call_target="tpu_custom_call" | custom-call | flops 9663676416 | bytes 3145728 | tf_op jit(solution)/shard_map/attend/pallas_call | solution.py:188
  138.6 15.2 %collective-permute-done.5.refs_16_ = bf16[640,640]{1,0:T(8,128)(2,1)S(1)} collective-permute-done((bf16[640,640]{1,0:T(8,128)(2,1)}, bf16[640,640]{1,0:T(8,128)(2,1)S(1)}, u32[]{:S(2)}, u32[]{:S(2)}) %collective-permute-start.5) | collective-permute-done | bytes 819232 | tf_op jit(solution)/shard_map/ppermute | solution.py:298
  153.8 3.5 %all-to-all-done.2.got_ref = bf16[32,128,256]{2,1,0:T(8,128)(2,1)} async-done(((bf16[32,128,256]{2,1,0:T(8,128)(2,1)}), bf16[32,128,256]{2,1,0:T(8,128)(2,1)}, u32[]{:S(2)}, u32[]{:S(2)}) %all-to-all-start.2) | async-done | bytes 2097184 | tf_op jit(solution)/shard_map/all_to_all | solution.py:335
  157.3 7.2 %all-to-all-start.3 = ((bf16[32,48,384]{2,1,0:T(8,128)(2,1)}), bf16[32,48,384]{2,1,0:T(8,128)(2,1)}, u32[]{:S(2)}, u32[]{:S(2)}) async-start(bf16[32,48,384]{2,1,0:T(8,128)(2,1)} %attend.2), calls=%async_computation.3 | async-start | bytes 2359296 | tf_op jit(solution)/shard_map/all_to_all | solution.py:335
  164.5 14.5 %attend.3 = bf16[32,48,256]{2,1,0:T(8,128)(2,1)} custom-call(s32[1]{0:T(128)} %bitcast.2.over_ref, bf16[32,128,256]{2,1,0:T(8,128)(2,1)} %all-to-all-done.2.got_ref, bf16[32,128,640]{2,1,0:T(8,128)(2,1)} %get-tuple-element.99.extra_ref), custom_call_target="tpu_custom_call" | custom-call | flops 6442450944 | bytes 2097152 | tf_op jit(solution)/shard_map/attend/pallas_call | solution.py:188
  179.0 13.1 %all-to-all-done.3.got_ref = bf16[32,48,384]{2,1,0:T(8,128)(2,1)} async-done(((bf16[32,48,384]{2,1,0:T(8,128)(2,1)}), bf16[32,48,384]{2,1,0:T(8,128)(2,1)}, u32[]{:S(2)}, u32[]{:S(2)}) %all-to-all-start.3) | async-done | bytes 1179680 | tf_op jit(solution)/shard_map/all_to_all | solution.py:335
  192.1 8.4 %all-to-all-start.4 = ((bf16[32,48,256]{2,1,0:T(8,128)(2,1)}), bf16[32,48,256]{2,1,0:T(8,128)(2,1)S(1)}, u32[]{:S(2)}, u32[]{:S(2)}) async-start(bf16[32,48,256]{2,1,0:T(8,128)(2,1)} %attend.3), calls=%async_computation.4 | async-start | bytes 1572864 | tf_op jit(solution)/shard_map/all_to_all | solution.py:335
  200.5 3.6 %unpack.3.refs_0_ = bf16[768,384]{1,0:T(8,128)(2,1)} custom-call(s32[768,128]{1,0:T(8,128)} %get-tuple-element.60.code_ref, bf16[32,48,384]{2,1,0:T(8,128)(2,1)} %all-to-all-done.3.got_ref), custom_call_target="tpu_custom_call" | custom-call | flops 905969664 | bytes 1179648 | tf_op jit(solution)/shard_map/unpack/pallas_call | solution.py:223
  204.1 1.1 collective-permute-start.9
  205.2 1.6 collective-permute-start.11
  206.8 12.1 %collective-permute-done.9.refs_1_ = bf16[768,384]{1,0:T(8,128)(2,1)S(1)} collective-permute-done((bf16[768,384]{1,0:T(8,128)(2,1)}, bf16[768,384]{1,0:T(8,128)(2,1)S(1)}, u32[]{:S(2)}, u32[]{:S(2)}) %collective-permute-start.9) | collective-permute-done | bytes 589856 | tf_op jit(solution)/shard_map/ppermute | solution.py:307
  218.9 0.1 collective-permute-start.10
  219.0 2.7 collective-permute-start.13
  221.7 0.1 collective-permute-start.14
  221.8 0.4 collective-permute-start.17
  222.3 2.7 %collective-permute-start.12 = (bf16[768,128]{1,0:T(8,128)(2,1)S(1)}, bf16[768,128]{1,0:T(8,128)(2,1)}, u32[]{:S(2)}, u32[]{:S(2)}) collective-permute-start(bf16[768,128]{1,0:T(8,128)(2,1)S(1)} %slice.21), channel_id=1, source_target_pairs={{0,6},{1,7},{2,0},{3,1},{4,2},{5,3},{6,4},{7,5},{8,14},{9,15},{10,... | collective-permute-start | bytes 589832 | tf_op jit(solution)/shard_map/ppermute | solution.py:307
  225.0 3.5 %collective-permute-done.10.refs_2_ = bf16[768,256]{1,0:T(8,128)(2,1)S(1)} collective-permute-done((bf16[768,256]{1,0:T(8,128)(2,1)S(1)}, bf16[768,256]{1,0:T(8,128)(2,1)S(1)}, u32[]{:S(2)}, u32[]{:S(2)}) %collective-permute-start.10) | collective-permute-done | bytes 393248 | tf_op jit(solution)/shard_map/ppermute | solution.py:307
  228.5 3.3 %collective-permute-start.15 = (bf16[768,256]{1,0:T(8,128)(2,1)S(1)}, bf16[768,256]{1,0:T(8,128)(2,1)}, u32[]{:S(2)}, u32[]{:S(2)}) collective-permute-start(bf16[768,256]{1,0:T(8,128)(2,1)S(1)} %collective-permute-done.10.refs_2_), channel_id=1, source_target_pairs={{0,1},{1,0},{2,3},{3,2},{4,5},{5,4},{6,7},{7,6},{8,9},{9,8},{10,11... | collective-permute-start | bytes 1179656 | tf_op jit(solution)/shard_map/ppermute | solution.py:315
  231.8 0.1 collective-permute-start.16
  231.9 0.0 all-to-all-done.4.got_ref
  231.9 0.9 copy-done.11
  232.7 2.8 %unpack.2.refs_0_ = bf16[768,256]{1,0:T(8,128)(2,1)} custom-call(s32[768,128]{1,0:T(8,128)} %get-tuple-element.60.code_ref, bf16[32,48,256]{2,1,0:T(8,128)(2,1)} %copy-done.11), custom_call_target="tpu_custom_call" | custom-call | flops 603979776 | bytes 786432 | tf_op jit(solution)/shard_map/unpack/pallas_call | solution.py:223
  235.6 0.1 collective-permute-start.7
  235.7 0.0 collective-permute-done.16.refs_8_
  235.7 2.7 collective-permute-start.8
  238.3 0.0 collective-permute-done.15.refs_7_
  238.4 0.8 copy-done.13
  239.2 9.0 %project.2.refs_18_ = f32[768,640]{1,0:T(8,128)} custom-call(bf16[768,384]{1,0:T(8,128)(2,1)} %unpack.3.refs_0_, bf16[768,384]{1,0:T(8,128)(2,1)} %copy-done.7, bf16[768,256]{1,0:T(8,128)(2,1)} %copy-done.15, bf16[768,128]{1,0:T(8,128)(2,1)} %collective-permute-done.12.refs_3_, bf16[768,384]{1,0:T(8,128)(2,1)} %copy-done.8, bf16[768,384]{1,0:T(8,128)(2,1)} %copy-done.12, ...), custom_call_target="tpu_custom_call" | custom-call | flops 3019898880 | bytes 8650752 | tf_op jit(solution)/shard_map/project/pallas_call | solution.py:274
  248.2 1.1 collective-permute-start.20
  249.3 0.1 collective-permute-start.18
  249.4 2.7 %collective-permute-start.19 = (bf16[768,128]{1,0:T(8,128)(2,1)S(1)}, bf16[768,128]{1,0:T(8,128)(2,1)S(1)}, u32[]{:S(2)}, u32[]{:S(2)}) collective-permute-start(bf16[768,128]{1,0:T(8,128)(2,1)S(1)} %slice.23), channel_id=1, source_target_pairs={{0,6},{1,7},{2,0},{3,1},{4,2},{5,3},{6,4},{7,5},{8,14},{9,15},{10,... | collective-permute-start | bytes 589832 | tf_op jit(solution)/shard_map/ppermute | solution.py:307
  252.2 0.6 collective-permute-start.21
  252.7 4.3 %collective-permute-done.18.refs_2_ = bf16[768,128]{1,0:T(8,128)(2,1)S(1)} collective-permute-done((bf16[768,128]{1,0:T(8,128)(2,1)S(1)}, bf16[768,128]{1,0:T(8,128)(2,1)S(1)}, u32[]{:S(2)}, u32[]{:S(2)}) %collective-permute-start.18) | collective-permute-done | bytes 196640 | tf_op jit(solution)/shard_map/ppermute | solution.py:307
  257.1 0.8 collective-permute-start.22
  257.9 0.1 collective-permute-start.23
  258.0 1.0 collective-permute-done.22.refs_7_
  259.0 0.4 collective-permute-done.23.refs_8_
  259.4 0.2 copy-done.21
  259.7 0.4 copy-done.22
  260.0 0.1 copy-done.17
  260.2 0.8 copy-done.18
  260.9 7.7 %project.3 = bf16[768,640]{1,0:T(8,128)(2,1)} custom-call(bf16[768,256]{1,0:T(8,128)(2,1)} %unpack.2.refs_0_, bf16[768,256]{1,0:T(8,128)(2,1)} %copy-done.9, bf16[768,128]{1,0:T(8,128)(2,1)} %copy-done.19, bf16[768,128]{1,0:T(8,128)(2,1)} %copy-done.20, bf16[768,256]{1,0:T(8,128)(2,1)} %copy-done.10, bf16[768,256]{1,0:T(8,128)(2,1)} %copy-done.16, ...), custom_call_target="tpu_custom_call" | custom-call | flops 2013265920 | bytes 5767168 | tf_op jit(solution)/shard_map/project/pallas_call | solution.py:274
  (65 shorter events, 0.2 us)
Async XLA Ops:
  10.4 12.3 %copy-start.23 = (bf16[768,640]{1,0:T(8,128)(2,1)S(1)}, bf16[768,640]{1,0:T(8,128)(2,1)}, u32[]{:S(2)}) copy-start(bf16[768,640]{1,0:T(8,128)(2,1)} %refs_4_.3) | copy-start | bytes 2949124
  10.4 12.3 %copy-start.24 = (bf16[768,640]{1,0:T(8,128)(2,1)S(1)}, bf16[768,640]{1,0:T(8,128)(2,1)}, u32[]{:S(2)}) copy-start(bf16[768,640]{1,0:T(8,128)(2,1)} %refs_5_.3) | copy-start | bytes 2949124
  10.4 12.3 %copy-start.25 = (bf16[768,640]{1,0:T(8,128)(2,1)S(1)}, bf16[768,640]{1,0:T(8,128)(2,1)}, u32[]{:S(2)}) copy-start(bf16[768,640]{1,0:T(8,128)(2,1)} %refs_6_.3) | copy-start | bytes 2949124
  10.4 83.8 %all-to-all-start.1 = ((bf16[32,128,384]{2,1,0:T(8,128)(2,1)}), bf16[32,128,384]{2,1,0:T(8,128)(2,1)}, u32[]{:S(2)}, u32[]{:S(2)}) async-start(bf16[32,128,384]{2,1,0:T(8,128)(2,1)} %pack.4), calls=%async_computation.1 | async-start | bytes 6291456 | tf_op jit(solution)/shard_map/all_to_all | solution.py:335
  29.2 20.2 %collective-permute-start = (bf16[640,640]{1,0:T(8,128)(2,1)S(1)}, bf16[640,640]{1,0:T(8,128)(2,1)S(1)}, u32[]{:S(2)}, u32[]{:S(2)}) collective-permute-start(bf16[640,640]{1,0:T(8,128)(2,1)S(1)} %get-tuple-element.97), channel_id=1, source_target_pairs={{0,2},{1,3},{2,4},{3,5},{4,6},{5,7},{6,0},{7,1},{8,10},{9,11},{10,... | collective-permute-start | bytes 2457608 | tf_op jit(solution)/shard_map/ppermute | solution.py:298
  30.5 37.6 %collective-permute-start.1 = (bf16[640,640]{1,0:T(8,128)(2,1)S(1)}, bf16[640,640]{1,0:T(8,128)(2,1)S(1)}, u32[]{:S(2)}, u32[]{:S(2)}) collective-permute-start(bf16[640,640]{1,0:T(8,128)(2,1)S(1)} %get-tuple-element.96), channel_id=1, source_target_pairs={{0,4},{1,5},{2,6},{3,7},{4,0},{5,1},{6,2},{7,3},{8,12},{9,13},{10,... | collective-permute-start | bytes 2457608 | tf_op jit(solution)/shard_map/ppermute | solution.py:298
  33.2 35.0 %collective-permute-start.2 = (bf16[640,640]{1,0:T(8,128)(2,1)S(1)}, bf16[640,640]{1,0:T(8,128)(2,1)S(1)}, u32[]{:S(2)}, u32[]{:S(2)}) collective-permute-start(bf16[640,640]{1,0:T(8,128)(2,1)S(1)} %get-tuple-element.95), channel_id=1, source_target_pairs={{0,6},{1,7},{2,0},{3,1},{4,2},{5,3},{6,4},{7,5},{8,14},{9,15},{10,... | collective-permute-start | bytes 2457608 | tf_op jit(solution)/shard_map/ppermute | solution.py:298
  49.5 46.8 %copy-start.1 = (bf16[640,640]{1,0:T(8,128)(2,1)}, bf16[640,640]{1,0:T(8,128)(2,1)S(1)}, u32[]{:S(2)}) copy-start(bf16[640,640]{1,0:T(8,128)(2,1)S(1)} %collective-permute-done.refs_11_) | copy-start | bytes 2457604
  68.1 28.1 %copy-start.2 = (bf16[640,640]{1,0:T(8,128)(2,1)}, bf16[640,640]{1,0:T(8,128)(2,1)S(1)}, u32[]{:S(2)}) copy-start(bf16[640,640]{1,0:T(8,128)(2,1)S(1)} %collective-permute-done.1.refs_12_) | copy-start | bytes 2457604
  68.2 28.1 %copy-start.3 = (bf16[640,640]{1,0:T(8,128)(2,1)}, bf16[640,640]{1,0:T(8,128)(2,1)S(1)}, u32[]{:S(2)}) copy-start(bf16[640,640]{1,0:T(8,128)(2,1)S(1)} %collective-permute-done.2.refs_13_) | copy-start | bytes 2457604
  99.4 57.9 %all-to-all-start.2 = ((bf16[32,128,256]{2,1,0:T(8,128)(2,1)}), bf16[32,128,256]{2,1,0:T(8,128)(2,1)}, u32[]{:S(2)}, u32[]{:S(2)}) async-start(bf16[32,128,256]{2,1,0:T(8,128)(2,1)} %pack.5), calls=%async_computation.2 | async-start | bytes 4194304 | tf_op jit(solution)/shard_map/all_to_all | solution.py:335
  108.5 10.0 %copy-start = (bf16[32,128,640]{2,1,0:T(8,128)(2,1)S(1)}, bf16[32,128,640]{2,1,0:T(8,128)(2,1)}, u32[]{:S(2)}) copy-start(bf16[32,128,640]{2,1,0:T(8,128)(2,1)} %get-tuple-element.99.extra_ref) | copy-start | bytes 15728644
  112.4 26.2 %collective-permute-start.3 = (bf16[640,640]{1,0:T(8,128)(2,1)}, bf16[640,640]{1,0:T(8,128)(2,1)S(1)}, u32[]{:S(2)}, u32[]{:S(2)}) collective-permute-start(bf16[640,640]{1,0:T(8,128)(2,1)} %get-tuple-element.94), channel_id=1, source_target_pairs={{0,1},{1,0},{2,3},{3,2},{4,5},{5,4},{6,7},{7,6},{8,9},{9,8},{10,11... | collective-permute-start | bytes 2457608 | tf_op jit(solution)/shard_map/ppermute | solution.py:298
  113.4 25.2 %collective-permute-start.4 = (bf16[640,640]{1,0:T(8,128)(2,1)}, bf16[640,640]{1,0:T(8,128)(2,1)S(1)}, u32[]{:S(2)}, u32[]{:S(2)}) collective-permute-start(bf16[640,640]{1,0:T(8,128)(2,1)} %get-tuple-element.93), channel_id=1, source_target_pairs={{0,3},{1,2},{2,5},{3,4},{4,7},{5,6},{6,1},{7,0},{8,11},{9,10},{10,... | collective-permute-start | bytes 2457608 | tf_op jit(solution)/shard_map/ppermute | solution.py:298
  114.5 39.3 %collective-permute-start.5 = (bf16[640,640]{1,0:T(8,128)(2,1)}, bf16[640,640]{1,0:T(8,128)(2,1)S(1)}, u32[]{:S(2)}, u32[]{:S(2)}) collective-permute-start(bf16[640,640]{1,0:T(8,128)(2,1)} %get-tuple-element.92), channel_id=1, source_target_pairs={{0,5},{1,4},{2,7},{3,6},{4,1},{5,0},{6,3},{7,2},{8,13},{9,12},{10,... | collective-permute-start | bytes 2457608 | tf_op jit(solution)/shard_map/ppermute | solution.py:298
  117.5 36.3 %collective-permute-start.6 = (bf16[640,640]{1,0:T(8,128)(2,1)}, bf16[640,640]{1,0:T(8,128)(2,1)}, u32[]{:S(2)}, u32[]{:S(2)}) collective-permute-start(bf16[640,640]{1,0:T(8,128)(2,1)} %get-tuple-element.91), channel_id=1, source_target_pairs={{0,7},{1,6},{2,1},{3,0},{4,3},{5,2},{6,5},{7,4},{8,15},{9,14},{10,... | collective-permute-start | bytes 2457608 | tf_op jit(solution)/shard_map/ppermute | solution.py:298
  138.6 40.4 %copy-start.4 = (bf16[640,640]{1,0:T(8,128)(2,1)}, bf16[640,640]{1,0:T(8,128)(2,1)S(1)}, u32[]{:S(2)}) copy-start(bf16[640,640]{1,0:T(8,128)(2,1)S(1)} %collective-permute-done.3.refs_14_) | copy-start | bytes 2457604
  138.6 40.4 %copy-start.5 = (bf16[640,640]{1,0:T(8,128)(2,1)}, bf16[640,640]{1,0:T(8,128)(2,1)S(1)}, u32[]{:S(2)}) copy-start(bf16[640,640]{1,0:T(8,128)(2,1)S(1)} %collective-permute-done.4.refs_15_) | copy-start | bytes 2457604
  153.8 25.2 %copy-start.6 = (bf16[640,640]{1,0:T(8,128)(2,1)}, bf16[640,640]{1,0:T(8,128)(2,1)S(1)}, u32[]{:S(2)}) copy-start(bf16[640,640]{1,0:T(8,128)(2,1)S(1)} %collective-permute-done.5.refs_16_) | copy-start | bytes 2457604
  157.3 34.8 %all-to-all-start.3 = ((bf16[32,48,384]{2,1,0:T(8,128)(2,1)}), bf16[32,48,384]{2,1,0:T(8,128)(2,1)}, u32[]{:S(2)}, u32[]{:S(2)}) async-start(bf16[32,48,384]{2,1,0:T(8,128)(2,1)} %attend.2), calls=%async_computation.3 | async-start | bytes 2359296 | tf_op jit(solution)/shard_map/all_to_all | solution.py:335
  192.1 39.8 %all-to-all-start.4 = ((bf16[32,48,256]{2,1,0:T(8,128)(2,1)}), bf16[32,48,256]{2,1,0:T(8,128)(2,1)S(1)}, u32[]{:S(2)}, u32[]{:S(2)}) async-start(bf16[32,48,256]{2,1,0:T(8,128)(2,1)} %attend.3), calls=%async_computation.4 | async-start | bytes 1572864 | tf_op jit(solution)/shard_map/all_to_all | solution.py:335
  204.1 14.8 %collective-permute-start.9 = (bf16[768,384]{1,0:T(8,128)(2,1)}, bf16[768,384]{1,0:T(8,128)(2,1)S(1)}, u32[]{:S(2)}, u32[]{:S(2)}) collective-permute-start(bf16[768,384]{1,0:T(8,128)(2,1)} %unpack.3.refs_0_), channel_id=1, source_target_pairs={{0,2},{1,3},{2,4},{3,5},{4,6},{5,7},{6,0},{7,1},{8,10},{9,11},{10,... | collective-permute-start | bytes 1769480 | tf_op jit(solution)/shard_map/ppermute | solution.py:307
  205.2 16.6 %collective-permute-start.11 = (bf16[768,384]{1,0:T(8,128)(2,1)}, bf16[768,384]{1,0:T(8,128)(2,1)S(1)}, u32[]{:S(2)}, u32[]{:S(2)}) collective-permute-start(bf16[768,384]{1,0:T(8,128)(2,1)} %unpack.3.refs_0_), channel_id=1, source_target_pairs={{0,6},{1,7},{2,0},{3,1},{4,2},{5,3},{6,4},{7,5},{8,14},{9,15},{10,... | collective-permute-start | bytes 1769480 | tf_op jit(solution)/shard_map/ppermute | solution.py:307
  218.9 19.4 %copy-start.7 = (bf16[768,384]{1,0:T(8,128)(2,1)}, bf16[768,384]{1,0:T(8,128)(2,1)S(1)}, u32[]{:S(2)}) copy-start(bf16[768,384]{1,0:T(8,128)(2,1)S(1)} %collective-permute-done.9.refs_1_) | copy-start | bytes 1769476
  218.9 9.5 %collective-permute-start.10 = (bf16[768,256]{1,0:T(8,128)(2,1)S(1)}, bf16[768,256]{1,0:T(8,128)(2,1)S(1)}, u32[]{:S(2)}, u32[]{:S(2)}) collective-permute-start(bf16[768,256]{1,0:T(8,128)(2,1)S(1)} %slice.20), channel_id=1, source_target_pairs={{0,2},{1,3},{2,4},{3,5},{4,6},{5,7},{6,0},{7,1},{8,10},{9,11},{10,... | collective-permute-start | bytes 1179656 | tf_op jit(solution)/shard_map/ppermute | solution.py:307
  219.0 16.5 %collective-permute-start.13 = (bf16[768,384]{1,0:T(8,128)(2,1)}, bf16[768,384]{1,0:T(8,128)(2,1)S(1)}, u32[]{:S(2)}, u32[]{:S(2)}) collective-permute-start(bf16[768,384]{1,0:T(8,128)(2,1)} %unpack.3.refs_0_), channel_id=1, source_target_pairs={{0,1},{1,0},{2,3},{3,2},{4,5},{5,4},{6,7},{7,6},{8,9},{9,8},{10,11... | collective-permute-start | bytes 1769480 | tf_op jit(solution)/shard_map/ppermute | solution.py:315
  221.7 16.6 %collective-permute-start.14 = (bf16[768,384]{1,0:T(8,128)(2,1)S(1)}, bf16[768,384]{1,0:T(8,128)(2,1)S(1)}, u32[]{:S(2)}, u32[]{:S(2)}) collective-permute-start(bf16[768,384]{1,0:T(8,128)(2,1)S(1)} %collective-permute-done.9.refs_1_), channel_id=1, source_target_pairs={{0,1},{1,0},{2,3},{3,2},{4,5},{5,4},{6,7},{7,6},{8,9},{9,8},{10,11... | collective-permute-start | bytes 1769480 | tf_op jit(solution)/shard_map/ppermute | solution.py:315
  221.8 16.5 %copy-start.8 = (bf16[768,384]{1,0:T(8,128)(2,1)}, bf16[768,384]{1,0:T(8,128)(2,1)S(1)}, u32[]{:S(2)}) copy-start(bf16[768,384]{1,0:T(8,128)(2,1)S(1)} %collective-permute-done.11.refs_4_) | copy-start | bytes 1769476
  221.8 16.5 %collective-permute-start.17 = (bf16[768,384]{1,0:T(8,128)(2,1)S(1)}, bf16[768,384]{1,0:T(8,128)(2,1)}, u32[]{:S(2)}, u32[]{:S(2)}) collective-permute-start(bf16[768,384]{1,0:T(8,128)(2,1)S(1)} %collective-permute-done.11.refs_4_), channel_id=1, source_target_pairs={{0,1},{1,0},{2,3},{3,2},{4,5},{5,4},{6,7},{7,6},{8,9},{9,8},{10,11... | collective-permute-start | bytes 1769480 | tf_op jit(solution)/shard_map/ppermute | solution.py:315
  222.3 9.5 %collective-permute-start.12 = (bf16[768,128]{1,0:T(8,128)(2,1)S(1)}, bf16[768,128]{1,0:T(8,128)(2,1)}, u32[]{:S(2)}, u32[]{:S(2)}) collective-permute-start(bf16[768,128]{1,0:T(8,128)(2,1)S(1)} %slice.21), channel_id=1, source_target_pairs={{0,6},{1,7},{2,0},{3,1},{4,2},{5,3},{6,4},{7,5},{8,14},{9,15},{10,... | collective-permute-start | bytes 589832 | tf_op jit(solution)/shard_map/ppermute | solution.py:307
  228.5 9.9 %copy-start.15 = (bf16[768,256]{1,0:T(8,128)(2,1)}, bf16[768,256]{1,0:T(8,128)(2,1)S(1)}, u32[]{:S(2)}) copy-start(bf16[768,256]{1,0:T(8,128)(2,1)S(1)} %collective-permute-done.10.refs_2_) | copy-start | bytes 1179652
  228.5 9.9 %collective-permute-start.15 = (bf16[768,256]{1,0:T(8,128)(2,1)S(1)}, bf16[768,256]{1,0:T(8,128)(2,1)}, u32[]{:S(2)}, u32[]{:S(2)}) collective-permute-start(bf16[768,256]{1,0:T(8,128)(2,1)S(1)} %collective-permute-done.10.refs_2_), channel_id=1, source_target_pairs={{0,1},{1,0},{2,3},{3,2},{4,5},{5,4},{6,7},{7,6},{8,9},{9,8},{10,11... | collective-permute-start | bytes 1179656 | tf_op jit(solution)/shard_map/ppermute | solution.py:315
  231.8 3.9 %collective-permute-start.16 = (bf16[768,128]{1,0:T(8,128)(2,1)}, bf16[768,128]{1,0:T(8,128)(2,1)}, u32[]{:S(2)}, u32[]{:S(2)}) collective-permute-start(bf16[768,128]{1,0:T(8,128)(2,1)} %collective-permute-done.12.refs_3_), channel_id=1, source_target_pairs={{0,1},{1,0},{2,3},{3,2},{4,5},{5,4},{6,7},{7,6},{8,9},{9,8},{10,11... | collective-permute-start | bytes 589832 | tf_op jit(solution)/shard_map/ppermute | solution.py:315
  231.9 0.9 copy-start.11
  235.6 12.6 %copy-start.14 = (bf16[768,256]{1,0:T(8,128)(2,1)S(1)}, bf16[768,256]{1,0:T(8,128)(2,1)}, u32[]{:S(2)}) copy-start(bf16[768,256]{1,0:T(8,128)(2,1)} %unpack.2.refs_0_) | copy-start | bytes 1179652
  235.6 2.8 %copy-start.12 = (bf16[768,384]{1,0:T(8,128)(2,1)}, bf16[768,384]{1,0:T(8,128)(2,1)S(1)}, u32[]{:S(2)}) copy-start(bf16[768,384]{1,0:T(8,128)(2,1)S(1)} %collective-permute-done.13.refs_5_) | copy-start | bytes 1769476
  235.6 13.7 %collective-permute-start.7 = (bf16[768,256]{1,0:T(8,128)(2,1)}, bf16[768,256]{1,0:T(8,128)(2,1)S(1)}, u32[]{:S(2)}, u32[]{:S(2)}) collective-permute-start(bf16[768,256]{1,0:T(8,128)(2,1)} %unpack.2.refs_0_), channel_id=1, source_target_pairs={{0,2},{1,3},{2,4},{3,5},{4,6},{5,7},{6,0},{7,1},{8,10},{9,11},{10,... | collective-permute-start | bytes 1179656 | tf_op jit(solution)/shard_map/ppermute | solution.py:307
  235.7 13.6 %collective-permute-start.8 = (bf16[768,256]{1,0:T(8,128)(2,1)}, bf16[768,256]{1,0:T(8,128)(2,1)S(1)}, u32[]{:S(2)}, u32[]{:S(2)}) collective-permute-start(bf16[768,256]{1,0:T(8,128)(2,1)} %unpack.2.refs_0_), channel_id=1, source_target_pairs={{0,6},{1,7},{2,0},{3,1},{4,2},{5,3},{6,4},{7,5},{8,14},{9,15},{10,... | collective-permute-start | bytes 1179656 | tf_op jit(solution)/shard_map/ppermute | solution.py:307
  238.3 0.8 copy-start.13
  248.2 9.8 %collective-permute-start.20 = (bf16[768,256]{1,0:T(8,128)(2,1)S(1)}, bf16[768,256]{1,0:T(8,128)(2,1)S(1)}, u32[]{:S(2)}, u32[]{:S(2)}) collective-permute-start(bf16[768,256]{1,0:T(8,128)(2,1)S(1)} %copy-done.14), channel_id=1, source_target_pairs={{0,1},{1,0},{2,3},{3,2},{4,5},{5,4},{6,7},{7,6},{8,9},{9,8},{10,11... | collective-permute-start | bytes 1179656 | tf_op jit(solution)/shard_map/ppermute | solution.py:315
  249.3 10.1 %copy-start.9 = (bf16[768,256]{1,0:T(8,128)(2,1)}, bf16[768,256]{1,0:T(8,128)(2,1)S(1)}, u32[]{:S(2)}) copy-start(bf16[768,256]{1,0:T(8,128)(2,1)S(1)} %collective-permute-done.7.refs_1_) | copy-start | bytes 1179652
  249.3 10.1 %copy-start.10 = (bf16[768,256]{1,0:T(8,128)(2,1)}, bf16[768,256]{1,0:T(8,128)(2,1)S(1)}, u32[]{:S(2)}) copy-start(bf16[768,256]{1,0:T(8,128)(2,1)S(1)} %collective-permute-done.8.refs_4_) | copy-start | bytes 1179652
  249.3 7.8 %collective-permute-start.18 = (bf16[768,128]{1,0:T(8,128)(2,1)S(1)}, bf16[768,128]{1,0:T(8,128)(2,1)S(1)}, u32[]{:S(2)}, u32[]{:S(2)}) collective-permute-start(bf16[768,128]{1,0:T(8,128)(2,1)S(1)} %slice.22), channel_id=1, source_target_pairs={{0,2},{1,3},{2,4},{3,5},{4,6},{5,7},{6,0},{7,1},{8,10},{9,11},{10,... | collective-permute-start | bytes 589832 | tf_op jit(solution)/shard_map/ppermute | solution.py:307
  249.4 8.5 %collective-permute-start.19 = (bf16[768,128]{1,0:T(8,128)(2,1)S(1)}, bf16[768,128]{1,0:T(8,128)(2,1)S(1)}, u32[]{:S(2)}, u32[]{:S(2)}) collective-permute-start(bf16[768,128]{1,0:T(8,128)(2,1)S(1)} %slice.23), channel_id=1, source_target_pairs={{0,6},{1,7},{2,0},{3,1},{4,2},{5,3},{6,4},{7,5},{8,14},{9,15},{10,... | collective-permute-start | bytes 589832 | tf_op jit(solution)/shard_map/ppermute | solution.py:307
  252.2 7.2 %collective-permute-start.21 = (bf16[768,256]{1,0:T(8,128)(2,1)S(1)}, bf16[768,256]{1,0:T(8,128)(2,1)S(1)}, u32[]{:S(2)}, u32[]{:S(2)}) collective-permute-start(bf16[768,256]{1,0:T(8,128)(2,1)S(1)} %collective-permute-done.7.refs_1_), channel_id=1, source_target_pairs={{0,1},{1,0},{2,3},{3,2},{4,5},{5,4},{6,7},{7,6},{8,9},{9,8},{10,11... | collective-permute-start | bytes 1179656 | tf_op jit(solution)/shard_map/ppermute | solution.py:315
  252.7 6.6 %collective-permute-start.24 = (bf16[768,256]{1,0:T(8,128)(2,1)S(1)}, bf16[768,256]{1,0:T(8,128)(2,1)S(1)}, u32[]{:S(2)}, u32[]{:S(2)}) collective-permute-start(bf16[768,256]{1,0:T(8,128)(2,1)S(1)} %collective-permute-done.8.refs_4_), channel_id=1, source_target_pairs={{0,1},{1,0},{2,3},{3,2},{4,5},{5,4},{6,7},{7,6},{8,9},{9,8},{10,11... | collective-permute-start | bytes 1179656 | tf_op jit(solution)/shard_map/ppermute | solution.py:315
  257.1 2.3 copy-start.19
  257.1 1.9 collective-permute-start.22
  257.9 1.5 copy-start.20
  257.9 1.4 collective-permute-start.23
  258.0 1.4 copy-start.16
  259.0 0.7 copy-start.21
  259.4 0.7 copy-start.22
  259.4 0.8 copy-start.17
  260.2 0.8 copy-start.18

commit v2 on v1

--- a/solution.py
+++ b/solution.py
@@ -15,6 +15,7 @@
 DEAD = 64.0
 ALARM = 256.0
 CHUNKS = ((0, 3), (3, 5))
+BACK = ((0, 0, 3), (1, 3, 5))
 F32, BF16 = jnp.float32, jnp.bfloat16
 
 
@@ -179,9 +180,10 @@
         result(key_ref.shape[0])
 
 
-def attend(over, got, extra, chunk, qslots, kslots):
-    members, total, width = got.shape
-    heads = width // HDIM
+def attend(over, got, extra, start, chunk, qslots, kslots):
+    members, total, _ = got.shape
+    heads = chunk[1] - chunk[0]
+    width = heads * HDIM
     sources = 8
     more = extra.shape[1]
     keys = members * more // 2
@@ -191,7 +193,7 @@
             num_scalar_prefetch=1,
             grid=(heads, members // sources),
             in_specs=[
-                pl.BlockSpec((members, total, HDIM), lambda h, i, over_ref: (0, 0, h)),
+                pl.BlockSpec((members, total, HDIM), lambda h, i, over_ref: (0, 0, h + chunk[0] - start)),
                 pl.BlockSpec((members, more, HDIM), lambda h, i, over_ref: (0, 0, h + chunk[0])),
             ],
             out_specs=pl.BlockSpec((sources, qslots, HDIM), lambda h, i, over_ref: (i, 0, h)),
@@ -303,17 +305,33 @@
 
 
 def head_gather(rows, groups, meanwhile=None):
-    def moved(part, along):
-        return lax.ppermute(part, "head", [(g, (g + along) % groups) for g in range(groups)])
-
-    cut = (rows.shape[1] // HDIM + 1) // 2 * HDIM
-    after_me, before_me = moved(rows, 2), moved(rows, groups - 2)
-    far = [moved(after_me[:, :cut], 2), moved(before_me[:, cut:], groups - 2)]
+    steps = sorted(range(2, groups, 2), key=lambda along: -min(along, groups - along))
+    along_y = {0: rows}
+    for along in steps:
+        along_y[along] = lax.ppermute(rows, "head", [(g, (g + along) % groups) for g in range(groups)])
     if meanwhile is not None:
-        after_me, before_me, meanwhile = lax.optimization_barrier((after_me, before_me, meanwhile))
-    along_y = [rows, after_me, *far, before_me]
-    swapped = [lax.ppermute(part, "head", [(g, g ^ 1) for g in range(groups)]) for part in along_y]
-    return along_y + swapped, meanwhile
+        *held, meanwhile = lax.optimization_barrier((*[along_y[along] for along in steps], meanwhile))
+        along_y.update(zip(steps, held))
+    swapped = {
+        along: lax.ppermute(part, "head", [(g, g ^ 1) for g in range(groups)])
+        for along, part in along_y.items()
+    }
+    parts = [swapped[along] if core else along_y[along] for along, core in shifts(groups)]
+    return parts, meanwhile
+
+
+def unwritten_kernel(out_ref):
+    del out_ref
+
+
+def unwritten(shape):
+    return pl.pallas_call(
+        unwritten_kernel,
+        out_specs=pl.BlockSpec(memory_space=pl.ANY),
+        out_shape=jax.ShapeDtypeStruct(shape, BF16),
+        compiler_params=params(),
+        name="unwritten",
+    )()
 
 
 def per_device(queries, keys, values, query_label, key_label, pattern, out_weight):
@@ -338,7 +356,7 @@
         return exchange(packed((0, heads), 0, kmost))
 
     def none(over):
-        return jnp.zeros((members, 2 * kmost, heads * HDIM), BF16)
+        return unwritten((members, 2 * kmost, heads * HDIM))
 
     sent0 = packed(CHUNKS[0], qslots, KEEP)
     got0 = exchange(sent0)
@@ -350,16 +368,23 @@
     sent1, got0, extra, late_weight = after((sent1, got0, extra, late_weight))
     got1 = exchange(sent1)
     weights += own_columns(late_weight, me, groups, half[1])
-    answer0 = attend(over, got0, extra, CHUNKS[0], qslots, KEEP)
+    gots = got0, got1
+
+    def attended(back):
+        which, *chunk = back
+        return attend(over, gots[which], extra, CHUNKS[which][0], chunk, qslots, KEEP)
+
+    answer0 = attended(BACK[0])
     answer0, got1, *weights = after((answer0, got1, *weights))
+    gots = got0, got1
     back0 = exchange(answer0)
-    answer1 = attend(over, got1, extra, CHUNKS[1], qslots, KEEP)
-    answer1, back0 = after((answer1, back0))
+    answer1, back0 = after((attended(BACK[1]), back0))
     back1 = exchange(answer1)
-    parts0, _ = head_gather(unpack(code, back0), groups)
-    total = project(parts0, weights, CHUNKS[0], None, F32)
-    parts1, total = head_gather(unpack(code, back1), groups, total)
-    return project(parts1, weights, CHUNKS[1], total, BF16)
+    mine1 = unpack(code, back1)
+    parts0, _ = head_gather(unpack(code, back0), groups, mine1)
+    total = project(parts0, weights, BACK[0][1:], None, F32)
+    parts1, total = head_gather(mine1, groups, total)
+    return project(parts1, weights, BACK[1][1:], total, BF16)
 
 
 def solution(mesh):

time: 270 us -> 266 us (0.985)
  starting transfers between devices: 68.2 us -> 64 us
  waiting for transfers between devices: 113 us -> 117 us
  local copies, waits for them, and re-layouts: 14.7 us -> 11 us
    all_to_all x4, waiting for transfers between devices: 42.5 us -> 50.4 us  [exchange(): return lax.all_to_all(block, 'ctx', split_axis=0, concat_axis=0, tiled=True)]
    ppermute x8 -> x6, waiting for transfers between devices: 19.9 us -> 15.6 us  [head_gather(): lax.ppermute(rows, 'head', [(g, (g + along) % groups) for g in range(grou...]
    ppermute x10 -> x8, starting transfers between devices: 9.17 us -> 5.72 us  [head_gather(): lax.ppermute(part, 'head', [(g, g ^ 1) for g in range(groups)])]
    another operation x1 -> x0, local copies, waits for them, and re-layouts: 3.1 us -> none
    ppermute x8 -> x6, starting transfers between devices: 11 us -> 10.2 us  [head_gather(): lax.ppermute(rows, 'head', [(g, (g + along) % groups) for g in range(grou...]
  transfers between devices with their start and end apart: 29 -> 25, of which waited for: 11 -> 12; matrix products, arithmetic and copies ran while one was open for 3% -> 3% of each run, Pallas kernels for 20% -> 20%
where the time goes in v2:
time: 266 us; the launch traced here: 265 us
  waiting for transfers between devices  117 us (44%)
  Pallas kernels  70.4 us (26%)
  starting transfers between devices  64 us (24%)
  local copies, waits for them, and re-layouts  11 us (4%)
    all_to_all x4, waiting for transfers between devices, exchange(): return lax.all_to_all(block, 'ctx', split_axis=0, concat_axis=0, tiled=True)  50.4 us
    ppermute x7, waiting for transfers between devices, own_columns(): lax.ppermute(block, 'head', [(g, ((g ^ core) + along) % groups) for g in...  49 us
    all_to_all x4, starting transfers between devices, exchange(): return lax.all_to_all(block, 'ctx', split_axis=0, concat_axis=0, tiled=True)  36.7 us
    pallas_call x2, Pallas kernels, attend(): pl.pallas_call(functools.partial(attend_kernel, qslots, kslots, sources),...  34.8 us
    pallas_call x2, Pallas kernels, project(): pl.pallas_call(functools.partial(project_kernel, rows_used, (groups, len(...  16.7 us
    ppermute x6, waiting for transfers between devices, head_gather(): lax.ppermute(rows, 'head', [(g, (g + along) % groups) for g in range(grou...  15.6 us
    ppermute x7, starting transfers between devices, own_columns(): lax.ppermute(block, 'head', [(g, ((g ^ core) + along) % groups) for g in...  11.3 us
    ppermute x6, starting transfers between devices, head_gather(): lax.ppermute(rows, 'head', [(g, (g + along) % groups) for g in range(grou...  10.2 us
  transfers between devices with their start and end apart: 25, of which 12 were waited for; matrix products, arithmetic and copies ran while one was open for 3% of the time, Pallas kernels for 20%

profile of v2, /device:TPU:1, one launch (start us, length us, event | category | flops | bytes accessed | tf_op | source)
XLA Modules:
  0.0 265.0 jit_solution(16013315251170516363)
XLA Ops:
  0.0 1.4 copy.8.pattern_ref
  1.4 2.3 plan.1
  3.6 6.7 %pack.4 = bf16[32,128,384]{2,1,0:T(8,128)(2,1)} custom-call(s32[32,768]{1,0:T(8,128)S(1)} %get-tuple-element.65.refs_0_, s32[32,768]{1,0:T(8,128)S(1)} %get-tuple-element.66.refs_1_, s32[32,128]{1,0:T(8,128)S(1)} %get-tuple-element.67.refs_2_, s32[8,128]{1,0:T(8,128)S(1)} %get-tuple-element.68.refs_3_, bf16[768,640]{1,0:T(8,128)(2,1)} %refs_4_.3, ...), custom_call_target="tpu_custom_call" | custom-call | flops 2415919104 | bytes 3145728 | tf_op jit(solution)/shard_map/pack/pallas_call | solution.py:118
  10.4 12.2 %all-to-all-start.1 = ((bf16[32,128,384]{2,1,0:T(8,128)(2,1)}), bf16[32,128,384]{2,1,0:T(8,128)(2,1)}, u32[]{:S(2)}, u32[]{:S(2)}) async-start(bf16[32,128,384]{2,1,0:T(8,128)(2,1)} %pack.4), calls=%async_computation.1 | async-start | bytes 6291456 | tf_op jit(solution)/shard_map/all_to_all | solution.py:353
  22.7 3.4 %pack.5 = bf16[32,128,256]{2,1,0:T(8,128)(2,1)} custom-call(s32[32,768]{1,0:T(8,128)S(1)} %get-tuple-element.65.refs_0_, s32[32,768]{1,0:T(8,128)S(1)} %get-tuple-element.66.refs_1_, s32[32,128]{1,0:T(8,128)S(1)} %get-tuple-element.67.refs_2_, s32[8,128]{1,0:T(8,128)S(1)} %get-tuple-element.68.refs_3_, bf16[768,640]{1,0:T(8,128)(2,1)S(1)} %copy-done.22, ...), custom_call_target="tpu_custom_call" | custom-call | flops 1610612736 | bytes 2097152 | tf_op jit(solution)/shard_map/pack/pallas_call | solution.py:118
  26.1 3.1 %constant_dynamic-slice_fusion.4 = (bf16[640,640]{1,0:T(8,128)(2,1)S(1)}, bf16[640,640]{1,0:T(8,128)(2,1)S(1)}, bf16[640,640]{1,0:T(8,128)(2,1)S(1)}, bf16[640,640]{1,0:T(8,128)(2,1)}) fusion(bf16[640,5120]{1,0:T(8,128)(2,1)} %param.15, s32[]{:T(128)S(6)} %select_n.27, s32[]{:T(128)S(6)} %select_n.26, s32[]{:T(128)S(6)} %select_n.25, s32[]{:T(128)S(6)} %select_n.24), kind=kLoop, calls=%fused_computation.6 | loop fusion | bytes 6553616 | tf_op jit(solution)/shard_map/dynamic_slice | solution.py:298
  29.2 1.3 collective-permute-start
  30.5 2.6 collective-permute-start.1
  33.1 1.1 collective-permute-start.2
  34.2 15.3 %collective-permute-done.refs_9_ = bf16[640,640]{1,0:T(8,128)(2,1)S(1)} collective-permute-done((bf16[640,640]{1,0:T(8,128)(2,1)S(1)}, bf16[640,640]{1,0:T(8,128)(2,1)S(1)}, u32[]{:S(2)}, u32[]{:S(2)}) %collective-permute-start) | collective-permute-done | bytes 819232 | tf_op jit(solution)/shard_map/ppermute | solution.py:300
  49.5 18.7 %collective-permute-done.1.refs_10_ = bf16[640,640]{1,0:T(8,128)(2,1)S(1)} collective-permute-done((bf16[640,640]{1,0:T(8,128)(2,1)S(1)}, bf16[640,640]{1,0:T(8,128)(2,1)S(1)}, u32[]{:S(2)}, u32[]{:S(2)}) %collective-permute-start.1) | collective-permute-done | bytes 819232 | tf_op jit(solution)/shard_map/ppermute | solution.py:300
  68.1 0.0 collective-permute-done.2.refs_11_
  68.2 26.0 %all-to-all-done.1.got_ref = bf16[32,128,384]{2,1,0:T(8,128)(2,1)} async-done(((bf16[32,128,384]{2,1,0:T(8,128)(2,1)}), bf16[32,128,384]{2,1,0:T(8,128)(2,1)}, u32[]{:S(2)}, u32[]{:S(2)}) %all-to-all-start.1) | async-done | bytes 3145760 | tf_op jit(solution)/shard_map/all_to_all | solution.py:353
  94.1 1.5 fusion
  96.4 8.9 %all-to-all-start.2 = ((bf16[32,128,256]{2,1,0:T(8,128)(2,1)}), bf16[32,128,256]{2,1,0:T(8,128)(2,1)}, u32[]{:S(2)}, u32[]{:S(2)}) async-start(bf16[32,128,256]{2,1,0:T(8,128)(2,1)} %pack.5), calls=%async_computation.2 | async-start | bytes 4194304 | tf_op jit(solution)/shard_map/all_to_all | solution.py:353
  105.3 3.8 %constant_dynamic-slice_fusion = (bf16[640,640]{1,0:T(8,128)(2,1)}, bf16[640,640]{1,0:T(8,128)(2,1)}, bf16[640,640]{1,0:T(8,128)(2,1)}, bf16[640,640]{1,0:T(8,128)(2,1)}) fusion(bf16[640,5120]{1,0:T(8,128)(2,1)} %param.15, s32[]{:T(128)S(6)} %select_n.31, s32[]{:T(128)S(6)} %select_n.30, s32[]{:T(128)S(6)} %select_n.29, s32[]{:T(128)S(6)} %select_n.28), kind=kLoop, calls=%fused_computation.2 | loop fusion | bytes 6553616 | tf_op jit(solution)/shard_map/dynamic_slice | solution.py:298
  109.2 1.1 collective-permute-start.3
  110.3 1.3 collective-permute-start.4
  111.6 2.9 %collective-permute-start.5 = (bf16[640,640]{1,0:T(8,128)(2,1)}, bf16[640,640]{1,0:T(8,128)(2,1)S(1)}, u32[]{:S(2)}, u32[]{:S(2)}) collective-permute-start(bf16[640,640]{1,0:T(8,128)(2,1)} %get-tuple-element.100), channel_id=1, source_target_pairs={{0,5},{1,4},{2,7},{3,6},{4,1},{5,0},{6,3},{7,2},{8,13},{9,12},{10,... | collective-permute-start | bytes 2457608 | tf_op jit(solution)/shard_map/ppermute | solution.py:300
  114.5 1.0 collective-permute-start.6
  115.5 20.2 %attend.2 = bf16[32,48,384]{2,1,0:T(8,128)(2,1)} custom-call(s32[1]{0:T(128)} %bitcast.2.over_ref, bf16[32,128,384]{2,1,0:T(8,128)(2,1)} %all-to-all-done.1.got_ref, bf16[32,128,640]{2,1,0:T(8,128)(2,1)S(1)} %copy-done), custom_call_target="tpu_custom_call" | custom-call | flops 9663676416 | bytes 3145728 | tf_op jit(solution)/shard_map/attend/pallas_call | solution.py:190
  135.7 0.0 collective-permute-done.3.refs_12_
  135.7 0.0 collective-permute-done.4.refs_13_
  135.7 15.1 %collective-permute-done.5.refs_14_ = bf16[640,640]{1,0:T(8,128)(2,1)S(1)} collective-permute-done((bf16[640,640]{1,0:T(8,128)(2,1)}, bf16[640,640]{1,0:T(8,128)(2,1)S(1)}, u32[]{:S(2)}, u32[]{:S(2)}) %collective-permute-start.5) | collective-permute-done | bytes 819232 | tf_op jit(solution)/shard_map/ppermute | solution.py:300
  150.8 0.0 collective-permute-done.6.refs_15_
  150.8 3.2 %all-to-all-done.2.got_ref = bf16[32,128,256]{2,1,0:T(8,128)(2,1)} async-done(((bf16[32,128,256]{2,1,0:T(8,128)(2,1)}), bf16[32,128,256]{2,1,0:T(8,128)(2,1)}, u32[]{:S(2)}, u32[]{:S(2)}) %all-to-all-start.2) | async-done | bytes 2097184 | tf_op jit(solution)/shard_map/all_to_all | solution.py:353
  154.0 7.2 %all-to-all-start.3 = ((bf16[32,48,384]{2,1,0:T(8,128)(2,1)}), bf16[32,48,384]{2,1,0:T(8,128)(2,1)}, u32[]{:S(2)}, u32[]{:S(2)}) async-start(bf16[32,48,384]{2,1,0:T(8,128)(2,1)} %attend.2), calls=%async_computation.3 | async-start | bytes 2359296 | tf_op jit(solution)/shard_map/all_to_all | solution.py:353
  161.2 14.6 %attend.3 = bf16[32,48,256]{2,1,0:T(8,128)(2,1)} custom-call(s32[1]{0:T(128)} %bitcast.2.over_ref, bf16[32,128,256]{2,1,0:T(8,128)(2,1)} %all-to-all-done.2.got_ref, bf16[32,128,640]{2,1,0:T(8,128)(2,1)} %get-tuple-element.107.extra_ref), custom_call_target="tpu_custom_call" | custom-call | flops 6442450944 | bytes 2097152 | tf_op jit(solution)/shard_map/attend/pallas_call | solution.py:190
  175.8 13.0 %all-to-all-done.3.got_ref = bf16[32,48,384]{2,1,0:T(8,128)(2,1)} async-done(((bf16[32,48,384]{2,1,0:T(8,128)(2,1)}), bf16[32,48,384]{2,1,0:T(8,128)(2,1)}, u32[]{:S(2)}, u32[]{:S(2)}) %all-to-all-start.3) | async-done | bytes 1179680 | tf_op jit(solution)/shard_map/all_to_all | solution.py:353
  188.8 8.4 %all-to-all-start.4 = ((bf16[32,48,256]{2,1,0:T(8,128)(2,1)}), bf16[32,48,256]{2,1,0:T(8,128)(2,1)S(1)}, u32[]{:S(2)}, u32[]{:S(2)}) async-start(bf16[32,48,256]{2,1,0:T(8,128)(2,1)} %attend.3), calls=%async_computation.4 | async-start | bytes 1572864 | tf_op jit(solution)/shard_map/all_to_all | solution.py:353
  197.3 3.6 %unpack.3.refs_0_ = bf16[768,384]{1,0:T(8,128)(2,1)} custom-call(s32[768,128]{1,0:T(8,128)} %get-tuple-element.64.code_ref, bf16[32,48,384]{2,1,0:T(8,128)(2,1)} %all-to-all-done.3.got_ref), custom_call_target="tpu_custom_call" | custom-call | flops 905969664 | bytes 1179648 | tf_op jit(solution)/shard_map/unpack/pallas_call | solution.py:225
  200.9 3.0 %collective-permute-start.10 = (bf16[768,384]{1,0:T(8,128)(2,1)}, bf16[768,384]{1,0:T(8,128)(2,1)S(1)}, u32[]{:S(2)}, u32[]{:S(2)}) collective-permute-start(bf16[768,384]{1,0:T(8,128)(2,1)} %unpack.3.refs_0_), channel_id=1, source_target_pairs={{0,4},{1,5},{2,6},{3,7},{4,0},{5,1},{6,2},{7,3},{8,12},{9,13},{10,... | collective-permute-start | bytes 1769480 | tf_op jit(solution)/shard_map/ppermute | solution.py:311
  203.9 0.4 collective-permute-start.11
  204.3 2.3 collective-permute-start.12
  206.6 2.3 collective-permute-start.13
  208.9 8.2 %all-to-all-done.4.got_ref = bf16[32,48,256]{2,1,0:T(8,128)(2,1)S(1)} async-done(((bf16[32,48,256]{2,1,0:T(8,128)(2,1)}), bf16[32,48,256]{2,1,0:T(8,128)(2,1)S(1)}, u32[]{:S(2)}, u32[]{:S(2)}) %all-to-all-start.4) | async-done | bytes 786464 | tf_op jit(solution)/shard_map/all_to_all | solution.py:353
  217.0 0.9 copy-done.7
  217.9 2.8 %unpack.2.refs_0_ = bf16[768,256]{1,0:T(8,128)(2,1)} custom-call(s32[768,128]{1,0:T(8,128)} %get-tuple-element.64.code_ref, bf16[32,48,256]{2,1,0:T(8,128)(2,1)} %copy-done.7), custom_call_target="tpu_custom_call" | custom-call | flops 603979776 | bytes 786432 | tf_op jit(solution)/shard_map/unpack/pallas_call | solution.py:225
  220.7 0.0 collective-permute-done.10.refs_2_
  220.7 9.8 %collective-permute-done.11.refs_1_ = bf16[768,384]{1,0:T(8,128)(2,1)S(1)} collective-permute-done((bf16[768,384]{1,0:T(8,128)(2,1)}, bf16[768,384]{1,0:T(8,128)(2,1)S(1)}, u32[]{:S(2)}, u32[]{:S(2)}) %collective-permute-start.11) | collective-permute-done | bytes 589856 | tf_op jit(solution)/shard_map/ppermute | solution.py:311
  230.5 0.0 collective-permute-done.12.refs_3_
  230.5 0.9 collective-permute-start.14
  231.5 0.0 collective-permute-start.15
  231.5 0.5 collective-permute-start.16
  232.0 1.9 collective-permute-start.7
  233.9 0.0 collective-permute-done.13.refs_4_
  233.9 1.0 collective-permute-start.8
  234.9 0.0 collective-permute-done.14.refs_5_
  234.9 1.6 collective-permute-start.9
  236.5 0.0 collective-permute-done.15.refs_6_
  236.6 0.9 collective-permute-start.17
  237.5 0.0 collective-permute-done.16.refs_7_
  237.5 0.8 copy-done.14
  238.3 9.0 %project.2.refs_16_ = f32[768,640]{1,0:T(8,128)} custom-call(bf16[768,384]{1,0:T(8,128)(2,1)} %unpack.3.refs_0_, bf16[768,384]{1,0:T(8,128)(2,1)} %copy-done.9, bf16[768,384]{1,0:T(8,128)(2,1)} %copy-done.8, bf16[768,384]{1,0:T(8,128)(2,1)} %copy-done.10, bf16[768,384]{1,0:T(8,128)(2,1)} %copy-done.11, bf16[768,384]{1,0:T(8,128)(2,1)} %copy-done.12, ...), custom_call_target="tpu_custom_call" | custom-call | flops 3019898880 | bytes 8650752 | tf_op jit(solution)/shard_map/project/pallas_call | solution.py:276
  247.4 5.8 %collective-permute-done.8.refs_1_ = bf16[768,256]{1,0:T(8,128)(2,1)S(1)} collective-permute-done((bf16[768,256]{1,0:T(8,128)(2,1)}, bf16[768,256]{1,0:T(8,128)(2,1)S(1)}, u32[]{:S(2)}, u32[]{:S(2)}) %collective-permute-start.8) | collective-permute-done | bytes 393248 | tf_op jit(solution)/shard_map/ppermute | solution.py:311
  253.2 0.6 collective-permute-start.18
  253.7 0.1 collective-permute-start.19
  253.8 0.4 collective-permute-start.20
  254.2 0.8 collective-permute-done.18.refs_5_
  255.1 0.6 collective-permute-done.19.refs_6_
  255.6 0.6 collective-permute-done.20.refs_7_
  256.2 0.2 copy-done.20
  256.4 0.7 copy-done.21
  257.1 7.7 %project.3 = bf16[768,640]{1,0:T(8,128)(2,1)} custom-call(bf16[768,256]{1,0:T(8,128)(2,1)} %unpack.2.refs_0_, bf16[768,256]{1,0:T(8,128)(2,1)} %copy-done.16, bf16[768,256]{1,0:T(8,128)(2,1)} %copy-done.15, bf16[768,256]{1,0:T(8,128)(2,1)} %copy-done.17, bf16[768,256]{1,0:T(8,128)(2,1)} %copy-done.18, bf16[768,256]{1,0:T(8,128)(2,1)} %copy-done.19, ...), custom_call_target="tpu_custom_call" | custom-call | flops 2013265920 | bytes 5767168 | tf_op jit(solution)/shard_map/project/pallas_call | solution.py:276
  (51 shorter events, 0.1 us)
Async XLA Ops:
  10.4 12.3 %copy-start.22 = (bf16[768,640]{1,0:T(8,128)(2,1)S(1)}, bf16[768,640]{1,0:T(8,128)(2,1)}, u32[]{:S(2)}) copy-start(bf16[768,640]{1,0:T(8,128)(2,1)} %refs_4_.3) | copy-start | bytes 2949124
  10.4 12.3 %copy-start.23 = (bf16[768,640]{1,0:T(8,128)(2,1)S(1)}, bf16[768,640]{1,0:T(8,128)(2,1)}, u32[]{:S(2)}) copy-start(bf16[768,640]{1,0:T(8,128)(2,1)} %refs_5_.3) | copy-start | bytes 2949124
  10.4 12.3 %copy-start.24 = (bf16[768,640]{1,0:T(8,128)(2,1)S(1)}, bf16[768,640]{1,0:T(8,128)(2,1)}, u32[]{:S(2)}) copy-start(bf16[768,640]{1,0:T(8,128)(2,1)} %refs_6_.3) | copy-start | bytes 2949124
  10.4 83.8 %all-to-all-start.1 = ((bf16[32,128,384]{2,1,0:T(8,128)(2,1)}), bf16[32,128,384]{2,1,0:T(8,128)(2,1)}, u32[]{:S(2)}, u32[]{:S(2)}) async-start(bf16[32,128,384]{2,1,0:T(8,128)(2,1)} %pack.4), calls=%async_computation.1 | async-start | bytes 6291456 | tf_op jit(solution)/shard_map/all_to_all | solution.py:353
  29.2 20.3 %collective-permute-start = (bf16[640,640]{1,0:T(8,128)(2,1)S(1)}, bf16[640,640]{1,0:T(8,128)(2,1)S(1)}, u32[]{:S(2)}, u32[]{:S(2)}) collective-permute-start(bf16[640,640]{1,0:T(8,128)(2,1)S(1)} %get-tuple-element.105), channel_id=1, source_target_pairs={{0,2},{1,3},{2,4},{3,5},{4,6},{5,7},{6,0},{7,1},{8,10},{9,11},{10,... | collective-permute-start | bytes 2457608 | tf_op jit(solution)/shard_map/ppermute | solution.py:300
  30.5 37.6 %collective-permute-start.1 = (bf16[640,640]{1,0:T(8,128)(2,1)S(1)}, bf16[640,640]{1,0:T(8,128)(2,1)S(1)}, u32[]{:S(2)}, u32[]{:S(2)}) collective-permute-start(bf16[640,640]{1,0:T(8,128)(2,1)S(1)} %get-tuple-element.104), channel_id=1, source_target_pairs={{0,4},{1,5},{2,6},{3,7},{4,0},{5,1},{6,2},{7,3},{8,12},{9,13},{10,... | collective-permute-start | bytes 2457608 | tf_op jit(solution)/shard_map/ppermute | solution.py:300
  33.1 35.0 %collective-permute-start.2 = (bf16[640,640]{1,0:T(8,128)(2,1)S(1)}, bf16[640,640]{1,0:T(8,128)(2,1)S(1)}, u32[]{:S(2)}, u32[]{:S(2)}) collective-permute-start(bf16[640,640]{1,0:T(8,128)(2,1)S(1)} %get-tuple-element.103), channel_id=1, source_target_pairs={{0,6},{1,7},{2,0},{3,1},{4,2},{5,3},{6,4},{7,5},{8,14},{9,15},{10,... | collective-permute-start | bytes 2457608 | tf_op jit(solution)/shard_map/ppermute | solution.py:300
  49.5 46.8 %copy-start.1 = (bf16[640,640]{1,0:T(8,128)(2,1)}, bf16[640,640]{1,0:T(8,128)(2,1)S(1)}, u32[]{:S(2)}) copy-start(bf16[640,640]{1,0:T(8,128)(2,1)S(1)} %collective-permute-done.refs_9_) | copy-start | bytes 2457604
  68.1 28.2 %copy-start.2 = (bf16[640,640]{1,0:T(8,128)(2,1)}, bf16[640,640]{1,0:T(8,128)(2,1)S(1)}, u32[]{:S(2)}) copy-start(bf16[640,640]{1,0:T(8,128)(2,1)S(1)} %collective-permute-done.1.refs_10_) | copy-start | bytes 2457604
  68.2 28.2 %copy-start.3 = (bf16[640,640]{1,0:T(8,128)(2,1)}, bf16[640,640]{1,0:T(8,128)(2,1)S(1)}, u32[]{:S(2)}) copy-start(bf16[640,640]{1,0:T(8,128)(2,1)S(1)} %collective-permute-done.2.refs_11_) | copy-start | bytes 2457604
  96.4 57.7 %all-to-all-start.2 = ((bf16[32,128,256]{2,1,0:T(8,128)(2,1)}), bf16[32,128,256]{2,1,0:T(8,128)(2,1)}, u32[]{:S(2)}, u32[]{:S(2)}) async-start(bf16[32,128,256]{2,1,0:T(8,128)(2,1)} %pack.5), calls=%async_computation.2 | async-start | bytes 4194304 | tf_op jit(solution)/shard_map/all_to_all | solution.py:353
  105.3 10.2 %copy-start = (bf16[32,128,640]{2,1,0:T(8,128)(2,1)S(1)}, bf16[32,128,640]{2,1,0:T(8,128)(2,1)}, u32[]{:S(2)}) copy-start(bf16[32,128,640]{2,1,0:T(8,128)(2,1)} %get-tuple-element.107.extra_ref) | copy-start | bytes 15728644
  109.2 26.5 %collective-permute-start.3 = (bf16[640,640]{1,0:T(8,128)(2,1)}, bf16[640,640]{1,0:T(8,128)(2,1)S(1)}, u32[]{:S(2)}, u32[]{:S(2)}) collective-permute-start(bf16[640,640]{1,0:T(8,128)(2,1)} %get-tuple-element.102), channel_id=1, source_target_pairs={{0,1},{1,0},{2,3},{3,2},{4,5},{5,4},{6,7},{7,6},{8,9},{9,8},{10,11... | collective-permute-start | bytes 2457608 | tf_op jit(solution)/shard_map/ppermute | solution.py:300
  110.3 25.4 %collective-permute-start.4 = (bf16[640,640]{1,0:T(8,128)(2,1)}, bf16[640,640]{1,0:T(8,128)(2,1)S(1)}, u32[]{:S(2)}, u32[]{:S(2)}) collective-permute-start(bf16[640,640]{1,0:T(8,128)(2,1)} %get-tuple-element.101), channel_id=1, source_target_pairs={{0,3},{1,2},{2,5},{3,4},{4,7},{5,6},{6,1},{7,0},{8,11},{9,10},{10,... | collective-permute-start | bytes 2457608 | tf_op jit(solution)/shard_map/ppermute | solution.py:300
  111.6 39.2 %collective-permute-start.5 = (bf16[640,640]{1,0:T(8,128)(2,1)}, bf16[640,640]{1,0:T(8,128)(2,1)S(1)}, u32[]{:S(2)}, u32[]{:S(2)}) collective-permute-start(bf16[640,640]{1,0:T(8,128)(2,1)} %get-tuple-element.100), channel_id=1, source_target_pairs={{0,5},{1,4},{2,7},{3,6},{4,1},{5,0},{6,3},{7,2},{8,13},{9,12},{10,... | collective-permute-start | bytes 2457608 | tf_op jit(solution)/shard_map/ppermute | solution.py:300
  114.5 36.3 %collective-permute-start.6 = (bf16[640,640]{1,0:T(8,128)(2,1)}, bf16[640,640]{1,0:T(8,128)(2,1)}, u32[]{:S(2)}, u32[]{:S(2)}) collective-permute-start(bf16[640,640]{1,0:T(8,128)(2,1)} %get-tuple-element.99), channel_id=1, source_target_pairs={{0,7},{1,6},{2,1},{3,0},{4,3},{5,2},{6,5},{7,4},{8,15},{9,14},{10,... | collective-permute-start | bytes 2457608 | tf_op jit(solution)/shard_map/ppermute | solution.py:300
  135.7 40.1 %copy-start.4 = (bf16[640,640]{1,0:T(8,128)(2,1)}, bf16[640,640]{1,0:T(8,128)(2,1)S(1)}, u32[]{:S(2)}) copy-start(bf16[640,640]{1,0:T(8,128)(2,1)S(1)} %collective-permute-done.3.refs_12_) | copy-start | bytes 2457604
  135.7 40.1 %copy-start.5 = (bf16[640,640]{1,0:T(8,128)(2,1)}, bf16[640,640]{1,0:T(8,128)(2,1)S(1)}, u32[]{:S(2)}) copy-start(bf16[640,640]{1,0:T(8,128)(2,1)S(1)} %collective-permute-done.4.refs_13_) | copy-start | bytes 2457604
  150.8 25.0 %copy-start.6 = (bf16[640,640]{1,0:T(8,128)(2,1)}, bf16[640,640]{1,0:T(8,128)(2,1)S(1)}, u32[]{:S(2)}) copy-start(bf16[640,640]{1,0:T(8,128)(2,1)S(1)} %collective-permute-done.5.refs_14_) | copy-start | bytes 2457604
  154.0 34.8 %all-to-all-start.3 = ((bf16[32,48,384]{2,1,0:T(8,128)(2,1)}), bf16[32,48,384]{2,1,0:T(8,128)(2,1)}, u32[]{:S(2)}, u32[]{:S(2)}) async-start(bf16[32,48,384]{2,1,0:T(8,128)(2,1)} %attend.2), calls=%async_computation.3 | async-start | bytes 2359296 | tf_op jit(solution)/shard_map/all_to_all | solution.py:353
  188.8 28.2 %all-to-all-start.4 = ((bf16[32,48,256]{2,1,0:T(8,128)(2,1)}), bf16[32,48,256]{2,1,0:T(8,128)(2,1)S(1)}, u32[]{:S(2)}, u32[]{:S(2)}) async-start(bf16[32,48,256]{2,1,0:T(8,128)(2,1)} %attend.3), calls=%async_computation.4 | async-start | bytes 1572864 | tf_op jit(solution)/shard_map/all_to_all | solution.py:353
  200.9 19.8 %collective-permute-start.10 = (bf16[768,384]{1,0:T(8,128)(2,1)}, bf16[768,384]{1,0:T(8,128)(2,1)S(1)}, u32[]{:S(2)}, u32[]{:S(2)}) collective-permute-start(bf16[768,384]{1,0:T(8,128)(2,1)} %unpack.3.refs_0_), channel_id=1, source_target_pairs={{0,4},{1,5},{2,6},{3,7},{4,0},{5,1},{6,2},{7,3},{8,12},{9,13},{10,... | collective-permute-start | bytes 1769480 | tf_op jit(solution)/shard_map/ppermute | solution.py:311
  203.9 26.6 %collective-permute-start.11 = (bf16[768,384]{1,0:T(8,128)(2,1)}, bf16[768,384]{1,0:T(8,128)(2,1)S(1)}, u32[]{:S(2)}, u32[]{:S(2)}) collective-permute-start(bf16[768,384]{1,0:T(8,128)(2,1)} %unpack.3.refs_0_), channel_id=1, source_target_pairs={{0,2},{1,3},{2,4},{3,5},{4,6},{5,7},{6,0},{7,1},{8,10},{9,11},{10,... | collective-permute-start | bytes 1769480 | tf_op jit(solution)/shard_map/ppermute | solution.py:311
  204.3 26.2 %collective-permute-start.12 = (bf16[768,384]{1,0:T(8,128)(2,1)}, bf16[768,384]{1,0:T(8,128)(2,1)S(1)}, u32[]{:S(2)}, u32[]{:S(2)}) collective-permute-start(bf16[768,384]{1,0:T(8,128)(2,1)} %unpack.3.refs_0_), channel_id=1, source_target_pairs={{0,6},{1,7},{2,0},{3,1},{4,2},{5,3},{6,4},{7,5},{8,14},{9,15},{10,... | collective-permute-start | bytes 1769480 | tf_op jit(solution)/shard_map/ppermute | solution.py:311
  206.6 27.3 %collective-permute-start.13 = (bf16[768,384]{1,0:T(8,128)(2,1)}, bf16[768,384]{1,0:T(8,128)(2,1)S(1)}, u32[]{:S(2)}, u32[]{:S(2)}) collective-permute-start(bf16[768,384]{1,0:T(8,128)(2,1)} %unpack.3.refs_0_), channel_id=1, source_target_pairs={{0,1},{1,0},{2,3},{3,2},{4,5},{5,4},{6,7},{7,6},{8,9},{9,8},{10,11... | collective-permute-start | bytes 1769480 | tf_op jit(solution)/shard_map/ppermute | solution.py:316
  217.0 0.9 copy-start.7
  220.7 16.8 %copy-start.8 = (bf16[768,384]{1,0:T(8,128)(2,1)}, bf16[768,384]{1,0:T(8,128)(2,1)S(1)}, u32[]{:S(2)}) copy-start(bf16[768,384]{1,0:T(8,128)(2,1)S(1)} %collective-permute-done.10.refs_2_) | copy-start | bytes 1769476
  230.5 7.0 %copy-start.9 = (bf16[768,384]{1,0:T(8,128)(2,1)}, bf16[768,384]{1,0:T(8,128)(2,1)S(1)}, u32[]{:S(2)}) copy-start(bf16[768,384]{1,0:T(8,128)(2,1)S(1)} %collective-permute-done.11.refs_1_) | copy-start | bytes 1769476
  230.5 7.0 %copy-start.10 = (bf16[768,384]{1,0:T(8,128)(2,1)}, bf16[768,384]{1,0:T(8,128)(2,1)S(1)}, u32[]{:S(2)}) copy-start(bf16[768,384]{1,0:T(8,128)(2,1)S(1)} %collective-permute-done.12.refs_3_) | copy-start | bytes 1769476
  230.5 4.4 %collective-permute-start.14 = (bf16[768,384]{1,0:T(8,128)(2,1)S(1)}, bf16[768,384]{1,0:T(8,128)(2,1)S(1)}, u32[]{:S(2)}, u32[]{:S(2)}) collective-permute-start(bf16[768,384]{1,0:T(8,128)(2,1)S(1)} %collective-permute-done.11.refs_1_), channel_id=1, source_target_pairs={{0,1},{1,0},{2,3},{3,2},{4,5},{5,4},{6,7},{7,6},{8,9},{9,8},{10,11... | collective-permute-start | bytes 1769480 | tf_op jit(solution)/shard_map/ppermute | solution.py:316
  231.5 5.1 %collective-permute-start.15 = (bf16[768,384]{1,0:T(8,128)(2,1)S(1)}, bf16[768,384]{1,0:T(8,128)(2,1)S(1)}, u32[]{:S(2)}, u32[]{:S(2)}) collective-permute-start(bf16[768,384]{1,0:T(8,128)(2,1)S(1)} %collective-permute-done.10.refs_2_), channel_id=1, source_target_pairs={{0,1},{1,0},{2,3},{3,2},{4,5},{5,4},{6,7},{7,6},{8,9},{9,8},{10,11... | collective-permute-start | bytes 1769480 | tf_op jit(solution)/shard_map/ppermute | solution.py:316
  231.5 6.0 %collective-permute-start.16 = (bf16[768,384]{1,0:T(8,128)(2,1)S(1)}, bf16[768,384]{1,0:T(8,128)(2,1)S(1)}, u32[]{:S(2)}, u32[]{:S(2)}) collective-permute-start(bf16[768,384]{1,0:T(8,128)(2,1)S(1)} %collective-permute-done.12.refs_3_), channel_id=1, source_target_pairs={{0,1},{1,0},{2,3},{3,2},{4,5},{5,4},{6,7},{7,6},{8,9},{9,8},{10,11... | collective-permute-start | bytes 1769480 | tf_op jit(solution)/shard_map/ppermute | solution.py:316
  232.0 15.4 %collective-permute-start.7 = (bf16[768,256]{1,0:T(8,128)(2,1)}, bf16[768,256]{1,0:T(8,128)(2,1)S(1)}, u32[]{:S(2)}, u32[]{:S(2)}) collective-permute-start(bf16[768,256]{1,0:T(8,128)(2,1)} %unpack.2.refs_0_), channel_id=1, source_target_pairs={{0,4},{1,5},{2,6},{3,7},{4,0},{5,1},{6,2},{7,3},{8,12},{9,13},{10,... | collective-permute-start | bytes 1179656 | tf_op jit(solution)/shard_map/ppermute | solution.py:311
  233.9 3.6 %copy-start.11 = (bf16[768,384]{1,0:T(8,128)(2,1)}, bf16[768,384]{1,0:T(8,128)(2,1)S(1)}, u32[]{:S(2)}) copy-start(bf16[768,384]{1,0:T(8,128)(2,1)S(1)} %collective-permute-done.13.refs_4_) | copy-start | bytes 1769476
  233.9 19.3 %collective-permute-start.8 = (bf16[768,256]{1,0:T(8,128)(2,1)}, bf16[768,256]{1,0:T(8,128)(2,1)S(1)}, u32[]{:S(2)}, u32[]{:S(2)}) collective-permute-start(bf16[768,256]{1,0:T(8,128)(2,1)} %unpack.2.refs_0_), channel_id=1, source_target_pairs={{0,2},{1,3},{2,4},{3,5},{4,6},{5,7},{6,0},{7,1},{8,10},{9,11},{10,... | collective-permute-start | bytes 1179656 | tf_op jit(solution)/shard_map/ppermute | solution.py:311
  234.9 2.6 copy-start.12
  234.9 18.3 %collective-permute-start.9 = (bf16[768,256]{1,0:T(8,128)(2,1)}, bf16[768,256]{1,0:T(8,128)(2,1)S(1)}, u32[]{:S(2)}, u32[]{:S(2)}) collective-permute-start(bf16[768,256]{1,0:T(8,128)(2,1)} %unpack.2.refs_0_), channel_id=1, source_target_pairs={{0,6},{1,7},{2,0},{3,1},{4,2},{5,3},{6,4},{7,5},{8,14},{9,15},{10,... | collective-permute-start | bytes 1179656 | tf_op jit(solution)/shard_map/ppermute | solution.py:311
  236.5 1.0 copy-start.13
  236.6 17.7 %collective-permute-start.17 = (bf16[768,256]{1,0:T(8,128)(2,1)}, bf16[768,256]{1,0:T(8,128)(2,1)S(1)}, u32[]{:S(2)}, u32[]{:S(2)}) collective-permute-start(bf16[768,256]{1,0:T(8,128)(2,1)} %unpack.2.refs_0_), channel_id=1, source_target_pairs={{0,1},{1,0},{2,3},{3,2},{4,5},{5,4},{6,7},{7,6},{8,9},{9,8},{10,11... | collective-permute-start | bytes 1179656 | tf_op jit(solution)/shard_map/ppermute | solution.py:316
  237.5 0.8 copy-start.14
  247.4 8.8 %copy-start.15 = (bf16[768,256]{1,0:T(8,128)(2,1)}, bf16[768,256]{1,0:T(8,128)(2,1)S(1)}, u32[]{:S(2)}) copy-start(bf16[768,256]{1,0:T(8,128)(2,1)S(1)} %collective-permute-done.7.refs_2_) | copy-start | bytes 1179652
  253.2 3.0 %copy-start.16 = (bf16[768,256]{1,0:T(8,128)(2,1)}, bf16[768,256]{1,0:T(8,128)(2,1)S(1)}, u32[]{:S(2)}) copy-start(bf16[768,256]{1,0:T(8,128)(2,1)S(1)} %collective-permute-done.8.refs_1_) | copy-start | bytes 1179652
  253.2 3.0 %copy-start.17 = (bf16[768,256]{1,0:T(8,128)(2,1)}, bf16[768,256]{1,0:T(8,128)(2,1)S(1)}, u32[]{:S(2)}) copy-start(bf16[768,256]{1,0:T(8,128)(2,1)S(1)} %collective-permute-done.9.refs_3_) | copy-start | bytes 1179652
  253.2 1.9 collective-permute-start.18
  253.7 1.9 collective-permute-start.19
  253.8 2.4 collective-permute-start.20
  254.2 2.0 copy-start.18
  255.1 1.1 copy-start.19
  255.6 0.8 copy-start.20
  256.4 0.7 copy-start.21

commit v3 on v2

--- a/solution.py
+++ b/solution.py
@@ -231,23 +231,23 @@
     )(code, got)
 
 
-def project_kernel(rows_used, counts, *refs):
-    groups, pieces = counts
-    part_refs, weight_refs = refs[:pieces], refs[pieces : pieces + groups]
+def project_kernel(spans, *refs):
+    count = len(spans)
+    part_refs, weight_refs = refs[:count], refs[count : 2 * count]
     out_ref, lined_ref, arrived = refs[-3:]
-    first, end = rows_used
-    depth = end - first
 
     @pl.when(pl.program_id(0) == 0)
     def _():
-        copies = [
-            pltpu.make_async_copy(
-                weight_refs[k].at[first:end, :],
-                lined_ref.at[k * depth : (k + 1) * depth, :],
-                arrived.at[k],
+        copies, at = [], 0
+        for k, (first, end) in enumerate(spans):
+            copies.append(
+                pltpu.make_async_copy(
+                    weight_refs[k].at[first:end, :],
+                    lined_ref.at[at : at + end - first, :],
+                    arrived.at[k],
+                )
             )
-            for k in range(groups)
-        ]
+            at += end - first
         for copy in copies:
             copy.start()
         for copy in copies:
@@ -255,31 +255,30 @@
 
     lined = jnp.concatenate([part_ref[...] for part_ref in part_refs], axis=1)
     product = jnp.dot(lined, lined_ref[...], preferred_element_type=F32)
-    if len(refs) == pieces + groups + 4:
-        product += refs[pieces + groups][...]
+    if len(refs) == 2 * count + 4:
+        product += refs[2 * count][...]
     out_ref[...] = product.astype(out_ref.dtype)
 
 
-def project(parts, weights, chunk, before, kind):
-    rows = parts[0].shape[0]
-    groups, columns = len(weights), weights[0].shape[1]
-    rows_used = (chunk[0] * HDIM, chunk[1] * HDIM)
-    depth = groups * (rows_used[1] - rows_used[0])
-    step = rows // 3
+def project(items, before, kind):
+    rows, columns = items[0][0].shape[0], items[0][1].shape[1]
+    spans = tuple((first * HDIM, end * HDIM) for _, _, (first, end) in items)
+    depth = sum(end - first for first, end in spans)
+    step = rows // 2
     block = pl.BlockSpec((step, columns), lambda i: (i, 0))
-    in_specs = [pl.BlockSpec((step, part.shape[1]), lambda i: (i, 0)) for part in parts]
-    in_specs += [pl.BlockSpec(memory_space=pl.ANY)] * groups
-    operands = [*parts, *weights]
+    in_specs = [pl.BlockSpec((step, part.shape[1]), lambda i: (i, 0)) for part, _, _ in items]
+    in_specs += [pl.BlockSpec(memory_space=pl.ANY)] * len(items)
+    operands = [part for part, _, _ in items] + [weight for _, weight, _ in items]
     if before is not None:
         in_specs.append(block)
         operands.append(before)
     return pl.pallas_call(
-        functools.partial(project_kernel, rows_used, (groups, len(parts))),
+        functools.partial(project_kernel, spans),
         grid=(rows // step,),
         in_specs=in_specs,
         out_specs=block,
         out_shape=jax.ShapeDtypeStruct((rows, columns), kind),
-        scratch_shapes=[pltpu.VMEM((depth, columns), BF16), pltpu.SemaphoreType.DMA((groups,))],
+        scratch_shapes=[pltpu.VMEM((depth, columns), BF16), pltpu.SemaphoreType.DMA((len(items),))],
         compiler_params=params("arbitrary"),
         cost_estimate=cost(2 * rows * depth * columns, 2 * depth * (rows + columns)),
         name="project",
@@ -304,20 +303,17 @@
     return parts
 
 
-def head_gather(rows, groups, meanwhile=None):
+def along_y(rows, groups):
     steps = sorted(range(2, groups, 2), key=lambda along: -min(along, groups - along))
-    along_y = {0: rows}
-    for along in steps:
-        along_y[along] = lax.ppermute(rows, "head", [(g, (g + along) % groups) for g in range(groups)])
-    if meanwhile is not None:
-        *held, meanwhile = lax.optimization_barrier((*[along_y[along] for along in steps], meanwhile))
-        along_y.update(zip(steps, held))
-    swapped = {
-        along: lax.ppermute(part, "head", [(g, g ^ 1) for g in range(groups)])
-        for along, part in along_y.items()
+    moved = {
+        along: lax.ppermute(rows, "head", [(g, (g + along) % groups) for g in range(groups)])
+        for along in steps
     }
-    parts = [swapped[along] if core else along_y[along] for along, core in shifts(groups)]
-    return parts, meanwhile
+    return [moved[along] for along in sorted(moved)]
+
+
+def swapped(rows, groups):
+    return lax.ppermute(rows, "head", [(g, g ^ 1) for g in range(groups)])
 
 
 def unwritten_kernel(out_ref):
@@ -381,10 +377,25 @@
     answer1, back0 = after((attended(BACK[1]), back0))
     back1 = exchange(answer1)
     mine1 = unpack(code, back1)
-    parts0, _ = head_gather(unpack(code, back0), groups, mine1)
-    total = project(parts0, weights, BACK[0][1:], None, F32)
-    parts1, total = head_gather(mine1, groups, total)
-    return project(parts1, weights, BACK[1][1:], total, BF16)
+    mine0 = unpack(code, back0)
+    own_w, y_w, other_w, far_w = weights[0], weights[1:4], weights[4], weights[5:]
+    chunk0, chunk1 = BACK[0][1:], BACK[1][1:]
+
+    def items(parts, weights, chunk):
+        return [(part, weight, chunk) for part, weight in zip(parts, weights)]
+
+    y0 = along_y(mine0, groups)
+    *y0, _ = after((*y0, mine1))
+    parts0 = [mine0, *y0, swapped(mine0, groups), *[swapped(part, groups) for part in y0]]
+    y1 = along_y(mine1, groups)
+    near1 = [mine1, swapped(mine1, groups)]
+    total = project(
+        items(parts0, weights, chunk0) + items(near1, [own_w, other_w], chunk1), None, F32
+    )
+    *y1, total = after((*y1, total))
+    far1 = [swapped(part, groups) for part in y1]
+    total = project(items(y1, y_w, chunk1), total, F32)
+    return project(items(far1, far_w, chunk1), total, BF16)
 
 
 def solution(mesh):

time: 266 us -> 269 us (1.011)
  Pallas kernels: 70.4 us -> 75.3 us
    pallas_call x2 -> x3, Pallas kernels: 16.7 us -> 19.8 us  [project(): pl.pallas_call(functools.partial(project_kernel, spans), grid=(rows // st...]
    unnamed x51 -> x41, local copies, waits for them, and re-layouts: 4.05 us -> 5.72 us
  transfers between devices with their start and end apart: 25 -> 25, of which waited for: 12 -> 12; matrix products, arithmetic and copies ran while one was open for 3% -> 3% of each run, Pallas kernels for 20% -> 23%
where the time goes in v3:
time: 269 us; the launch traced here: 268 us
  waiting for transfers between devices  115 us (43%)
  Pallas kernels  75.3 us (28%)
  starting transfers between devices  63 us (23%)
  local copies, waits for them, and re-layouts  12.6 us (5%)
    all_to_all x4, waiting for transfers between devices, exchange(): return lax.all_to_all(block, 'ctx', split_axis=0, concat_axis=0, tiled=True)  49.4 us
    ppermute x7, waiting for transfers between devices, own_columns(): lax.ppermute(block, 'head', [(g, ((g ^ core) + along) % groups) for g in...  49.1 us
    all_to_all x4, starting transfers between devices, exchange(): return lax.all_to_all(block, 'ctx', split_axis=0, concat_axis=0, tiled=True)  36.4 us
    pallas_call x2, Pallas kernels, attend(): pl.pallas_call(functools.partial(attend_kernel, qslots, kslots, sources),...  34.7 us
    pallas_call x3, Pallas kernels, project(): pl.pallas_call(functools.partial(project_kernel, spans), grid=(rows // st...  19.8 us
    ppermute x6, waiting for transfers between devices, along_y(): lax.ppermute(rows, 'head', [(g, (g + along) % groups) for g in range(grou...  14.6 us
    pallas_call x2, Pallas kernels, pack(): pl.pallas_call(functools.partial(pack_kernel, columns, qslots, kslots), g...  12 us
    ppermute x7, starting transfers between devices, own_columns(): lax.ppermute(block, 'head', [(g, ((g ^ core) + along) % groups) for g in...  11.2 us
  transfers between devices with their start and end apart: 25, of which 12 were waited for; matrix products, arithmetic and copies ran while one was open for 3% of the time, Pallas kernels for 23%

profile of v3, /device:TPU:1, one launch (start us, length us, event | category | flops | bytes accessed | tf_op | source)
XLA Modules:
  0.0 268.3 jit_solution(8553302709771462988)
XLA Ops:
  0.0 1.4 copy.8.pattern_ref
  1.4 2.3 plan.1
  3.6 6.7 %pack.4 = bf16[32,128,384]{2,1,0:T(8,128)(2,1)} custom-call(s32[32,768]{1,0:T(8,128)S(1)} %get-tuple-element.65.refs_0_, s32[32,768]{1,0:T(8,128)S(1)} %get-tuple-element.66.refs_1_, s32[32,128]{1,0:T(8,128)S(1)} %get-tuple-element.67.refs_2_, s32[8,128]{1,0:T(8,128)S(1)} %get-tuple-element.68.refs_3_, bf16[768,640]{1,0:T(8,128)(2,1)} %refs_4_.3, ...), custom_call_target="tpu_custom_call" | custom-call | flops 2415919104 | bytes 3145728 | tf_op jit(solution)/shard_map/pack/pallas_call | solution.py:118
  10.4 11.9 %all-to-all-start.1 = ((bf16[32,128,384]{2,1,0:T(8,128)(2,1)}), bf16[32,128,384]{2,1,0:T(8,128)(2,1)S(1)}, u32[]{:S(2)}, u32[]{:S(2)}) async-start(bf16[32,128,384]{2,1,0:T(8,128)(2,1)} %pack.4), calls=%async_computation.1 | async-start | bytes 6291456 | tf_op jit(solution)/shard_map/all_to_all | solution.py:349
  22.3 5.2 %pack.5 = bf16[32,128,256]{2,1,0:T(8,128)(2,1)} custom-call(s32[32,768]{1,0:T(8,128)S(1)} %get-tuple-element.65.refs_0_, s32[32,768]{1,0:T(8,128)S(1)} %get-tuple-element.66.refs_1_, s32[32,128]{1,0:T(8,128)S(1)} %get-tuple-element.67.refs_2_, s32[8,128]{1,0:T(8,128)S(1)} %get-tuple-element.68.refs_3_, bf16[768,640]{1,0:T(8,128)(2,1)} %refs_4_.3, ...), custom_call_target="tpu_custom_call" | custom-call | flops 1610612736 | bytes 2097152 | tf_op jit(solution)/shard_map/pack/pallas_call | solution.py:118
  27.5 3.1 %constant_dynamic-slice_fusion.4 = (bf16[640,640]{1,0:T(8,128)(2,1)S(1)}, bf16[640,640]{1,0:T(8,128)(2,1)S(1)}, bf16[640,640]{1,0:T(8,128)(2,1)S(1)}, bf16[640,640]{1,0:T(8,128)(2,1)}) fusion(bf16[640,5120]{1,0:T(8,128)(2,1)} %param.15, s32[]{:T(128)S(6)} %select_n.27, s32[]{:T(128)S(6)} %select_n.26, s32[]{:T(128)S(6)} %select_n.25, s32[]{:T(128)S(6)} %select_n.24), kind=kLoop, calls=%fused_computation.6 | loop fusion | bytes 6553616 | tf_op jit(solution)/shard_map/dynamic_slice | solution.py:297
  30.6 1.3 collective-permute-start
  31.9 2.6 collective-permute-start.1
  34.5 1.1 collective-permute-start.2
  35.6 15.3 %collective-permute-done.refs_11_.refs_3_ = bf16[640,640]{1,0:T(8,128)(2,1)} collective-permute-done((bf16[640,640]{1,0:T(8,128)(2,1)S(1)}, bf16[640,640]{1,0:T(8,128)(2,1)}, u32[]{:S(2)}, u32[]{:S(2)}) %collective-permute-start) | collective-permute-done | bytes 819232 | tf_op jit(solution)/shard_map/ppermute | solution.py:299
  50.8 18.7 %collective-permute-done.1.refs_12_.refs_4_ = bf16[640,640]{1,0:T(8,128)(2,1)} collective-permute-done((bf16[640,640]{1,0:T(8,128)(2,1)S(1)}, bf16[640,640]{1,0:T(8,128)(2,1)}, u32[]{:S(2)}, u32[]{:S(2)}) %collective-permute-start.1) | collective-permute-done | bytes 819232 | tf_op jit(solution)/shard_map/ppermute | solution.py:299
  69.5 24.3 %all-to-all-done.1.got_ref = bf16[32,128,384]{2,1,0:T(8,128)(2,1)S(1)} async-done(((bf16[32,128,384]{2,1,0:T(8,128)(2,1)}), bf16[32,128,384]{2,1,0:T(8,128)(2,1)S(1)}, u32[]{:S(2)}, u32[]{:S(2)}) %all-to-all-start.1) | async-done | bytes 3145760 | tf_op jit(solution)/shard_map/all_to_all | solution.py:349
  93.8 0.8 fusion
  95.3 0.2 copy-done.4
  95.5 8.9 %all-to-all-start.2 = ((bf16[32,128,256]{2,1,0:T(8,128)(2,1)}), bf16[32,128,256]{2,1,0:T(8,128)(2,1)}, u32[]{:S(2)}, u32[]{:S(2)}) async-start(bf16[32,128,256]{2,1,0:T(8,128)(2,1)} %pack.5), calls=%async_computation.2 | async-start | bytes 4194304 | tf_op jit(solution)/shard_map/all_to_all | solution.py:349
  104.5 3.8 %constant_dynamic-slice_fusion = (bf16[640,640]{1,0:T(8,128)(2,1)}, bf16[640,640]{1,0:T(8,128)(2,1)}, bf16[640,640]{1,0:T(8,128)(2,1)}, bf16[640,640]{1,0:T(8,128)(2,1)}) fusion(bf16[640,5120]{1,0:T(8,128)(2,1)} %param.15, s32[]{:T(128)S(6)} %select_n.31, s32[]{:T(128)S(6)} %select_n.30, s32[]{:T(128)S(6)} %select_n.29, s32[]{:T(128)S(6)} %select_n.28), kind=kLoop, calls=%fused_computation.2 | loop fusion | bytes 6553616 | tf_op jit(solution)/shard_map/dynamic_slice | solution.py:297
  108.3 1.1 collective-permute-start.3
  109.4 1.2 collective-permute-start.4
  110.6 3.0 %collective-permute-start.5 = (bf16[640,640]{1,0:T(8,128)(2,1)}, bf16[640,640]{1,0:T(8,128)(2,1)S(1)}, u32[]{:S(2)}, u32[]{:S(2)}) collective-permute-start(bf16[640,640]{1,0:T(8,128)(2,1)} %get-tuple-element.100), channel_id=1, source_target_pairs={{0,5},{1,4},{2,7},{3,6},{4,1},{5,0},{6,3},{7,2},{8,13},{9,12},{10,... | collective-permute-start | bytes 2457608 | tf_op jit(solution)/shard_map/ppermute | solution.py:299
  113.6 1.0 collective-permute-start.6
  114.6 20.2 %attend.2 = bf16[32,48,384]{2,1,0:T(8,128)(2,1)} custom-call(s32[1]{0:T(128)} %bitcast.2.over_ref, bf16[32,128,384]{2,1,0:T(8,128)(2,1)} %copy-done.4, bf16[32,128,640]{2,1,0:T(8,128)(2,1)S(1)} %copy-done), custom_call_target="tpu_custom_call" | custom-call | flops 9663676416 | bytes 3145728 | tf_op jit(solution)/shard_map/attend/pallas_call | solution.py:190
  134.8 15.1 %collective-permute-done.5.refs_16_.refs_4_ = bf16[640,640]{1,0:T(8,128)(2,1)S(1)} collective-permute-done((bf16[640,640]{1,0:T(8,128)(2,1)}, bf16[640,640]{1,0:T(8,128)(2,1)S(1)}, u32[]{:S(2)}, u32[]{:S(2)}) %collective-permute-start.5) | collective-permute-done | bytes 819232 | tf_op jit(solution)/shard_map/ppermute | solution.py:299
  149.9 0.0 collective-permute-done.6.refs_17_.refs_5_
  149.9 3.3 %all-to-all-done.2.got_ref = bf16[32,128,256]{2,1,0:T(8,128)(2,1)} async-done(((bf16[32,128,256]{2,1,0:T(8,128)(2,1)}), bf16[32,128,256]{2,1,0:T(8,128)(2,1)}, u32[]{:S(2)}, u32[]{:S(2)}) %all-to-all-start.2) | async-done | bytes 2097184 | tf_op jit(solution)/shard_map/all_to_all | solution.py:349
  153.2 7.2 %all-to-all-start.3 = ((bf16[32,48,384]{2,1,0:T(8,128)(2,1)}), bf16[32,48,384]{2,1,0:T(8,128)(2,1)}, u32[]{:S(2)}, u32[]{:S(2)}) async-start(bf16[32,48,384]{2,1,0:T(8,128)(2,1)} %attend.2), calls=%async_computation.3 | async-start | bytes 2359296 | tf_op jit(solution)/shard_map/all_to_all | solution.py:349
  160.4 14.6 %attend.3 = bf16[32,48,256]{2,1,0:T(8,128)(2,1)} custom-call(s32[1]{0:T(128)} %bitcast.2.over_ref, bf16[32,128,256]{2,1,0:T(8,128)(2,1)} %all-to-all-done.2.got_ref, bf16[32,128,640]{2,1,0:T(8,128)(2,1)} %get-tuple-element.107.extra_ref), custom_call_target="tpu_custom_call" | custom-call | flops 6442450944 | bytes 2097152 | tf_op jit(solution)/shard_map/attend/pallas_call | solution.py:190
  175.0 13.0 %all-to-all-done.3.got_ref = bf16[32,48,384]{2,1,0:T(8,128)(2,1)} async-done(((bf16[32,48,384]{2,1,0:T(8,128)(2,1)}), bf16[32,48,384]{2,1,0:T(8,128)(2,1)}, u32[]{:S(2)}, u32[]{:S(2)}) %all-to-all-start.3) | async-done | bytes 1179680 | tf_op jit(solution)/shard_map/all_to_all | solution.py:349
  188.0 8.4 %all-to-all-start.4 = ((bf16[32,48,256]{2,1,0:T(8,128)(2,1)}), bf16[32,48,256]{2,1,0:T(8,128)(2,1)S(1)}, u32[]{:S(2)}, u32[]{:S(2)}) async-start(bf16[32,48,256]{2,1,0:T(8,128)(2,1)} %attend.3), calls=%async_computation.4 | async-start | bytes 1572864 | tf_op jit(solution)/shard_map/all_to_all | solution.py:349
  196.4 3.7 %unpack.3.refs_0_ = bf16[768,384]{1,0:T(8,128)(2,1)} custom-call(s32[768,128]{1,0:T(8,128)} %get-tuple-element.64.code_ref, bf16[32,48,384]{2,1,0:T(8,128)(2,1)} %all-to-all-done.3.got_ref), custom_call_target="tpu_custom_call" | custom-call | flops 905969664 | bytes 1179648 | tf_op jit(solution)/shard_map/unpack/pallas_call | solution.py:225
  200.1 1.3 collective-permute-start.10
  201.4 2.6 collective-permute-start.11
  204.0 1.1 collective-permute-start.12
  205.1 2.3 collective-permute-start.13
  207.4 8.8 %all-to-all-done.4.got_ref = bf16[32,48,256]{2,1,0:T(8,128)(2,1)S(1)} async-done(((bf16[32,48,256]{2,1,0:T(8,128)(2,1)}), bf16[32,48,256]{2,1,0:T(8,128)(2,1)S(1)}, u32[]{:S(2)}, u32[]{:S(2)}) %all-to-all-start.4) | async-done | bytes 786464 | tf_op jit(solution)/shard_map/all_to_all | solution.py:349
  216.2 0.9 copy-done.5
  217.1 2.8 %unpack.2.refs_8_ = bf16[768,256]{1,0:T(8,128)(2,1)} custom-call(s32[768,128]{1,0:T(8,128)} %get-tuple-element.64.code_ref, bf16[32,48,256]{2,1,0:T(8,128)(2,1)} %copy-done.5), custom_call_target="tpu_custom_call" | custom-call | flops 603979776 | bytes 786432 | tf_op jit(solution)/shard_map/unpack/pallas_call | solution.py:225
  219.9 0.0 collective-permute-done.10.refs_1_
  219.9 8.8 %collective-permute-done.11.refs_2_ = bf16[768,384]{1,0:T(8,128)(2,1)S(1)} collective-permute-done((bf16[768,384]{1,0:T(8,128)(2,1)}, bf16[768,384]{1,0:T(8,128)(2,1)S(1)}, u32[]{:S(2)}, u32[]{:S(2)}) %collective-permute-start.11) | collective-permute-done | bytes 589856 | tf_op jit(solution)/shard_map/ppermute | solution.py:309
  228.8 0.4 collective-permute-done.12.refs_3_
  229.1 2.1 collective-permute-start.14
  231.2 0.1 collective-permute-start.15
  231.3 0.4 collective-permute-start.16
  231.7 0.1 collective-permute-start.17
  231.8 0.0 collective-permute-done.13.refs_4_
  231.8 0.8 collective-permute-start.7
  232.6 2.3 collective-permute-done.17.refs_9_
  234.9 2.2 collective-permute-start.8
  237.1 1.0 collective-permute-start.9
  238.2 0.8 copy-done.11
  238.9 0.8 copy-done.12
  239.7 9.8 %project.3.refs_6_ = f32[768,640]{1,0:T(8,128)} custom-call(bf16[768,384]{1,0:T(8,128)(2,1)} %unpack.3.refs_0_, bf16[768,384]{1,0:T(8,128)(2,1)} %copy-done.6, bf16[768,384]{1,0:T(8,128)(2,1)} %copy-done.7, bf16[768,384]{1,0:T(8,128)(2,1)} %copy-done.8, bf16[768,384]{1,0:T(8,128)(2,1)} %copy-done.9, bf16[768,384]{1,0:T(8,128)(2,1)} %copy-done.10, ...), custom_call_target="tpu_custom_call" | custom-call | flops 3523215360 | bytes 10092544 | tf_op jit(solution)/shard_map/project/pallas_call | solution.py:275
  249.6 0.0 collective-permute-done.7.refs_0_
  249.6 0.0 copy-start.16
  249.6 2.6 collective-permute-done.8.refs_1_
  252.1 2.8 %collective-permute-done.9.refs_2_ = bf16[768,256]{1,0:T(8,128)(2,1)S(1)} collective-permute-done((bf16[768,256]{1,0:T(8,128)(2,1)}, bf16[768,256]{1,0:T(8,128)(2,1)S(1)}, u32[]{:S(2)}, u32[]{:S(2)}) %collective-permute-start.9) | collective-permute-done | bytes 393248 | tf_op jit(solution)/shard_map/ppermute | solution.py:309
  255.0 1.0 collective-permute-start.18
  255.9 0.0 collective-permute-start.19
  255.9 0.5 collective-permute-start.20
  256.5 5.1 %project.4.refs_6_ = f32[768,640]{1,0:T(8,128)} custom-call(bf16[768,256]{1,0:T(8,128)(2,1)} %copy-done.16, bf16[768,256]{1,0:T(8,128)(2,1)} %copy-done.17, bf16[768,256]{1,0:T(8,128)(2,1)} %copy-done.18, bf16[640,640]{1,0:T(8,128)(2,1)} %collective-permute-done.refs_11_.refs_3_, bf16[640,640]{1,0:T(8,128)(2,1)} %collective-permute-done.1.refs_12_.refs_4_, ...), custom_call_target="tpu_custom_call" | custom-call | flops 754974720 | bytes 2162688 | tf_op jit(solution)/shard_map/project/pallas_call | solution.py:275
  261.6 0.0 collective-permute-done.18.refs_0_
  261.6 0.7 copy-done.13
  262.3 0.1 copy-done.14
  262.5 0.7 copy-done.15
  263.2 4.9 %project.5 = bf16[768,640]{1,0:T(8,128)(2,1)} custom-call(bf16[768,256]{1,0:T(8,128)(2,1)} %copy-done.13, bf16[768,256]{1,0:T(8,128)(2,1)} %copy-done.14, bf16[768,256]{1,0:T(8,128)(2,1)} %copy-done.15, bf16[640,640]{1,0:T(8,128)(2,1)} %copy-done.1, bf16[640,640]{1,0:T(8,128)(2,1)} %copy-done.2, bf16[640,640]{1,0:T(8,128)(2,1)} %copy-done.3, ...), custom_call_target="tpu_custom_call" | custom-call | flops 754974720 | bytes 2162688 | tf_op jit(solution)/shard_map/project/pallas_call | solution.py:275
  (42 shorter events, 0.1 us)
Async XLA Ops:
  10.4 83.4 %all-to-all-start.1 = ((bf16[32,128,384]{2,1,0:T(8,128)(2,1)}), bf16[32,128,384]{2,1,0:T(8,128)(2,1)S(1)}, u32[]{:S(2)}, u32[]{:S(2)}) async-start(bf16[32,128,384]{2,1,0:T(8,128)(2,1)} %pack.4), calls=%async_computation.1 | async-start | bytes 6291456 | tf_op jit(solution)/shard_map/all_to_all | solution.py:349
  30.6 20.3 %collective-permute-start = (bf16[640,640]{1,0:T(8,128)(2,1)S(1)}, bf16[640,640]{1,0:T(8,128)(2,1)}, u32[]{:S(2)}, u32[]{:S(2)}) collective-permute-start(bf16[640,640]{1,0:T(8,128)(2,1)S(1)} %get-tuple-element.105), channel_id=1, source_target_pairs={{0,2},{1,3},{2,4},{3,5},{4,6},{5,7},{6,0},{7,1},{8,10},{9,11},{10,... | collective-permute-start | bytes 2457608 | tf_op jit(solution)/shard_map/ppermute | solution.py:299
  31.9 37.6 %collective-permute-start.1 = (bf16[640,640]{1,0:T(8,128)(2,1)S(1)}, bf16[640,640]{1,0:T(8,128)(2,1)}, u32[]{:S(2)}, u32[]{:S(2)}) collective-permute-start(bf16[640,640]{1,0:T(8,128)(2,1)S(1)} %get-tuple-element.104), channel_id=1, source_target_pairs={{0,4},{1,5},{2,6},{3,7},{4,0},{5,1},{6,2},{7,3},{8,12},{9,13},{10,... | collective-permute-start | bytes 2457608 | tf_op jit(solution)/shard_map/ppermute | solution.py:299
  34.5 35.0 %collective-permute-start.2 = (bf16[640,640]{1,0:T(8,128)(2,1)S(1)}, bf16[640,640]{1,0:T(8,128)(2,1)}, u32[]{:S(2)}, u32[]{:S(2)}) collective-permute-start(bf16[640,640]{1,0:T(8,128)(2,1)S(1)} %get-tuple-element.103), channel_id=1, source_target_pairs={{0,6},{1,7},{2,0},{3,1},{4,2},{5,3},{6,4},{7,5},{8,14},{9,15},{10,... | collective-permute-start | bytes 2457608 | tf_op jit(solution)/shard_map/ppermute | solution.py:299
  93.8 1.8 copy-start.4
  95.5 57.7 %all-to-all-start.2 = ((bf16[32,128,256]{2,1,0:T(8,128)(2,1)}), bf16[32,128,256]{2,1,0:T(8,128)(2,1)}, u32[]{:S(2)}, u32[]{:S(2)}) async-start(bf16[32,128,256]{2,1,0:T(8,128)(2,1)} %pack.5), calls=%async_computation.2 | async-start | bytes 4194304 | tf_op jit(solution)/shard_map/all_to_all | solution.py:349
  104.5 10.1 %copy-start = (bf16[32,128,640]{2,1,0:T(8,128)(2,1)S(1)}, bf16[32,128,640]{2,1,0:T(8,128)(2,1)}, u32[]{:S(2)}) copy-start(bf16[32,128,640]{2,1,0:T(8,128)(2,1)} %get-tuple-element.107.extra_ref) | copy-start | bytes 15728644
  108.3 26.4 %collective-permute-start.3 = (bf16[640,640]{1,0:T(8,128)(2,1)}, bf16[640,640]{1,0:T(8,128)(2,1)}, u32[]{:S(2)}, u32[]{:S(2)}) collective-permute-start(bf16[640,640]{1,0:T(8,128)(2,1)} %get-tuple-element.102), channel_id=1, source_target_pairs={{0,1},{1,0},{2,3},{3,2},{4,5},{5,4},{6,7},{7,6},{8,9},{9,8},{10,11... | collective-permute-start | bytes 2457608 | tf_op jit(solution)/shard_map/ppermute | solution.py:299
  109.4 25.3 %collective-permute-start.4 = (bf16[640,640]{1,0:T(8,128)(2,1)}, bf16[640,640]{1,0:T(8,128)(2,1)S(1)}, u32[]{:S(2)}, u32[]{:S(2)}) collective-permute-start(bf16[640,640]{1,0:T(8,128)(2,1)} %get-tuple-element.101), channel_id=1, source_target_pairs={{0,3},{1,2},{2,5},{3,4},{4,7},{5,6},{6,1},{7,0},{8,11},{9,10},{10,... | collective-permute-start | bytes 2457608 | tf_op jit(solution)/shard_map/ppermute | solution.py:299
  110.6 39.3 %collective-permute-start.5 = (bf16[640,640]{1,0:T(8,128)(2,1)}, bf16[640,640]{1,0:T(8,128)(2,1)S(1)}, u32[]{:S(2)}, u32[]{:S(2)}) collective-permute-start(bf16[640,640]{1,0:T(8,128)(2,1)} %get-tuple-element.100), channel_id=1, source_target_pairs={{0,5},{1,4},{2,7},{3,6},{4,1},{5,0},{6,3},{7,2},{8,13},{9,12},{10,... | collective-permute-start | bytes 2457608 | tf_op jit(solution)/shard_map/ppermute | solution.py:299
  113.6 36.3 %collective-permute-start.6 = (bf16[640,640]{1,0:T(8,128)(2,1)}, bf16[640,640]{1,0:T(8,128)(2,1)S(1)}, u32[]{:S(2)}, u32[]{:S(2)}) collective-permute-start(bf16[640,640]{1,0:T(8,128)(2,1)} %get-tuple-element.99), channel_id=1, source_target_pairs={{0,7},{1,6},{2,1},{3,0},{4,3},{5,2},{6,5},{7,4},{8,15},{9,14},{10,... | collective-permute-start | bytes 2457608 | tf_op jit(solution)/shard_map/ppermute | solution.py:299
  134.8 40.2 %copy-start.1 = (bf16[640,640]{1,0:T(8,128)(2,1)}, bf16[640,640]{1,0:T(8,128)(2,1)S(1)}, u32[]{:S(2)}) copy-start(bf16[640,640]{1,0:T(8,128)(2,1)S(1)} %collective-permute-done.4.refs_15_.refs_3_) | copy-start | bytes 2457604
  149.9 25.1 %copy-start.2 = (bf16[640,640]{1,0:T(8,128)(2,1)}, bf16[640,640]{1,0:T(8,128)(2,1)S(1)}, u32[]{:S(2)}) copy-start(bf16[640,640]{1,0:T(8,128)(2,1)S(1)} %collective-permute-done.5.refs_16_.refs_4_) | copy-start | bytes 2457604
  149.9 25.1 %copy-start.3 = (bf16[640,640]{1,0:T(8,128)(2,1)}, bf16[640,640]{1,0:T(8,128)(2,1)S(1)}, u32[]{:S(2)}) copy-start(bf16[640,640]{1,0:T(8,128)(2,1)S(1)} %collective-permute-done.6.refs_17_.refs_5_) | copy-start | bytes 2457604
  153.2 34.8 %all-to-all-start.3 = ((bf16[32,48,384]{2,1,0:T(8,128)(2,1)}), bf16[32,48,384]{2,1,0:T(8,128)(2,1)}, u32[]{:S(2)}, u32[]{:S(2)}) async-start(bf16[32,48,384]{2,1,0:T(8,128)(2,1)} %attend.2), calls=%async_computation.3 | async-start | bytes 2359296 | tf_op jit(solution)/shard_map/all_to_all | solution.py:349
  188.0 28.2 %all-to-all-start.4 = ((bf16[32,48,256]{2,1,0:T(8,128)(2,1)}), bf16[32,48,256]{2,1,0:T(8,128)(2,1)S(1)}, u32[]{:S(2)}, u32[]{:S(2)}) async-start(bf16[32,48,256]{2,1,0:T(8,128)(2,1)} %attend.3), calls=%async_computation.4 | async-start | bytes 1572864 | tf_op jit(solution)/shard_map/all_to_all | solution.py:349
  200.1 19.8 %collective-permute-start.10 = (bf16[768,384]{1,0:T(8,128)(2,1)}, bf16[768,384]{1,0:T(8,128)(2,1)S(1)}, u32[]{:S(2)}, u32[]{:S(2)}) collective-permute-start(bf16[768,384]{1,0:T(8,128)(2,1)} %unpack.3.refs_0_), channel_id=1, source_target_pairs={{0,2},{1,3},{2,4},{3,5},{4,6},{5,7},{6,0},{7,1},{8,10},{9,11},{10,... | collective-permute-start | bytes 1769480 | tf_op jit(solution)/shard_map/ppermute | solution.py:309
  201.4 27.4 %collective-permute-start.11 = (bf16[768,384]{1,0:T(8,128)(2,1)}, bf16[768,384]{1,0:T(8,128)(2,1)S(1)}, u32[]{:S(2)}, u32[]{:S(2)}) collective-permute-start(bf16[768,384]{1,0:T(8,128)(2,1)} %unpack.3.refs_0_), channel_id=1, source_target_pairs={{0,4},{1,5},{2,6},{3,7},{4,0},{5,1},{6,2},{7,3},{8,12},{9,13},{10,... | collective-permute-start | bytes 1769480 | tf_op jit(solution)/shard_map/ppermute | solution.py:309
  204.0 25.1 %collective-permute-start.12 = (bf16[768,384]{1,0:T(8,128)(2,1)}, bf16[768,384]{1,0:T(8,128)(2,1)S(1)}, u32[]{:S(2)}, u32[]{:S(2)}) collective-permute-start(bf16[768,384]{1,0:T(8,128)(2,1)} %unpack.3.refs_0_), channel_id=1, source_target_pairs={{0,6},{1,7},{2,0},{3,1},{4,2},{5,3},{6,4},{7,5},{8,14},{9,15},{10,... | collective-permute-start | bytes 1769480 | tf_op jit(solution)/shard_map/ppermute | solution.py:309
  205.1 26.8 %collective-permute-start.13 = (bf16[768,384]{1,0:T(8,128)(2,1)}, bf16[768,384]{1,0:T(8,128)(2,1)S(1)}, u32[]{:S(2)}, u32[]{:S(2)}) collective-permute-start(bf16[768,384]{1,0:T(8,128)(2,1)} %unpack.3.refs_0_), channel_id=1, source_target_pairs={{0,1},{1,0},{2,3},{3,2},{4,5},{5,4},{6,7},{7,6},{8,9},{9,8},{10,11... | collective-permute-start | bytes 1769480 | tf_op jit(solution)/shard_map/ppermute | solution.py:316
  216.2 0.9 copy-start.5
  219.9 18.2 %copy-start.6 = (bf16[768,384]{1,0:T(8,128)(2,1)}, bf16[768,384]{1,0:T(8,128)(2,1)S(1)}, u32[]{:S(2)}) copy-start(bf16[768,384]{1,0:T(8,128)(2,1)S(1)} %collective-permute-done.10.refs_1_) | copy-start | bytes 1769476
  228.7 9.4 %copy-start.7 = (bf16[768,384]{1,0:T(8,128)(2,1)}, bf16[768,384]{1,0:T(8,128)(2,1)S(1)}, u32[]{:S(2)}) copy-start(bf16[768,384]{1,0:T(8,128)(2,1)S(1)} %collective-permute-done.11.refs_2_) | copy-start | bytes 1769476
  229.1 9.0 %copy-start.8 = (bf16[768,384]{1,0:T(8,128)(2,1)}, bf16[768,384]{1,0:T(8,128)(2,1)S(1)}, u32[]{:S(2)}) copy-start(bf16[768,384]{1,0:T(8,128)(2,1)S(1)} %collective-permute-done.12.refs_3_) | copy-start | bytes 1769476
  229.1 8.0 %collective-permute-start.14 = (bf16[768,384]{1,0:T(8,128)(2,1)S(1)}, bf16[768,384]{1,0:T(8,128)(2,1)S(1)}, u32[]{:S(2)}, u32[]{:S(2)}) collective-permute-start(bf16[768,384]{1,0:T(8,128)(2,1)S(1)} %collective-permute-done.10.refs_1_), channel_id=1, source_target_pairs={{0,1},{1,0},{2,3},{3,2},{4,5},{5,4},{6,7},{7,6},{8,9},{9,8},{10,11... | collective-permute-start | bytes 1769480 | tf_op jit(solution)/shard_map/ppermute | solution.py:316
  231.2 6.9 %collective-permute-start.15 = (bf16[768,384]{1,0:T(8,128)(2,1)S(1)}, bf16[768,384]{1,0:T(8,128)(2,1)S(1)}, u32[]{:S(2)}, u32[]{:S(2)}) collective-permute-start(bf16[768,384]{1,0:T(8,128)(2,1)S(1)} %collective-permute-done.11.refs_2_), channel_id=1, source_target_pairs={{0,1},{1,0},{2,3},{3,2},{4,5},{5,4},{6,7},{7,6},{8,9},{9,8},{10,11... | collective-permute-start | bytes 1769480 | tf_op jit(solution)/shard_map/ppermute | solution.py:316
  231.3 6.8 %collective-permute-start.16 = (bf16[768,384]{1,0:T(8,128)(2,1)S(1)}, bf16[768,384]{1,0:T(8,128)(2,1)S(1)}, u32[]{:S(2)}, u32[]{:S(2)}) collective-permute-start(bf16[768,384]{1,0:T(8,128)(2,1)S(1)} %collective-permute-done.12.refs_3_), channel_id=1, source_target_pairs={{0,1},{1,0},{2,3},{3,2},{4,5},{5,4},{6,7},{7,6},{8,9},{9,8},{10,11... | collective-permute-start | bytes 1769480 | tf_op jit(solution)/shard_map/ppermute | solution.py:316
  231.7 3.2 %collective-permute-start.17 = (bf16[768,256]{1,0:T(8,128)(2,1)}, bf16[768,256]{1,0:T(8,128)(2,1)S(1)}, u32[]{:S(2)}, u32[]{:S(2)}) collective-permute-start(bf16[768,256]{1,0:T(8,128)(2,1)} %unpack.2.refs_8_), channel_id=1, source_target_pairs={{0,1},{1,0},{2,3},{3,2},{4,5},{5,4},{6,7},{7,6},{8,9},{9,8},{10,11... | collective-permute-start | bytes 1179656 | tf_op jit(solution)/shard_map/ppermute | solution.py:316
  231.8 6.3 %copy-start.9 = (bf16[768,384]{1,0:T(8,128)(2,1)}, bf16[768,384]{1,0:T(8,128)(2,1)S(1)}, u32[]{:S(2)}) copy-start(bf16[768,384]{1,0:T(8,128)(2,1)S(1)} %collective-permute-done.13.refs_4_) | copy-start | bytes 1769476
  231.8 17.7 %collective-permute-start.7 = (bf16[768,256]{1,0:T(8,128)(2,1)}, bf16[768,256]{1,0:T(8,128)(2,1)S(1)}, u32[]{:S(2)}, u32[]{:S(2)}) collective-permute-start(bf16[768,256]{1,0:T(8,128)(2,1)} %unpack.2.refs_8_), channel_id=1, source_target_pairs={{0,2},{1,3},{2,4},{3,5},{4,6},{5,7},{6,0},{7,1},{8,10},{9,11},{10,... | collective-permute-start | bytes 1179656 | tf_op jit(solution)/shard_map/ppermute | solution.py:309
  234.9 3.2 %copy-start.19 = (bf16[768,256]{1,0:T(8,128)(2,1)}, bf16[768,256]{1,0:T(8,128)(2,1)S(1)}, u32[]{:S(2)}) copy-start(bf16[768,256]{1,0:T(8,128)(2,1)S(1)} %collective-permute-done.17.refs_9_) | copy-start | bytes 1179652
  234.9 17.2 %collective-permute-start.8 = (bf16[768,256]{1,0:T(8,128)(2,1)}, bf16[768,256]{1,0:T(8,128)(2,1)S(1)}, u32[]{:S(2)}, u32[]{:S(2)}) collective-permute-start(bf16[768,256]{1,0:T(8,128)(2,1)} %unpack.2.refs_8_), channel_id=1, source_target_pairs={{0,4},{1,5},{2,6},{3,7},{4,0},{5,1},{6,2},{7,3},{8,12},{9,13},{10,... | collective-permute-start | bytes 1179656 | tf_op jit(solution)/shard_map/ppermute | solution.py:309
  237.1 1.0 copy-start.10
  237.1 17.9 %collective-permute-start.9 = (bf16[768,256]{1,0:T(8,128)(2,1)}, bf16[768,256]{1,0:T(8,128)(2,1)S(1)}, u32[]{:S(2)}, u32[]{:S(2)}) collective-permute-start(bf16[768,256]{1,0:T(8,128)(2,1)} %unpack.2.refs_8_), channel_id=1, source_target_pairs={{0,6},{1,7},{2,0},{3,1},{4,2},{5,3},{6,4},{7,5},{8,14},{9,15},{10,... | collective-permute-start | bytes 1179656 | tf_op jit(solution)/shard_map/ppermute | solution.py:309
  238.1 0.8 copy-start.11
  238.9 0.8 copy-start.12
  249.6 6.9 %copy-start.16 = (bf16[768,256]{1,0:T(8,128)(2,1)}, bf16[768,256]{1,0:T(8,128)(2,1)S(1)}, u32[]{:S(2)}) copy-start(bf16[768,256]{1,0:T(8,128)(2,1)S(1)} %collective-permute-done.7.refs_0_) | copy-start | bytes 1179652
  252.1 4.3 %copy-start.17 = (bf16[768,256]{1,0:T(8,128)(2,1)}, bf16[768,256]{1,0:T(8,128)(2,1)S(1)}, u32[]{:S(2)}) copy-start(bf16[768,256]{1,0:T(8,128)(2,1)S(1)} %collective-permute-done.8.refs_1_) | copy-start | bytes 1179652
  255.0 1.5 copy-start.18
  255.0 6.6 %collective-permute-start.18 = (bf16[768,256]{1,0:T(8,128)(2,1)S(1)}, bf16[768,256]{1,0:T(8,128)(2,1)S(1)}, u32[]{:S(2)}, u32[]{:S(2)}) collective-permute-start(bf16[768,256]{1,0:T(8,128)(2,1)S(1)} %collective-permute-done.7.refs_0_), channel_id=1, source_target_pairs={{0,1},{1,0},{2,3},{3,2},{4,5},{5,4},{6,7},{7,6},{8,9},{9,8},{10,11... | collective-permute-start | bytes 1179656 | tf_op jit(solution)/shard_map/ppermute | solution.py:316
  255.9 5.6 %collective-permute-start.19 = (bf16[768,256]{1,0:T(8,128)(2,1)S(1)}, bf16[768,256]{1,0:T(8,128)(2,1)S(1)}, u32[]{:S(2)}, u32[]{:S(2)}) collective-permute-start(bf16[768,256]{1,0:T(8,128)(2,1)S(1)} %collective-permute-done.8.refs_1_), channel_id=1, source_target_pairs={{0,1},{1,0},{2,3},{3,2},{4,5},{5,4},{6,7},{7,6},{8,9},{9,8},{10,11... | collective-permute-start | bytes 1179656 | tf_op jit(solution)/shard_map/ppermute | solution.py:316
  255.9 5.7 %collective-permute-start.20 = (bf16[768,256]{1,0:T(8,128)(2,1)S(1)}, bf16[768,256]{1,0:T(8,128)(2,1)S(1)}, u32[]{:S(2)}, u32[]{:S(2)}) collective-permute-start(bf16[768,256]{1,0:T(8,128)(2,1)S(1)} %collective-permute-done.9.refs_2_), channel_id=1, source_target_pairs={{0,1},{1,0},{2,3},{3,2},{4,5},{5,4},{6,7},{7,6},{8,9},{9,8},{10,11... | collective-permute-start | bytes 1179656 | tf_op jit(solution)/shard_map/ppermute | solution.py:316
  261.6 0.7 copy-start.13
  261.6 0.9 copy-start.14
  262.5 0.7 copy-start.15

commit v4 on v3

--- a/solution.py
+++ b/solution.py
@@ -378,7 +378,6 @@
     back1 = exchange(answer1)
     mine1 = unpack(code, back1)
     mine0 = unpack(code, back0)
-    own_w, y_w, other_w, far_w = weights[0], weights[1:4], weights[4], weights[5:]
     chunk0, chunk1 = BACK[0][1:], BACK[1][1:]
 
     def items(parts, weights, chunk):
@@ -386,16 +385,12 @@
 
     y0 = along_y(mine0, groups)
     *y0, _ = after((*y0, mine1))
-    parts0 = [mine0, *y0, swapped(mine0, groups), *[swapped(part, groups) for part in y0]]
+    parts0 = [mine0, *y0, *[swapped(part, groups) for part in (mine0, *y0)]]
     y1 = along_y(mine1, groups)
-    near1 = [mine1, swapped(mine1, groups)]
-    total = project(
-        items(parts0, weights, chunk0) + items(near1, [own_w, other_w], chunk1), None, F32
-    )
+    total = project(items(parts0, weights, chunk0) + items([mine1], weights, chunk1), None, F32)
     *y1, total = after((*y1, total))
-    far1 = [swapped(part, groups) for part in y1]
-    total = project(items(y1, y_w, chunk1), total, F32)
-    return project(items(far1, far_w, chunk1), total, BF16)
+    parts1 = [*y1, *[swapped(part, groups) for part in (mine1, *y1)]]
+    return project(items(parts1, weights[1:], chunk1), total, BF16)
 
 
 def solution(mesh):

time: 269 us -> 266 us (0.989)
  Pallas kernels: 75.3 us -> 69.9 us
    pallas_call x3 -> x2, Pallas kernels: 19.8 us -> 16.2 us  [project(): pl.pallas_call(functools.partial(project_kernel, spans), grid=(rows // st...]
    unnamed x41 -> x51, local copies, waits for them, and re-layouts: 5.72 us -> 4.06 us
  transfers between devices with their start and end apart: 25 -> 25, of which waited for: 12 -> 13; matrix products, arithmetic and copies ran while one was open for 3% -> 3% of each run, Pallas kernels for 23% -> 20%
where the time goes in v4:
time: 266 us; the launch traced here: 265 us
  waiting for transfers between devices  117 us (44%)
  Pallas kernels  69.9 us (26%)
  starting transfers between devices  64.8 us (24%)
  local copies, waits for them, and re-layouts  11 us (4%)
    all_to_all x4, waiting for transfers between devices, exchange(): return lax.all_to_all(block, 'ctx', split_axis=0, concat_axis=0, tiled=True)  51 us
    ppermute x7, waiting for transfers between devices, own_columns(): lax.ppermute(block, 'head', [(g, ((g ^ core) + along) % groups) for g in...  49 us
    all_to_all x4, starting transfers between devices, exchange(): return lax.all_to_all(block, 'ctx', split_axis=0, concat_axis=0, tiled=True)  36.7 us
    pallas_call x2, Pallas kernels, attend(): pl.pallas_call(functools.partial(attend_kernel, qslots, kslots, sources),...  34.7 us
    pallas_call x2, Pallas kernels, project(): pl.pallas_call(functools.partial(project_kernel, spans), grid=(rows // st...  16.2 us
    ppermute x6, waiting for transfers between devices, along_y(): lax.ppermute(rows, 'head', [(g, (g + along) % groups) for g in range(grou...  14.7 us
    ppermute x7, starting transfers between devices, own_columns(): lax.ppermute(block, 'head', [(g, ((g ^ core) + along) % groups) for g in...  11.3 us
    pallas_call x2, Pallas kernels, pack(): pl.pallas_call(functools.partial(pack_kernel, columns, qslots, kslots), g...  10.2 us
  transfers between devices with their start and end apart: 25, of which 13 were waited for; matrix products, arithmetic and copies ran while one was open for 3% of the time, Pallas kernels for 20%

profile of v4, /device:TPU:1, one launch (start us, length us, event | category | flops | bytes accessed | tf_op | source)
XLA Modules:
  0.0 265.1 jit_solution(12691328269709321580)
XLA Ops:
  0.0 1.4 copy.8.pattern_ref
  1.4 2.3 plan.1
  3.6 6.7 %pack.4 = bf16[32,128,384]{2,1,0:T(8,128)(2,1)} custom-call(s32[32,768]{1,0:T(8,128)S(1)} %get-tuple-element.65.refs_0_, s32[32,768]{1,0:T(8,128)S(1)} %get-tuple-element.66.refs_1_, s32[32,128]{1,0:T(8,128)S(1)} %get-tuple-element.67.refs_2_, s32[8,128]{1,0:T(8,128)S(1)} %get-tuple-element.68.refs_3_, bf16[768,640]{1,0:T(8,128)(2,1)} %refs_4_.3, ...), custom_call_target="tpu_custom_call" | custom-call | flops 2415919104 | bytes 3145728 | tf_op jit(solution)/shard_map/pack/pallas_call | solution.py:118
  10.4 12.2 %all-to-all-start.1 = ((bf16[32,128,384]{2,1,0:T(8,128)(2,1)}), bf16[32,128,384]{2,1,0:T(8,128)(2,1)}, u32[]{:S(2)}, u32[]{:S(2)}) async-start(bf16[32,128,384]{2,1,0:T(8,128)(2,1)} %pack.4), calls=%async_computation.1 | async-start | bytes 6291456 | tf_op jit(solution)/shard_map/all_to_all | solution.py:349
  22.7 3.4 %pack.5 = bf16[32,128,256]{2,1,0:T(8,128)(2,1)} custom-call(s32[32,768]{1,0:T(8,128)S(1)} %get-tuple-element.65.refs_0_, s32[32,768]{1,0:T(8,128)S(1)} %get-tuple-element.66.refs_1_, s32[32,128]{1,0:T(8,128)S(1)} %get-tuple-element.67.refs_2_, s32[8,128]{1,0:T(8,128)S(1)} %get-tuple-element.68.refs_3_, bf16[768,640]{1,0:T(8,128)(2,1)S(1)} %copy-done.22, ...), custom_call_target="tpu_custom_call" | custom-call | flops 1610612736 | bytes 2097152 | tf_op jit(solution)/shard_map/pack/pallas_call | solution.py:118
  26.1 3.1 %constant_dynamic-slice_fusion.4 = (bf16[640,640]{1,0:T(8,128)(2,1)S(1)}, bf16[640,640]{1,0:T(8,128)(2,1)S(1)}, bf16[640,640]{1,0:T(8,128)(2,1)S(1)}, bf16[640,640]{1,0:T(8,128)(2,1)}) fusion(bf16[640,5120]{1,0:T(8,128)(2,1)} %param.15, s32[]{:T(128)S(6)} %select_n.27, s32[]{:T(128)S(6)} %select_n.26, s32[]{:T(128)S(6)} %select_n.25, s32[]{:T(128)S(6)} %select_n.24), kind=kLoop, calls=%fused_computation.6 | loop fusion | bytes 6553616 | tf_op jit(solution)/shard_map/dynamic_slice | solution.py:297
  29.2 1.3 collective-permute-start
  30.5 2.6 collective-permute-start.1
  33.1 1.1 collective-permute-start.2
  34.2 15.3 %collective-permute-done.refs_10_.refs_7_ = bf16[640,640]{1,0:T(8,128)(2,1)S(1)} collective-permute-done((bf16[640,640]{1,0:T(8,128)(2,1)S(1)}, bf16[640,640]{1,0:T(8,128)(2,1)S(1)}, u32[]{:S(2)}, u32[]{:S(2)}) %collective-permute-start) | collective-permute-done | bytes 819232 | tf_op jit(solution)/shard_map/ppermute | solution.py:299
  49.5 18.7 %collective-permute-done.1.refs_11_.refs_8_ = bf16[640,640]{1,0:T(8,128)(2,1)S(1)} collective-permute-done((bf16[640,640]{1,0:T(8,128)(2,1)S(1)}, bf16[640,640]{1,0:T(8,128)(2,1)S(1)}, u32[]{:S(2)}, u32[]{:S(2)}) %collective-permute-start.1) | collective-permute-done | bytes 819232 | tf_op jit(solution)/shard_map/ppermute | solution.py:299
  68.1 0.0 collective-permute-done.2.refs_12_.refs_9_
  68.1 26.0 %all-to-all-done.1.got_ref = bf16[32,128,384]{2,1,0:T(8,128)(2,1)} async-done(((bf16[32,128,384]{2,1,0:T(8,128)(2,1)}), bf16[32,128,384]{2,1,0:T(8,128)(2,1)}, u32[]{:S(2)}, u32[]{:S(2)}) %all-to-all-start.1) | async-done | bytes 3145760 | tf_op jit(solution)/shard_map/all_to_all | solution.py:349
  94.1 1.5 fusion
  96.4 8.9 %all-to-all-start.2 = ((bf16[32,128,256]{2,1,0:T(8,128)(2,1)}), bf16[32,128,256]{2,1,0:T(8,128)(2,1)}, u32[]{:S(2)}, u32[]{:S(2)}) async-start(bf16[32,128,256]{2,1,0:T(8,128)(2,1)} %pack.5), calls=%async_computation.2 | async-start | bytes 4194304 | tf_op jit(solution)/shard_map/all_to_all | solution.py:349
  105.3 3.9 %constant_dynamic-slice_fusion = (bf16[640,640]{1,0:T(8,128)(2,1)}, bf16[640,640]{1,0:T(8,128)(2,1)}, bf16[640,640]{1,0:T(8,128)(2,1)}, bf16[640,640]{1,0:T(8,128)(2,1)}) fusion(bf16[640,5120]{1,0:T(8,128)(2,1)} %param.15, s32[]{:T(128)S(6)} %select_n.31, s32[]{:T(128)S(6)} %select_n.30, s32[]{:T(128)S(6)} %select_n.29, s32[]{:T(128)S(6)} %select_n.28), kind=kLoop, calls=%fused_computation.2 | loop fusion | bytes 6553616 | tf_op jit(solution)/shard_map/dynamic_slice | solution.py:297
  109.2 1.1 collective-permute-start.3
  110.3 1.3 collective-permute-start.4
  111.6 2.9 %collective-permute-start.5 = (bf16[640,640]{1,0:T(8,128)(2,1)}, bf16[640,640]{1,0:T(8,128)(2,1)S(1)}, u32[]{:S(2)}, u32[]{:S(2)}) collective-permute-start(bf16[640,640]{1,0:T(8,128)(2,1)} %get-tuple-element.100), channel_id=1, source_target_pairs={{0,5},{1,4},{2,7},{3,6},{4,1},{5,0},{6,3},{7,2},{8,13},{9,12},{10,... | collective-permute-start | bytes 2457608 | tf_op jit(solution)/shard_map/ppermute | solution.py:299
  114.6 1.0 collective-permute-start.6
  115.5 20.2 %attend.2 = bf16[32,48,384]{2,1,0:T(8,128)(2,1)} custom-call(s32[1]{0:T(128)} %bitcast.2.over_ref, bf16[32,128,384]{2,1,0:T(8,128)(2,1)} %all-to-all-done.1.got_ref, bf16[32,128,640]{2,1,0:T(8,128)(2,1)S(1)} %copy-done), custom_call_target="tpu_custom_call" | custom-call | flops 9663676416 | bytes 3145728 | tf_op jit(solution)/shard_map/attend/pallas_call | solution.py:190
  135.7 0.0 collective-permute-done.3.refs_13_.refs_10_
  135.7 0.0 collective-permute-done.4.refs_14_.refs_11_
  135.7 15.1 %collective-permute-done.5.refs_15_.refs_12_ = bf16[640,640]{1,0:T(8,128)(2,1)S(1)} collective-permute-done((bf16[640,640]{1,0:T(8,128)(2,1)}, bf16[640,640]{1,0:T(8,128)(2,1)S(1)}, u32[]{:S(2)}, u32[]{:S(2)}) %collective-permute-start.5) | collective-permute-done | bytes 819232 | tf_op jit(solution)/shard_map/ppermute | solution.py:299
  150.9 0.0 collective-permute-done.6.refs_16_.refs_13_
  150.9 3.2 %all-to-all-done.2.got_ref = bf16[32,128,256]{2,1,0:T(8,128)(2,1)} async-done(((bf16[32,128,256]{2,1,0:T(8,128)(2,1)}), bf16[32,128,256]{2,1,0:T(8,128)(2,1)}, u32[]{:S(2)}, u32[]{:S(2)}) %all-to-all-start.2) | async-done | bytes 2097184 | tf_op jit(solution)/shard_map/all_to_all | solution.py:349
  154.0 7.2 %all-to-all-start.3 = ((bf16[32,48,384]{2,1,0:T(8,128)(2,1)}), bf16[32,48,384]{2,1,0:T(8,128)(2,1)}, u32[]{:S(2)}, u32[]{:S(2)}) async-start(bf16[32,48,384]{2,1,0:T(8,128)(2,1)} %attend.2), calls=%async_computation.3 | async-start | bytes 2359296 | tf_op jit(solution)/shard_map/all_to_all | solution.py:349
  161.2 14.6 %attend.3 = bf16[32,48,256]{2,1,0:T(8,128)(2,1)} custom-call(s32[1]{0:T(128)} %bitcast.2.over_ref, bf16[32,128,256]{2,1,0:T(8,128)(2,1)} %all-to-all-done.2.got_ref, bf16[32,128,640]{2,1,0:T(8,128)(2,1)} %get-tuple-element.107.extra_ref), custom_call_target="tpu_custom_call" | custom-call | flops 6442450944 | bytes 2097152 | tf_op jit(solution)/shard_map/attend/pallas_call | solution.py:190
  175.8 13.0 %all-to-all-done.3.got_ref = bf16[32,48,384]{2,1,0:T(8,128)(2,1)} async-done(((bf16[32,48,384]{2,1,0:T(8,128)(2,1)}), bf16[32,48,384]{2,1,0:T(8,128)(2,1)}, u32[]{:S(2)}, u32[]{:S(2)}) %all-to-all-start.3) | async-done | bytes 1179680 | tf_op jit(solution)/shard_map/all_to_all | solution.py:349
  188.8 8.4 %all-to-all-start.4 = ((bf16[32,48,256]{2,1,0:T(8,128)(2,1)}), bf16[32,48,256]{2,1,0:T(8,128)(2,1)S(1)}, u32[]{:S(2)}, u32[]{:S(2)}) async-start(bf16[32,48,256]{2,1,0:T(8,128)(2,1)} %attend.3), calls=%async_computation.4 | async-start | bytes 1572864 | tf_op jit(solution)/shard_map/all_to_all | solution.py:349
  197.3 3.6 %unpack.3.refs_0_ = bf16[768,384]{1,0:T(8,128)(2,1)} custom-call(s32[768,128]{1,0:T(8,128)} %get-tuple-element.64.code_ref, bf16[32,48,384]{2,1,0:T(8,128)(2,1)} %all-to-all-done.3.got_ref), custom_call_target="tpu_custom_call" | custom-call | flops 905969664 | bytes 1179648 | tf_op jit(solution)/shard_map/unpack/pallas_call | solution.py:225
  200.9 1.5 collective-permute-start.10
  202.4 2.4 collective-permute-start.11
  204.9 1.1 collective-permute-start.12
  206.0 2.3 collective-permute-start.13
  208.3 8.8 %all-to-all-done.4.got_ref = bf16[32,48,256]{2,1,0:T(8,128)(2,1)S(1)} async-done(((bf16[32,48,256]{2,1,0:T(8,128)(2,1)}), bf16[32,48,256]{2,1,0:T(8,128)(2,1)S(1)}, u32[]{:S(2)}, u32[]{:S(2)}) %all-to-all-start.4) | async-done | bytes 786464 | tf_op jit(solution)/shard_map/all_to_all | solution.py:349
  217.0 0.9 copy-done.7
  217.9 2.8 %unpack.2.refs_8_ = bf16[768,256]{1,0:T(8,128)(2,1)} custom-call(s32[768,128]{1,0:T(8,128)} %get-tuple-element.64.code_ref, bf16[32,48,256]{2,1,0:T(8,128)(2,1)} %copy-done.7), custom_call_target="tpu_custom_call" | custom-call | flops 603979776 | bytes 786432 | tf_op jit(solution)/shard_map/unpack/pallas_call | solution.py:225
  220.7 0.0 collective-permute-done.10.refs_1_
  220.7 8.9 %collective-permute-done.11.refs_2_ = bf16[768,384]{1,0:T(8,128)(2,1)S(1)} collective-permute-done((bf16[768,384]{1,0:T(8,128)(2,1)}, bf16[768,384]{1,0:T(8,128)(2,1)S(1)}, u32[]{:S(2)}, u32[]{:S(2)}) %collective-permute-start.11) | collective-permute-done | bytes 589856 | tf_op jit(solution)/shard_map/ppermute | solution.py:309
  229.6 0.4 collective-permute-done.12.refs_3_
  230.0 2.1 collective-permute-start.14
  232.1 0.1 collective-permute-start.15
  232.2 0.4 collective-permute-start.16
  232.6 0.8 collective-permute-start.7
  233.4 0.0 collective-permute-done.13.refs_4_
  233.4 2.1 collective-permute-start.8
  235.5 0.0 collective-permute-done.14.refs_5_
  235.5 1.4 collective-permute-start.9
  236.9 0.0 collective-permute-done.15.refs_6_
  236.9 0.8 collective-permute-start.17
  237.8 0.8 copy-done.14
  238.7 9.4 %project.2.refs_14_ = f32[768,640]{1,0:T(8,128)} custom-call(bf16[768,384]{1,0:T(8,128)(2,1)} %unpack.3.refs_0_, bf16[768,384]{1,0:T(8,128)(2,1)} %copy-done.8, bf16[768,384]{1,0:T(8,128)(2,1)} %copy-done.9, bf16[768,384]{1,0:T(8,128)(2,1)} %copy-done.10, bf16[768,384]{1,0:T(8,128)(2,1)} %copy-done.11, bf16[768,384]{1,0:T(8,128)(2,1)} %copy-done.12, ...), custom_call_target="tpu_custom_call" | custom-call | flops 3271557120 | bytes 9371648 | tf_op jit(solution)/shard_map/project/pallas_call | solution.py:275
  248.1 5.3 %collective-permute-done.8.refs_1_ = bf16[768,256]{1,0:T(8,128)(2,1)S(1)} collective-permute-done((bf16[768,256]{1,0:T(8,128)(2,1)}, bf16[768,256]{1,0:T(8,128)(2,1)S(1)}, u32[]{:S(2)}, u32[]{:S(2)}) %collective-permute-start.8) | collective-permute-done | bytes 393248 | tf_op jit(solution)/shard_map/ppermute | solution.py:309
  253.4 0.0 collective-permute-done.9.refs_2_
  253.5 1.2 collective-permute-start.18
  254.6 0.0 collective-permute-start.19
  254.7 0.5 collective-permute-start.20
  255.2 0.8 collective-permute-done.18.refs_4_
  256.0 0.6 collective-permute-done.19.refs_5_
  256.6 0.6 collective-permute-done.20.refs_6_
  257.1 0.2 copy-done.20
  257.3 0.7 copy-done.21
  258.0 6.8 %project.3 = bf16[768,640]{1,0:T(8,128)(2,1)} custom-call(bf16[768,256]{1,0:T(8,128)(2,1)} %copy-done.15, bf16[768,256]{1,0:T(8,128)(2,1)} %copy-done.16, bf16[768,256]{1,0:T(8,128)(2,1)} %copy-done.17, bf16[768,256]{1,0:T(8,128)(2,1)} %copy-done.18, bf16[768,256]{1,0:T(8,128)(2,1)} %copy-done.19, bf16[768,256]{1,0:T(8,128)(2,1)} %copy-done.20, ...), custom_call_target="tpu_custom_call" | custom-call | flops 1761607680 | bytes 5046272 | tf_op jit(solution)/shard_map/project/pallas_call | solution.py:275
  (51 shorter events, 0.1 us)
Async XLA Ops:
  10.4 12.3 %copy-start.22 = (bf16[768,640]{1,0:T(8,128)(2,1)S(1)}, bf16[768,640]{1,0:T(8,128)(2,1)}, u32[]{:S(2)}) copy-start(bf16[768,640]{1,0:T(8,128)(2,1)} %refs_4_.3) | copy-start | bytes 2949124
  10.4 12.3 %copy-start.23 = (bf16[768,640]{1,0:T(8,128)(2,1)S(1)}, bf16[768,640]{1,0:T(8,128)(2,1)}, u32[]{:S(2)}) copy-start(bf16[768,640]{1,0:T(8,128)(2,1)} %refs_5_.3) | copy-start | bytes 2949124
  10.4 12.3 %copy-start.24 = (bf16[768,640]{1,0:T(8,128)(2,1)S(1)}, bf16[768,640]{1,0:T(8,128)(2,1)}, u32[]{:S(2)}) copy-start(bf16[768,640]{1,0:T(8,128)(2,1)} %refs_6_.3) | copy-start | bytes 2949124
  10.4 83.8 %all-to-all-start.1 = ((bf16[32,128,384]{2,1,0:T(8,128)(2,1)}), bf16[32,128,384]{2,1,0:T(8,128)(2,1)}, u32[]{:S(2)}, u32[]{:S(2)}) async-start(bf16[32,128,384]{2,1,0:T(8,128)(2,1)} %pack.4), calls=%async_computation.1 | async-start | bytes 6291456 | tf_op jit(solution)/shard_map/all_to_all | solution.py:349
  29.2 20.3 %collective-permute-start = (bf16[640,640]{1,0:T(8,128)(2,1)S(1)}, bf16[640,640]{1,0:T(8,128)(2,1)S(1)}, u32[]{:S(2)}, u32[]{:S(2)}) collective-permute-start(bf16[640,640]{1,0:T(8,128)(2,1)S(1)} %get-tuple-element.105), channel_id=1, source_target_pairs={{0,2},{1,3},{2,4},{3,5},{4,6},{5,7},{6,0},{7,1},{8,10},{9,11},{10,... | collective-permute-start | bytes 2457608 | tf_op jit(solution)/shard_map/ppermute | solution.py:299
  30.5 37.6 %collective-permute-start.1 = (bf16[640,640]{1,0:T(8,128)(2,1)S(1)}, bf16[640,640]{1,0:T(8,128)(2,1)S(1)}, u32[]{:S(2)}, u32[]{:S(2)}) collective-permute-start(bf16[640,640]{1,0:T(8,128)(2,1)S(1)} %get-tuple-element.104), channel_id=1, source_target_pairs={{0,4},{1,5},{2,6},{3,7},{4,0},{5,1},{6,2},{7,3},{8,12},{9,13},{10,... | collective-permute-start | bytes 2457608 | tf_op jit(solution)/shard_map/ppermute | solution.py:299
  33.1 35.0 %collective-permute-start.2 = (bf16[640,640]{1,0:T(8,128)(2,1)S(1)}, bf16[640,640]{1,0:T(8,128)(2,1)S(1)}, u32[]{:S(2)}, u32[]{:S(2)}) collective-permute-start(bf16[640,640]{1,0:T(8,128)(2,1)S(1)} %get-tuple-element.103), channel_id=1, source_target_pairs={{0,6},{1,7},{2,0},{3,1},{4,2},{5,3},{6,4},{7,5},{8,14},{9,15},{10,... | collective-permute-start | bytes 2457608 | tf_op jit(solution)/shard_map/ppermute | solution.py:299
  49.5 46.9 %copy-start.1 = (bf16[640,640]{1,0:T(8,128)(2,1)}, bf16[640,640]{1,0:T(8,128)(2,1)S(1)}, u32[]{:S(2)}) copy-start(bf16[640,640]{1,0:T(8,128)(2,1)S(1)} %collective-permute-done.refs_10_.refs_7_) | copy-start | bytes 2457604
  68.1 28.2 %copy-start.2 = (bf16[640,640]{1,0:T(8,128)(2,1)}, bf16[640,640]{1,0:T(8,128)(2,1)S(1)}, u32[]{:S(2)}) copy-start(bf16[640,640]{1,0:T(8,128)(2,1)S(1)} %collective-permute-done.1.refs_11_.refs_8_) | copy-start | bytes 2457604
  68.1 28.2 %copy-start.3 = (bf16[640,640]{1,0:T(8,128)(2,1)}, bf16[640,640]{1,0:T(8,128)(2,1)S(1)}, u32[]{:S(2)}) copy-start(bf16[640,640]{1,0:T(8,128)(2,1)S(1)} %collective-permute-done.2.refs_12_.refs_9_) | copy-start | bytes 2457604
  96.4 57.7 %all-to-all-start.2 = ((bf16[32,128,256]{2,1,0:T(8,128)(2,1)}), bf16[32,128,256]{2,1,0:T(8,128)(2,1)}, u32[]{:S(2)}, u32[]{:S(2)}) async-start(bf16[32,128,256]{2,1,0:T(8,128)(2,1)} %pack.5), calls=%async_computation.2 | async-start | bytes 4194304 | tf_op jit(solution)/shard_map/all_to_all | solution.py:349
  105.3 10.2 %copy-start = (bf16[32,128,640]{2,1,0:T(8,128)(2,1)S(1)}, bf16[32,128,640]{2,1,0:T(8,128)(2,1)}, u32[]{:S(2)}) copy-start(bf16[32,128,640]{2,1,0:T(8,128)(2,1)} %get-tuple-element.107.extra_ref) | copy-start | bytes 15728644
  109.2 26.5 %collective-permute-start.3 = (bf16[640,640]{1,0:T(8,128)(2,1)}, bf16[640,640]{1,0:T(8,128)(2,1)S(1)}, u32[]{:S(2)}, u32[]{:S(2)}) collective-permute-start(bf16[640,640]{1,0:T(8,128)(2,1)} %get-tuple-element.102), channel_id=1, source_target_pairs={{0,1},{1,0},{2,3},{3,2},{4,5},{5,4},{6,7},{7,6},{8,9},{9,8},{10,11... | collective-permute-start | bytes 2457608 | tf_op jit(solution)/shard_map/ppermute | solution.py:299
  110.3 25.4 %collective-permute-start.4 = (bf16[640,640]{1,0:T(8,128)(2,1)}, bf16[640,640]{1,0:T(8,128)(2,1)S(1)}, u32[]{:S(2)}, u32[]{:S(2)}) collective-permute-start(bf16[640,640]{1,0:T(8,128)(2,1)} %get-tuple-element.101), channel_id=1, source_target_pairs={{0,3},{1,2},{2,5},{3,4},{4,7},{5,6},{6,1},{7,0},{8,11},{9,10},{10,... | collective-permute-start | bytes 2457608 | tf_op jit(solution)/shard_map/ppermute | solution.py:299
  111.6 39.2 %collective-permute-start.5 = (bf16[640,640]{1,0:T(8,128)(2,1)}, bf16[640,640]{1,0:T(8,128)(2,1)S(1)}, u32[]{:S(2)}, u32[]{:S(2)}) collective-permute-start(bf16[640,640]{1,0:T(8,128)(2,1)} %get-tuple-element.100), channel_id=1, source_target_pairs={{0,5},{1,4},{2,7},{3,6},{4,1},{5,0},{6,3},{7,2},{8,13},{9,12},{10,... | collective-permute-start | bytes 2457608 | tf_op jit(solution)/shard_map/ppermute | solution.py:299
  114.6 36.3 %collective-permute-start.6 = (bf16[640,640]{1,0:T(8,128)(2,1)}, bf16[640,640]{1,0:T(8,128)(2,1)}, u32[]{:S(2)}, u32[]{:S(2)}) collective-permute-start(bf16[640,640]{1,0:T(8,128)(2,1)} %get-tuple-element.99), channel_id=1, source_target_pairs={{0,7},{1,6},{2,1},{3,0},{4,3},{5,2},{6,5},{7,4},{8,15},{9,14},{10,... | collective-permute-start | bytes 2457608 | tf_op jit(solution)/shard_map/ppermute | solution.py:299
  135.7 40.1 %copy-start.4 = (bf16[640,640]{1,0:T(8,128)(2,1)}, bf16[640,640]{1,0:T(8,128)(2,1)S(1)}, u32[]{:S(2)}) copy-start(bf16[640,640]{1,0:T(8,128)(2,1)S(1)} %collective-permute-done.3.refs_13_.refs_10_) | copy-start | bytes 2457604
  135.7 40.1 %copy-start.5 = (bf16[640,640]{1,0:T(8,128)(2,1)}, bf16[640,640]{1,0:T(8,128)(2,1)S(1)}, u32[]{:S(2)}) copy-start(bf16[640,640]{1,0:T(8,128)(2,1)S(1)} %collective-permute-done.4.refs_14_.refs_11_) | copy-start | bytes 2457604
  150.9 25.0 %copy-start.6 = (bf16[640,640]{1,0:T(8,128)(2,1)}, bf16[640,640]{1,0:T(8,128)(2,1)S(1)}, u32[]{:S(2)}) copy-start(bf16[640,640]{1,0:T(8,128)(2,1)S(1)} %collective-permute-done.5.refs_15_.refs_12_) | copy-start | bytes 2457604
  154.0 34.8 %all-to-all-start.3 = ((bf16[32,48,384]{2,1,0:T(8,128)(2,1)}), bf16[32,48,384]{2,1,0:T(8,128)(2,1)}, u32[]{:S(2)}, u32[]{:S(2)}) async-start(bf16[32,48,384]{2,1,0:T(8,128)(2,1)} %attend.2), calls=%async_computation.3 | async-start | bytes 2359296 | tf_op jit(solution)/shard_map/all_to_all | solution.py:349
  188.8 28.2 %all-to-all-start.4 = ((bf16[32,48,256]{2,1,0:T(8,128)(2,1)}), bf16[32,48,256]{2,1,0:T(8,128)(2,1)S(1)}, u32[]{:S(2)}, u32[]{:S(2)}) async-start(bf16[32,48,256]{2,1,0:T(8,128)(2,1)} %attend.3), calls=%async_computation.4 | async-start | bytes 1572864 | tf_op jit(solution)/shard_map/all_to_all | solution.py:349
  200.9 19.8 %collective-permute-start.10 = (bf16[768,384]{1,0:T(8,128)(2,1)}, bf16[768,384]{1,0:T(8,128)(2,1)S(1)}, u32[]{:S(2)}, u32[]{:S(2)}) collective-permute-start(bf16[768,384]{1,0:T(8,128)(2,1)} %unpack.3.refs_0_), channel_id=1, source_target_pairs={{0,2},{1,3},{2,4},{3,5},{4,6},{5,7},{6,0},{7,1},{8,10},{9,11},{10,... | collective-permute-start | bytes 1769480 | tf_op jit(solution)/shard_map/ppermute | solution.py:309
  202.4 27.2 %collective-permute-start.11 = (bf16[768,384]{1,0:T(8,128)(2,1)}, bf16[768,384]{1,0:T(8,128)(2,1)S(1)}, u32[]{:S(2)}, u32[]{:S(2)}) collective-permute-start(bf16[768,384]{1,0:T(8,128)(2,1)} %unpack.3.refs_0_), channel_id=1, source_target_pairs={{0,4},{1,5},{2,6},{3,7},{4,0},{5,1},{6,2},{7,3},{8,12},{9,13},{10,... | collective-permute-start | bytes 1769480 | tf_op jit(solution)/shard_map/ppermute | solution.py:309
  204.9 25.1 %collective-permute-start.12 = (bf16[768,384]{1,0:T(8,128)(2,1)}, bf16[768,384]{1,0:T(8,128)(2,1)S(1)}, u32[]{:S(2)}, u32[]{:S(2)}) collective-permute-start(bf16[768,384]{1,0:T(8,128)(2,1)} %unpack.3.refs_0_), channel_id=1, source_target_pairs={{0,6},{1,7},{2,0},{3,1},{4,2},{5,3},{6,4},{7,5},{8,14},{9,15},{10,... | collective-permute-start | bytes 1769480 | tf_op jit(solution)/shard_map/ppermute | solution.py:309
  206.0 27.4 %collective-permute-start.13 = (bf16[768,384]{1,0:T(8,128)(2,1)}, bf16[768,384]{1,0:T(8,128)(2,1)S(1)}, u32[]{:S(2)}, u32[]{:S(2)}) collective-permute-start(bf16[768,384]{1,0:T(8,128)(2,1)} %unpack.3.refs_0_), channel_id=1, source_target_pairs={{0,1},{1,0},{2,3},{3,2},{4,5},{5,4},{6,7},{7,6},{8,9},{9,8},{10,11... | collective-permute-start | bytes 1769480 | tf_op jit(solution)/shard_map/ppermute | solution.py:316
  217.0 0.9 copy-start.7
  220.7 17.0 %copy-start.8 = (bf16[768,384]{1,0:T(8,128)(2,1)}, bf16[768,384]{1,0:T(8,128)(2,1)S(1)}, u32[]{:S(2)}) copy-start(bf16[768,384]{1,0:T(8,128)(2,1)S(1)} %collective-permute-done.10.refs_1_) | copy-start | bytes 1769476
  229.6 8.1 %copy-start.9 = (bf16[768,384]{1,0:T(8,128)(2,1)}, bf16[768,384]{1,0:T(8,128)(2,1)S(1)}, u32[]{:S(2)}) copy-start(bf16[768,384]{1,0:T(8,128)(2,1)S(1)} %collective-permute-done.11.refs_2_) | copy-start | bytes 1769476
  230.0 7.8 %copy-start.10 = (bf16[768,384]{1,0:T(8,128)(2,1)}, bf16[768,384]{1,0:T(8,128)(2,1)S(1)}, u32[]{:S(2)}) copy-start(bf16[768,384]{1,0:T(8,128)(2,1)S(1)} %collective-permute-done.12.refs_3_) | copy-start | bytes 1769476
  230.0 5.5 %collective-permute-start.14 = (bf16[768,384]{1,0:T(8,128)(2,1)S(1)}, bf16[768,384]{1,0:T(8,128)(2,1)S(1)}, u32[]{:S(2)}, u32[]{:S(2)}) collective-permute-start(bf16[768,384]{1,0:T(8,128)(2,1)S(1)} %collective-permute-done.10.refs_1_), channel_id=1, source_target_pairs={{0,1},{1,0},{2,3},{3,2},{4,5},{5,4},{6,7},{7,6},{8,9},{9,8},{10,11... | collective-permute-start | bytes 1769480 | tf_op jit(solution)/shard_map/ppermute | solution.py:316
  232.1 4.8 %collective-permute-start.15 = (bf16[768,384]{1,0:T(8,128)(2,1)S(1)}, bf16[768,384]{1,0:T(8,128)(2,1)S(1)}, u32[]{:S(2)}, u32[]{:S(2)}) collective-permute-start(bf16[768,384]{1,0:T(8,128)(2,1)S(1)} %collective-permute-done.11.refs_2_), channel_id=1, source_target_pairs={{0,1},{1,0},{2,3},{3,2},{4,5},{5,4},{6,7},{7,6},{8,9},{9,8},{10,11... | collective-permute-start | bytes 1769480 | tf_op jit(solution)/shard_map/ppermute | solution.py:316
  232.2 5.6 %collective-permute-start.16 = (bf16[768,384]{1,0:T(8,128)(2,1)S(1)}, bf16[768,384]{1,0:T(8,128)(2,1)S(1)}, u32[]{:S(2)}, u32[]{:S(2)}) collective-permute-start(bf16[768,384]{1,0:T(8,128)(2,1)S(1)} %collective-permute-done.12.refs_3_), channel_id=1, source_target_pairs={{0,1},{1,0},{2,3},{3,2},{4,5},{5,4},{6,7},{7,6},{8,9},{9,8},{10,11... | collective-permute-start | bytes 1769480 | tf_op jit(solution)/shard_map/ppermute | solution.py:316
  232.6 15.4 %collective-permute-start.7 = (bf16[768,256]{1,0:T(8,128)(2,1)}, bf16[768,256]{1,0:T(8,128)(2,1)S(1)}, u32[]{:S(2)}, u32[]{:S(2)}) collective-permute-start(bf16[768,256]{1,0:T(8,128)(2,1)} %unpack.2.refs_8_), channel_id=1, source_target_pairs={{0,2},{1,3},{2,4},{3,5},{4,6},{5,7},{6,0},{7,1},{8,10},{9,11},{10,... | collective-permute-start | bytes 1179656 | tf_op jit(solution)/shard_map/ppermute | solution.py:309
  233.4 4.4 %copy-start.11 = (bf16[768,384]{1,0:T(8,128)(2,1)}, bf16[768,384]{1,0:T(8,128)(2,1)S(1)}, u32[]{:S(2)}) copy-start(bf16[768,384]{1,0:T(8,128)(2,1)S(1)} %collective-permute-done.13.refs_4_) | copy-start | bytes 1769476
  233.4 20.0 %collective-permute-start.8 = (bf16[768,256]{1,0:T(8,128)(2,1)}, bf16[768,256]{1,0:T(8,128)(2,1)S(1)}, u32[]{:S(2)}, u32[]{:S(2)}) collective-permute-start(bf16[768,256]{1,0:T(8,128)(2,1)} %unpack.2.refs_8_), channel_id=1, source_target_pairs={{0,4},{1,5},{2,6},{3,7},{4,0},{5,1},{6,2},{7,3},{8,12},{9,13},{10,... | collective-permute-start | bytes 1179656 | tf_op jit(solution)/shard_map/ppermute | solution.py:309
  235.5 2.3 copy-start.12
  235.5 17.9 %collective-permute-start.9 = (bf16[768,256]{1,0:T(8,128)(2,1)}, bf16[768,256]{1,0:T(8,128)(2,1)S(1)}, u32[]{:S(2)}, u32[]{:S(2)}) collective-permute-start(bf16[768,256]{1,0:T(8,128)(2,1)} %unpack.2.refs_8_), channel_id=1, source_target_pairs={{0,6},{1,7},{2,0},{3,1},{4,2},{5,3},{6,4},{7,5},{8,14},{9,15},{10,... | collective-permute-start | bytes 1179656 | tf_op jit(solution)/shard_map/ppermute | solution.py:309
  236.9 0.9 copy-start.13
  236.9 18.2 %collective-permute-start.17 = (bf16[768,256]{1,0:T(8,128)(2,1)}, bf16[768,256]{1,0:T(8,128)(2,1)S(1)}, u32[]{:S(2)}, u32[]{:S(2)}) collective-permute-start(bf16[768,256]{1,0:T(8,128)(2,1)} %unpack.2.refs_8_), channel_id=1, source_target_pairs={{0,1},{1,0},{2,3},{3,2},{4,5},{5,4},{6,7},{7,6},{8,9},{9,8},{10,11... | collective-permute-start | bytes 1179656 | tf_op jit(solution)/shard_map/ppermute | solution.py:316
  237.8 0.8 copy-start.14
  248.1 9.1 %copy-start.15 = (bf16[768,256]{1,0:T(8,128)(2,1)}, bf16[768,256]{1,0:T(8,128)(2,1)S(1)}, u32[]{:S(2)}) copy-start(bf16[768,256]{1,0:T(8,128)(2,1)S(1)} %collective-permute-done.7.refs_0_) | copy-start | bytes 1179652
  253.4 3.7 %copy-start.16 = (bf16[768,256]{1,0:T(8,128)(2,1)}, bf16[768,256]{1,0:T(8,128)(2,1)S(1)}, u32[]{:S(2)}) copy-start(bf16[768,256]{1,0:T(8,128)(2,1)S(1)} %collective-permute-done.8.refs_1_) | copy-start | bytes 1179652
  253.5 3.7 %copy-start.17 = (bf16[768,256]{1,0:T(8,128)(2,1)}, bf16[768,256]{1,0:T(8,128)(2,1)S(1)}, u32[]{:S(2)}) copy-start(bf16[768,256]{1,0:T(8,128)(2,1)S(1)} %collective-permute-done.9.refs_2_) | copy-start | bytes 1179652
  253.5 2.5 collective-permute-start.18
  254.6 1.9 collective-permute-start.19
  254.7 2.5 collective-permute-start.20
  255.2 2.0 copy-start.18
  256.0 1.1 copy-start.19
  256.6 0.8 copy-start.20
  257.3 0.7 copy-start.21
